TPU v7x, 32 devices: a whole 2x2x4 slice. The times are simulated.
32 devices in a mesh: fsdp: 8 (over y, x, core), seq: 4 (over z).
Axes of the slice: x: 2, y: 2, z: 4, core: 2. Of those that a mesh axis runs over, the one named last changes fastest.
Arguments:
- tokens: bfloat16 [8, 2048, 1024], P('fsdp', 'seq'), may hold values from -6 to 6
- cotangent: bfloat16 [8, 2048, 1024], P('fsdp', 'seq'), may hold values from -6 to 6
- segment_ids: int32 [8, 2048], P('fsdp', 'seq'), may hold values from 0 to 8, as said below
- norm_gain: float32 [1024], replicated, may hold values from 0.5 to 1.5
- ffn_gain: float32 [1024], replicated, may hold values from 0.5 to 1.5
- mixer_gain: float32 [1536], replicated, may hold values from 0.5 to 1.5
- conv_weight: float32 [4, 1792], replicated, may hold values from -3 to 3
- conv_bias: float32 [1792], replicated, may hold values from -3 to 3
- decay_log: float32 [24], replicated, may hold values from -7.6 to -0.7
- step_bias: float32 [24], replicated, may hold values from -1 to 1
- skip_gain: float32 [24], replicated, may hold values from 0.5 to 1.5
- in_proj: float32 [1024, 3352], P('fsdp'), may hold values from -0.1875 to 0.1875
- mixer_out: float32 [1536, 1024], P('fsdp'), may hold values from -0.15625 to 0.15625
- qkv_proj: float32 [1024, 768], P('fsdp'), may hold values from -0.1875 to 0.1875
- attn_proj: float32 [512, 1024], P('fsdp'), may hold values from -1 to 1
- gate_up: float32 [1024, 4096], P('fsdp'), may hold values from -0.1875 to 0.1875
- down_proj: float32 [2048, 1024], P('fsdp'), may hold values from -0.125 to 0.125
Outputs:
- layer_out: bfloat16 [8, 2048, 1024], P('fsdp', 'seq')
- input_grad: float32 [8, 2048, 1024], P('fsdp', 'seq')
- norm_gain_grad: float32 [1024], replicated
- ffn_gain_grad: float32 [1024], replicated
- mixer_gain_grad: float32 [1536], replicated
- conv_weight_grad: float32 [4, 1792], replicated
- conv_bias_grad: float32 [1792], replicated
- decay_log_grad: float32 [24], replicated
- step_bias_grad: float32 [24], replicated
- skip_gain_grad: float32 [24], replicated
- in_proj_grad: float32 [1024, 3352], P('fsdp')
- mixer_out_grad: float32 [1536, 1024], P('fsdp')
- qkv_proj_grad: float32 [1024, 768], P('fsdp')
- attn_proj_grad: float32 [512, 1024], P('fsdp')
- gate_up_grad: float32 [1024, 4096], P('fsdp')
- down_proj_grad: float32 [2048, 1024], P('fsdp')
Inputs may be any that keep to these rules, and one draw needn't show every extreme that they name: `segment_ids`: in each sequence the numbers never fall, each document is a run of equal numbers, and one document starts within the first 512 tokens and ends within the last 512.
All inputs are finite; a program needn't handle non-finite values.
Results may differ from a plain program's by a relative error of at most 0.019.
The roundings to bfloat16 on the way count: a program that leaves them out, or rounds other values in their place, can miss the bound.
Values may be sent and summed in bfloat16 or wider, within the bound.
A program may use at most 320 MiB of HBM per device.

v0:
```python
import jax
import jax.numpy as jnp
from jax import lax
from jax.sharding import PartitionSpec as P

FF = 2048
QUERY_HEADS = 8
KEY_VALUE_HEADS = 2
HEAD_WIDTH = 64
MH = 24
MP = 64
NS = 128
KC = 4
SUB = 128
KEYS_PER_BLOCK = 512
DI = 1536
CW = 1792


epsilon = 1e-05
rope_base = 100000000000.0
highest = lax.Precision.HIGHEST


def shifted(array, axis, by):
    devices = lax.axis_size(axis)
    pairs = [(i, i + by) for i in range(devices) if 0 <= i + by < devices]
    return lax.ppermute(array, axis, pairs)


def prefix(array, axis, combine, identity):
    devices, place = (lax.axis_size(axis), lax.axis_index(axis))
    everything = jax.tree.map(
        lambda part, kind: lax.all_gather(part.astype(kind), axis),
        array,
        (jnp.bfloat16, jnp.bfloat16),
    )
    start = jax.tree.map(
        lambda part, zero: jnp.broadcast_to(jnp.asarray(zero, part.dtype), part.shape),
        array,
        identity,
    )

    def prefix_step(k, before):
        reached = k < place
        new = combine(
            before, jax.tree.map(lambda part, own: part[k].astype(own.dtype), everything, array)
        )
        return jax.tree.map(lambda a, b: jnp.where(reached, a, b), new, before)

    return lax.fori_loop(0, devices, prefix_step, start)


def entering_2(array, axis, combine, identity):
    devices, place = (lax.axis_size(axis), lax.axis_index(axis))
    everything = jax.tree.map(
        lambda part, kind: lax.all_gather(part.astype(kind), axis),
        array,
        jax.tree.map(lambda a: jnp.bfloat16 if a.dtype == jnp.float32 else a.dtype, array),
    )
    start = jax.tree.map(
        lambda part, zero: jnp.broadcast_to(jnp.asarray(zero, part.dtype), part.shape),
        array,
        identity,
    )

    def entering_step(k, before):
        at = devices - 1 - k
        reached = at > place
        new = combine(
            before, jax.tree.map(lambda part, own: part[at].astype(own.dtype), everything, array)
        )
        return jax.tree.map(lambda a, b: jnp.where(reached, a, b), new, before)

    return lax.fori_loop(0, devices, entering_step, start)


def rounded(values):
    return lax.optimization_barrier(values.astype(jnp.bfloat16)).astype(jnp.float32)


def contract(left, right):
    return lax.dot_general(
        left, right, (((0,), (0,)), ((), ())), preferred_element_type=jnp.float32
    )


def compared_keys(left, right):
    return lax.dot_general(
        left, right, (((1,), (1,)), ((), ())), preferred_element_type=jnp.float32
    )


def rms_scale(values, gain_vec):
    return (
        values * lax.rsqrt(jnp.mean(values * values, axis=-1, keepdims=True) + epsilon) * gain_vec
    )


def apply_rotation(values, token_positions):
    half_width = values.shape[-1] // 2
    exponent = jnp.arange(half_width, dtype=jnp.float32) * (2.0 / values.shape[-1])
    frequencies = jnp.power(rope_base, -exponent)
    angles = token_positions.astype(jnp.float32)[:, None] * frequencies[None, :]
    cosine = jnp.cos(angles)[:, None, :]
    sine_part = jnp.sin(angles)[:, None, :]
    first_half = values[..., :half_width]
    second = values[..., half_width:]
    return jnp.concatenate(
        [first_half * cosine - second * sine_part, second * cosine + first_half * sine_part],
        axis=-1,
    )


def conv_apply(rows_in, edge_in, weight, bias_vec, segment_labels, edge_segments):
    tap_count = weight.shape[0]
    count_of_rows = rows_in.shape[0]
    padded = jnp.concatenate([edge_in, rows_in], axis=0)
    padded_seg = jnp.concatenate([edge_segments, segment_labels], axis=0)
    running = jnp.zeros_like(rows_in) + bias_vec[None, :]
    for offset in range(tap_count):
        same_doc = (padded_seg[offset : offset + count_of_rows] == segment_labels).astype(
            jnp.float32
        )
        running = (
            running
            + weight[offset][None, :] * padded[offset : offset + count_of_rows] * same_doc[:, None]
        )
    return jax.nn.silu(running)


def ssd_block(carried, inputs):
    values_in, key_mat, read_mat, step_size, log_decay, segment_labels, before = inputs
    cum_decay = jnp.cumsum(log_decay, axis=0)
    indices = jnp.arange(segment_labels.shape[0])
    allowed = (indices[:, None] >= indices[None, :]) & (
        segment_labels[:, None] == segment_labels[None, :]
    )
    mask_cube = allowed[:, :, None]
    log_gap = cum_decay[:, None, :] - cum_decay[None, :, :]
    decays = jnp.where(mask_cube, jnp.exp(jnp.where(mask_cube, log_gap, 0.0)), 0.0)
    affinity = jnp.dot(read_mat, key_mat.T, precision=highest)
    mixing = decays * affinity[:, :, None] * step_size[None, :, :]
    within = jnp.einsum("tsh,shp->thp", mixing, values_in, precision=highest)
    entry_decay = jnp.exp(cum_decay) * (segment_labels == before).astype(jnp.float32)[:, None]
    from_state = (
        jnp.einsum("tn,hpn->thp", read_mat, carried, precision=highest) * entry_decay[:, :, None]
    )
    keep_mask = (segment_labels == segment_labels[-1]).astype(jnp.float32)
    tail_weight = jnp.exp(cum_decay[-1][None, :] - cum_decay) * keep_mask[:, None] * step_size
    fresh_state = jnp.einsum("sh,shp,sn->hpn", tail_weight, values_in, key_mat, precision=highest)
    passing = jnp.exp(cum_decay[-1]) * (segment_labels[-1] == before).astype(jnp.float32)
    return (passing[:, None, None] * carried + fresh_state, within + from_state)


def ssd_local(
    values_in, key_mat, read_mat, step_raw, step_bias, decay_log, skip_gain, segment_labels, before
):
    count_of_rows = values_in.shape[0]
    step_size = jax.nn.softplus(step_raw + step_bias)
    log_decay = -step_size * jnp.exp(decay_log)
    block_count = count_of_rows // SUB
    befores = jnp.concatenate([before[None], segment_labels[:-1]])[::SUB]
    start_state = jnp.zeros((MH, MP, NS), jnp.float32)
    end_state, outputs = lax.scan(
        ssd_block,
        start_state,
        (
            values_in.reshape(block_count, SUB, MH, MP),
            key_mat.reshape(block_count, SUB, NS),
            read_mat.reshape(block_count, SUB, NS),
            step_size.reshape(block_count, SUB, MH),
            log_decay.reshape(block_count, SUB, MH),
            segment_labels.reshape(block_count, SUB),
            befores,
        ),
    )
    within = outputs.reshape(count_of_rows, MH, MP) + skip_gain[None, :, None] * values_in
    passing = jnp.exp(jnp.sum(log_decay, axis=0)) * (segment_labels[-1] == before).astype(
        jnp.float32
    )
    return (within, end_state, passing)


def state_term(read_mat, step_raw, step_bias, decay_log, carried, segment_labels, before):
    step_size = jax.nn.softplus(step_raw + step_bias)
    cum_decay = jnp.cumsum(-step_size * jnp.exp(decay_log), axis=0)
    entry_decay = jnp.exp(cum_decay) * (segment_labels == before).astype(jnp.float32)[:, None]
    return jnp.einsum("tn,hpn->thp", read_mat, carried, precision=highest) * entry_decay[:, :, None]


def chain_states(earlier, later_part):
    return (earlier[0] * later_part[0], later_part[0][:, None, None] * earlier[1] + later_part[1])


def chain_grads(earlier, later_part):
    return (earlier[0] * later_part[0], later_part[1] + later_part[0][:, None, None] * earlier[1])


def on_device(
    tokens,
    cotangent,
    segment_ids,
    norm_gain,
    ffn_gain,
    mixer_gain,
    conv_weight,
    conv_bias,
    decay_log,
    step_bias,
    skip_gain,
    in_proj,
    mixer_out,
    qkv_proj,
    attn_proj,
    gate_up,
    down_proj,
):
    token_rows = tokens[0].astype(jnp.float32)
    segment_labels = segment_ids[0]
    count_of_rows = token_rows.shape[0]
    query_group_width = QUERY_HEADS // KEY_VALUE_HEADS
    first_row = lax.axis_index("seq") * count_of_rows
    position = first_row + jnp.arange(count_of_rows, dtype=jnp.int32)
    in_full, mix_full, qkv_full, attention_whole, gate_full, down_full = (
        lax.all_gather(in_proj.astype(jnp.bfloat16), "fsdp", axis=0, tiled=True),
        lax.all_gather(mixer_out.astype(jnp.bfloat16), "fsdp", axis=0, tiled=True),
        lax.all_gather(qkv_proj.astype(jnp.bfloat16), "fsdp", axis=0, tiled=True),
        lax.all_gather(attn_proj.astype(jnp.bfloat16), "fsdp", axis=0, tiled=True),
        lax.all_gather(gate_up.astype(jnp.bfloat16), "fsdp", axis=0, tiled=True),
        lax.all_gather(down_proj.astype(jnp.bfloat16), "fsdp", axis=0, tiled=True),
    )
    normed32, norm_pull = jax.vjp(rms_scale, token_rows, norm_gain)
    normed = normed32.astype(jnp.bfloat16)
    mixed = jnp.dot(normed, in_full, preferred_element_type=jnp.float32)
    gate_z = mixed[:, :DI]
    conv_rows = mixed[:, DI : DI + CW].astype(jnp.bfloat16)
    step_raw = mixed[:, DI + CW :]
    edge_rows, edge_seg = shifted(
        (
            conv_rows[count_of_rows - (KC - 1) :],
            segment_labels[count_of_rows - (KC - 1) :].astype(jnp.bfloat16),
        ),
        "seq",
        1,
    )
    seg_edge = edge_seg.astype(jnp.int32)
    seg_before = seg_edge[KC - 2]

    def conv_local(rows_in, edge_in, weight, bias_vec):
        return conv_apply(rows_in, edge_in, weight, bias_vec, segment_labels, seg_edge)

    activated, conv_pull = jax.vjp(
        conv_local,
        conv_rows.astype(jnp.float32),
        edge_rows.astype(jnp.float32),
        conv_weight,
        conv_bias,
    )
    act_round = rounded(activated)
    values_in = act_round[:, :DI].reshape(count_of_rows, MH, MP)
    key_mat = act_round[:, DI : DI + NS]
    read_mat = act_round[:, DI + NS :]

    def summary(values_arg, key_arg, read_arg, raw_arg, bias_arg, rate_arg, skip_arg):
        return ssd_local(
            values_arg,
            key_arg,
            read_arg,
            raw_arg,
            bias_arg,
            rate_arg,
            skip_arg,
            segment_labels,
            seg_before,
        )

    (y_local, end_state, passing), summary_pull = jax.vjp(
        summary, values_in, key_mat, read_mat, step_raw, step_bias, decay_log, skip_gain
    )
    gains_in, state_in = prefix(
        (passing, end_state),
        "seq",
        chain_states,
        (jnp.ones_like(passing), jnp.zeros_like(end_state)),
    )

    def entering(read_arg, raw_arg, bias_arg, rate_arg, carried):
        return state_term(
            read_arg, raw_arg, bias_arg, rate_arg, carried, segment_labels, seg_before
        )

    y_state, state_pull = jax.vjp(entering, read_mat, step_raw, step_bias, decay_log, state_in)
    mixer_y = y_local + y_state

    def gating(values_arg, gate_arg, gain_arg):
        return rms_scale(values_arg.reshape(count_of_rows, DI) * jax.nn.silu(gate_arg), gain_arg)

    gated32, gate_pull = jax.vjp(gating, mixer_y, gate_z, mixer_gain)
    gated = gated32.astype(jnp.bfloat16)
    mamba_out = jnp.dot(gated, mix_full, preferred_element_type=jnp.float32)
    query_key_value = jnp.dot(normed, qkv_full, preferred_element_type=jnp.float32)

    def rotation_angles(values):
        return apply_rotation(values, position)

    rotated_queries, query_pull = jax.vjp(
        rotation_angles,
        query_key_value[:, : QUERY_HEADS * HEAD_WIDTH].reshape(
            count_of_rows, QUERY_HEADS, HEAD_WIDTH
        ),
    )
    rotated_keys, key_pullback = jax.vjp(
        rotation_angles,
        query_key_value[
            :, QUERY_HEADS * HEAD_WIDTH : (QUERY_HEADS + KEY_VALUE_HEADS) * HEAD_WIDTH
        ].reshape(count_of_rows, KEY_VALUE_HEADS, HEAD_WIDTH),
    )
    query_matrix = rotated_queries.astype(jnp.bfloat16).reshape(
        count_of_rows, KEY_VALUE_HEADS, query_group_width, HEAD_WIDTH
    )
    local_keys = rotated_keys.astype(jnp.bfloat16).reshape(
        count_of_rows, KEY_VALUE_HEADS * HEAD_WIDTH
    )
    local_values = query_key_value[:, (QUERY_HEADS + KEY_VALUE_HEADS) * HEAD_WIDTH :].astype(
        jnp.bfloat16
    )
    gathered_keys, gathered_values, seg_all = (
        lax.all_gather(local_keys, "seq", axis=0, tiled=True),
        lax.all_gather(local_values, "seq", axis=0, tiled=True),
        lax.all_gather(segment_labels.astype(jnp.bfloat16), "seq", axis=0, tiled=True),
    )
    sequence_length = gathered_keys.shape[0]
    gathered_keys = gathered_keys.reshape(sequence_length, KEY_VALUE_HEADS, HEAD_WIDTH)
    gathered_values = gathered_values.reshape(sequence_length, KEY_VALUE_HEADS, HEAD_WIDTH)
    key_seg = seg_all.astype(jnp.int32)
    score_scale = HEAD_WIDTH ** (-0.5)
    required_blocks = (first_row + count_of_rows - 1) // KEYS_PER_BLOCK + 1

    def block_scores(block_index):
        beginning_row = block_index * KEYS_PER_BLOCK
        key_rows = lax.dynamic_slice_in_dim(gathered_keys, beginning_row, KEYS_PER_BLOCK, 0)
        value_rows = lax.dynamic_slice_in_dim(gathered_values, beginning_row, KEYS_PER_BLOCK, 0)
        seg_rows = lax.dynamic_slice_in_dim(key_seg, beginning_row, KEYS_PER_BLOCK, 0)
        key_pos = beginning_row + jnp.arange(KEYS_PER_BLOCK, dtype=jnp.int32)
        allowed = (key_pos[None, :] <= position[:, None]) & (
            seg_rows[None, :] == segment_labels[:, None]
        )
        scores = (
            jnp.einsum("ikgd,jkd->kgij", query_matrix, key_rows, preferred_element_type=jnp.float32)
            * score_scale
        )
        return (key_rows, value_rows, allowed, jnp.where(allowed, scores, -1e30))

    def stats_step(block_index, carried):
        row_top, row_total = carried
        key_rows, value_rows, allowed, scores = block_scores(block_index)
        new_top = jnp.maximum(row_top, jnp.max(scores, axis=-1))
        row_total = row_total * jnp.exp(row_top - new_top) + jnp.sum(
            jnp.where(allowed, jnp.exp(scores - new_top[..., None]), 0.0), axis=-1
        )
        return (new_top, row_total)

    beginning_limit = jnp.full(
        (KEY_VALUE_HEADS, query_group_width, count_of_rows), -1e30, jnp.float32
    )
    row_top, row_total = lax.fori_loop(
        0, required_blocks, stats_step, (beginning_limit, jnp.zeros_like(beginning_limit))
    )
    log_total = row_top + jnp.log(row_total)

    def output_update(block_index, running):
        key_rows, value_rows, allowed, scores = block_scores(block_index)
        attn_weights = jnp.where(allowed, jnp.exp(scores - log_total[..., None]), 0.0).astype(
            jnp.bfloat16
        )
        return running + jnp.einsum(
            "kgij,jkd->ikgd", attn_weights, value_rows, preferred_element_type=jnp.float32
        )

    attended32 = lax.fori_loop(
        0,
        required_blocks,
        output_update,
        jnp.zeros((count_of_rows, KEY_VALUE_HEADS, query_group_width, HEAD_WIDTH), jnp.float32),
    )
    attended_rows = attended32.reshape(count_of_rows, QUERY_HEADS * HEAD_WIDTH).astype(jnp.bfloat16)
    attn_out = jnp.dot(attended_rows, attention_whole, preferred_element_type=jnp.float32)
    hidden = token_rows + (attn_out + mamba_out)
    ffn_in32, ffn_pull = jax.vjp(rms_scale, hidden, ffn_gain)
    ffn_in = ffn_in32.astype(jnp.bfloat16)
    gates = jnp.dot(ffn_in, gate_full, preferred_element_type=jnp.float32)

    def swiglu(values):
        return jax.nn.silu(values[:, :FF]) * values[:, FF:]

    act32, act_pull = jax.vjp(swiglu, gates)
    act = act32.astype(jnp.bfloat16)
    result = hidden + jnp.dot(act, down_full, preferred_element_type=jnp.float32)
    back_rows = cotangent[0]
    down_grad = contract(act, back_rows)
    act_grad = compared_keys(back_rows, down_full)
    (gates_grad,) = act_pull(act_grad)
    gates_grad = gates_grad.astype(jnp.bfloat16)
    gate_up_grad = contract(ffn_in, gates_grad)
    hidden_extra, ffn_gain_grad = ffn_pull(compared_keys(gates_grad, gate_full))
    hidden_grad = back_rows.astype(jnp.float32) + hidden_extra
    branch_gradient = hidden_grad.astype(jnp.bfloat16)
    attn_proj_grad = contract(attended_rows, branch_gradient)
    attended_grad = (
        compared_keys(branch_gradient, attention_whole)
        .astype(jnp.bfloat16)
        .reshape(count_of_rows, KEY_VALUE_HEADS, query_group_width, HEAD_WIDTH)
    )
    mixer_out_grad = contract(gated, branch_gradient)
    gated_grad = rounded(compared_keys(branch_gradient, mix_full))
    y_grad, gate_z_grad, mixer_gain_grad = gate_pull(gated_grad)
    spread = jnp.transpose(
        jnp.sum(attended_grad.astype(jnp.float32) * attended32, axis=-1), (1, 2, 0)
    )

    def grad_step(block_index, carried):
        running, key_store, value_store = carried
        key_rows, value_rows, allowed, scores = block_scores(block_index)
        attn_weights = jnp.where(allowed, jnp.exp(scores - log_total[..., None]), 0.0)
        weight_grad = jnp.einsum(
            "ikgd,jkd->kgij", attended_grad, value_rows, preferred_element_type=jnp.float32
        )
        score_grad = (attn_weights * (weight_grad - spread[..., None])).astype(jnp.bfloat16)
        running = (
            running
            + jnp.einsum("kgij,jkd->ikgd", score_grad, key_rows, preferred_element_type=jnp.float32)
            * score_scale
        )
        key_gradient = (
            jnp.einsum(
                "kgij,ikgd->jkd", score_grad, query_matrix, preferred_element_type=jnp.float32
            )
            * score_scale
        )
        value_gradient = jnp.einsum(
            "kgij,ikgd->jkd",
            attn_weights.astype(jnp.bfloat16),
            attended_grad,
            preferred_element_type=jnp.float32,
        )
        beginning_row = block_index * KEYS_PER_BLOCK
        key_store = lax.dynamic_update_slice_in_dim(
            key_store,
            key_gradient.reshape(KEYS_PER_BLOCK, KEY_VALUE_HEADS * HEAD_WIDTH),
            beginning_row,
            0,
        )
        value_store = lax.dynamic_update_slice_in_dim(
            value_store,
            value_gradient.reshape(KEYS_PER_BLOCK, KEY_VALUE_HEADS * HEAD_WIDTH),
            beginning_row,
            0,
        )
        return (running, key_store, value_store)

    blank_buffer = jnp.zeros((sequence_length, KEY_VALUE_HEADS * HEAD_WIDTH), jnp.float32)
    query_grad, key_store, value_store = lax.fori_loop(
        0,
        required_blocks,
        grad_step,
        (
            jnp.zeros((count_of_rows, KEY_VALUE_HEADS, query_group_width, HEAD_WIDTH), jnp.float32),
            blank_buffer,
            blank_buffer,
        ),
    )
    own_key_gradient, value_grad_own = (
        lax.psum_scatter(
            key_store.astype(jnp.bfloat16), "seq", scatter_dimension=0, tiled=True
        ).astype(jnp.float32),
        lax.psum_scatter(
            value_store.astype(jnp.bfloat16), "seq", scatter_dimension=0, tiled=True
        ).astype(jnp.float32),
    )
    (query_raw_grad,) = query_pull(query_grad.reshape(count_of_rows, QUERY_HEADS, HEAD_WIDTH))
    (unrotated_key_gradient,) = key_pullback(
        own_key_gradient.reshape(count_of_rows, KEY_VALUE_HEADS, HEAD_WIDTH)
    )
    qkv_grad = jnp.concatenate(
        [
            query_raw_grad.reshape(count_of_rows, QUERY_HEADS * HEAD_WIDTH),
            unrotated_key_gradient.reshape(count_of_rows, KEY_VALUE_HEADS * HEAD_WIDTH),
            value_grad_own,
        ],
        axis=1,
    ).astype(jnp.bfloat16)
    qkv_proj_grad = contract(normed, qkv_grad)
    normed_grad = compared_keys(qkv_grad, qkv_full)
    read_grad_a, raw_grad_a, bias_grad_a, rate_grad_a, state_grad = state_pull(y_grad)
    chain_back = entering_2(
        (passing, state_grad),
        "seq",
        chain_grads,
        (jnp.ones_like(passing), jnp.zeros_like(state_grad)),
    )
    later_grad = chain_back[1]
    passing_grad = jnp.sum(later_grad * state_in, axis=(1, 2))
    values_grad, key_mat_grad, read_grad_b, raw_grad_b, bias_grad_b, rate_grad_b, skip_grad = (
        summary_pull((y_grad, later_grad, passing_grad))
    )
    activated_grad = jnp.concatenate(
        [values_grad.reshape(count_of_rows, DI), key_mat_grad, read_grad_a + read_grad_b], axis=1
    )
    conv_rows_grad, edge_grad, conv_weight_grad, conv_bias_grad = conv_pull(activated_grad)
    edge_back = shifted(edge_grad, "seq", -1)
    conv_rows_grad = conv_rows_grad + jnp.pad(edge_back, ((count_of_rows - (KC - 1), 0), (0, 0)))
    mixed_grad = jnp.concatenate(
        [gate_z_grad, conv_rows_grad, raw_grad_a + raw_grad_b], axis=1
    ).astype(jnp.bfloat16)
    in_proj_grad = contract(normed, mixed_grad)
    normed_grad = normed_grad + compared_keys(mixed_grad, in_full)
    rows_extra, norm_gain_grad = norm_pull(normed_grad)
    input_grad = hidden_grad + rows_extra
    weight_grads = (
        in_proj_grad,
        mixer_out_grad,
        qkv_proj_grad,
        attn_proj_grad,
        gate_up_grad,
        down_grad,
    )
    pieces = (
        lax.psum_scatter(
            weight_grads[0].astype(jnp.bfloat16), "fsdp", scatter_dimension=0, tiled=True
        ).astype(jnp.float32),
        lax.psum_scatter(
            weight_grads[1].astype(jnp.bfloat16), "fsdp", scatter_dimension=0, tiled=True
        ).astype(jnp.float32),
        lax.psum_scatter(
            weight_grads[2].astype(jnp.bfloat16), "fsdp", scatter_dimension=0, tiled=True
        ).astype(jnp.float32),
        lax.psum_scatter(
            weight_grads[3].astype(jnp.bfloat16), "fsdp", scatter_dimension=0, tiled=True
        ).astype(jnp.float32),
        lax.psum_scatter(
            weight_grads[4].astype(jnp.bfloat16), "fsdp", scatter_dimension=0, tiled=True
        ).astype(jnp.float32),
        lax.psum_scatter(
            weight_grads[5].astype(jnp.bfloat16), "fsdp", scatter_dimension=0, tiled=True
        ).astype(jnp.float32),
    )
    shards = (
        lax.psum(pieces[0].astype(jnp.bfloat16), "seq").astype(jnp.float32),
        lax.psum(pieces[1].astype(jnp.bfloat16), "seq").astype(jnp.float32),
        lax.psum(pieces[2].astype(jnp.bfloat16), "seq").astype(jnp.float32),
        lax.psum(pieces[3].astype(jnp.bfloat16), "seq").astype(jnp.float32),
        lax.psum(pieces[4].astype(jnp.bfloat16), "seq").astype(jnp.float32),
        lax.psum(pieces[5].astype(jnp.bfloat16), "seq").astype(jnp.float32),
    )
    small = lax.psum(
        (
            norm_gain_grad,
            ffn_gain_grad,
            mixer_gain_grad,
            conv_weight_grad,
            conv_bias_grad,
            rate_grad_a + rate_grad_b,
            bias_grad_a + bias_grad_b,
            skip_grad,
        ),
        ("fsdp", "seq"),
    )
    return (
        result.astype(jnp.bfloat16)[None],
        input_grad[None],
        small[0],
        small[1],
        small[2],
        small[3],
        small[4],
        small[5],
        small[6],
        small[7],
        shards[0],
        shards[1],
        shards[2],
        shards[3],
        shards[4],
        shards[5],
    )


def solution(mesh):
    return jax.shard_map(
        on_device,
        mesh=mesh,
        in_specs=(
            P("fsdp", "seq", None),
            P("fsdp", "seq", None),
            P("fsdp", "seq"),
            P(),
            P(),
            P(),
            P(),
            P(),
            P(),
            P(),
            P(),
            P("fsdp", None),
            P("fsdp", None),
            P("fsdp", None),
            P("fsdp", None),
            P("fsdp", None),
            P("fsdp", None),
        ),
        out_specs=(
            P("fsdp", "seq", None),
            P("fsdp", "seq", None),
            P(),
            P(),
            P(),
            P(),
            P(),
            P(),
            P(),
            P(),
            P("fsdp", None),
            P("fsdp", None),
            P("fsdp", None),
            P("fsdp", None),
            P("fsdp", None),
            P("fsdp", None),
        ),
        check_vma=False,
    )
```

profile of v0, /device:TPU:0, one launch (start us, length us, event | category | flops | bytes accessed | tf_op | source)
XLA Modules:
  0.0 1431.3 jit_solution(17617164370530344158)
XLA Ops:
  10.6 4.9 collective-permute-start
  22.3 40.1 %all-gather.17.cloned.1.call-done = bf16[1024,3352]{0,1:T(8,128)(2,1)} async-done(((bf16[128,3352]{0,1:T(8,128)(2,1)}), bf16[1024,3352]{0,1:T(8,128)(2,1)}) %all-gather.17.cloned.1.call-update) | async-done | bytes 6864912 | tf_op jit(solution)/shard_map/all_gather | solution.py:226
  62.5 6.2 fusion.264
  77.6 7.7 collective-permute-done.1
  85.5 11.6 multiply_convert_fusion.1
  99.3 4.9 reshape_reshape.3
  110.9 222.1 %while.157 = (s32[]{:T(128)}, f32[24,64,128]{2,1,0:T(8,128)S(1)}, f32[4,128,24,64]{1,0,3,2:T(4,128)}, pred[4,128,128,24]{2,3,1,0:T(8,128)(4,1)}, f32[4,128,128,2...) while((s32[]{:T(128)}, f32[24,64,128]{2,1,0:T(8,128)S(1)}, ...), condition=%wide.region_9.11_spmd.clone, body=%wide.region_7.10_spmd.clone.sunk | while | flops 937302016 | bytes 24298096 | solution.py:165
  127.8 4.4 fusion.407
  132.2 20.1 %dynamic_update_slice.318 = f32[4,128,24,64]{1,0,3,2:T(4,128)} dynamic-update-slice(f32[4,128,24,64]{1,0,3,2:T(4,128)} %get-tuple-element.3234, f32[1,128,24,64]{1,0,3,2:T(1,128)S(1)} %bitcast.788, s32[]{:T(128)S(6)} %copy.491, s32[]{:T(128)} %constant.336.clone.1..sunk.4, s32[]{:T(128)} %constant.336.clone.1..sunk.4, s32[]{:T(128)} %constant.336.clone.1..sunk.4) | dynamic-update-slice | bytes 1572868 | tf_op jit(solution)/shard_map/jvp()/while/body/jit(dynamic_update_index_in_dim)/dynamic_update_slice | solution.py:165
  183.2 4.4 fusion.407
  187.6 20.1 %dynamic_update_slice.318 = f32[4,128,24,64]{1,0,3,2:T(4,128)} dynamic-update-slice(f32[4,128,24,64]{1,0,3,2:T(4,128)} %get-tuple-element.3234, f32[1,128,24,64]{1,0,3,2:T(1,128)S(1)} %bitcast.788, s32[]{:T(128)S(6)} %copy.491, s32[]{:T(128)} %constant.336.clone.1..sunk.4, s32[]{:T(128)} %constant.336.clone.1..sunk.4, s32[]{:T(128)} %constant.336.clone.1..sunk.4) | dynamic-update-slice | bytes 1572868 | tf_op jit(solution)/shard_map/jvp()/while/body/jit(dynamic_update_index_in_dim)/dynamic_update_slice | solution.py:165
  238.7 4.4 fusion.407
  243.1 20.1 %dynamic_update_slice.318 = f32[4,128,24,64]{1,0,3,2:T(4,128)} dynamic-update-slice(f32[4,128,24,64]{1,0,3,2:T(4,128)} %get-tuple-element.3234, f32[1,128,24,64]{1,0,3,2:T(1,128)S(1)} %bitcast.788, s32[]{:T(128)S(6)} %copy.491, s32[]{:T(128)} %constant.336.clone.1..sunk.4, s32[]{:T(128)} %constant.336.clone.1..sunk.4, s32[]{:T(128)} %constant.336.clone.1..sunk.4) | dynamic-update-slice | bytes 1572868 | tf_op jit(solution)/shard_map/jvp()/while/body/jit(dynamic_update_index_in_dim)/dynamic_update_slice | solution.py:165
  294.2 4.4 fusion.407
  298.7 20.1 %dynamic_update_slice.318 = f32[4,128,24,64]{1,0,3,2:T(4,128)} dynamic-update-slice(f32[4,128,24,64]{1,0,3,2:T(4,128)} %get-tuple-element.3234, f32[1,128,24,64]{1,0,3,2:T(1,128)S(1)} %bitcast.788, s32[]{:T(128)S(6)} %copy.491, s32[]{:T(128)} %constant.336.clone.1..sunk.4, s32[]{:T(128)} %constant.336.clone.1..sunk.4, s32[]{:T(128)} %constant.336.clone.1..sunk.4) | dynamic-update-slice | bytes 1572868 | tf_op jit(solution)/shard_map/jvp()/while/body/jit(dynamic_update_index_in_dim)/dynamic_update_slice | solution.py:165
  342.5 13.3 all-gather.3
  361.4 20.2 %all_gather.46 = bf16[2048,128]{1,0:T(8,128)(2,1)S(1)} all-gather(bf16[512,128]{1,0:T(8,128)(2,1)S(1)} %slice.284), channel_id=1, replica_groups=mesh['fsdp'=8,'seq'=4] {'seq'}, dimensions={0}, use_global_device_ids=true | all-gather | bytes 655360 | tf_op jit(solution)/shard_map/all_gather | solution.py:330
  382.9 15.2 %all_gather.48 = bf16[2048,128]{0,1:T(8,128)(2,1)S(1)} all-gather(bf16[512,128]{0,1:T(8,128)(2,1)S(1)} %bitcast.818), channel_id=1, replica_groups=mesh['fsdp'=8,'seq'=4] {'seq'}, dimensions={0}, use_global_device_ids=true | all-gather | bytes 655360 | tf_op jit(solution)/shard_map/all_gather | solution.py:329
  400.8 4.7 while.154
  405.6 5.0 while.155
  413.6 39.8 %all-reduce.17 = bf16[96]{0:T(256)(128)(2,1)S(1)} all-reduce(bf16[96]{0:T(256)(128)(2,1)S(1)} %dynamic-update-slice), channel_id=2, replica_groups=mesh['fsdp'=8,'seq'=4] {'seq'}, use_global_device_ids=true, to_apply=%add.17 | all-reduce | flops 96 | bytes 384
  458.1 5.1 reshape.825
  463.2 4.9 while.158
  468.1 7.9 multiply_add_fusion.2
  476.0 5.8 multiply_reduce_fusion.6
  481.9 6.3 fusion.246
  495.7 12.0 fusion.245
  507.7 27.2 %all-gather.23.cloned.1.call-done = bf16[2048,1024]{1,0:T(8,128)(2,1)} async-done(((bf16[256,1024]{1,0:T(8,128)(2,1)}), bf16[2048,1024]{1,0:T(8,128)(2,1)}) %all-gather.23.cloned.1.call-update) | async-done | bytes 4194320 | tf_op jit(solution)/shard_map/all_gather | solution.py:231
  534.9 9.9 fusion.218
  544.8 10.6 multiply_reduce_fusion.7
  562.6 5.8 multiply_reduce_fusion.4
  577.6 12.5 while.156
  591.9 4.9 reshape.837
  600.6 5.0 reduce-window.16
  610.6 4.9 while.159
  620.3 239.0 %while.153 = (s32[]{:T(128)}, f32[24,64,128]{2,1,0:T(8,128)S(1)}, f32[4,128,24,64]{1,0,3,2:T(4,128)}, f32[4,128,128]{2,1,0:T(8,128)}, f32[4,128,128]{2,1,0:T(8,1...) while((s32[]{:T(128)}, f32[24,64,128]{2,1,0:T(8,128)S(1)}, ...), condition=%wide.region_35.37_spmd, body=%wide.region_26.36_spmd.sunk | while | flops 1869392896 | bytes 46011132 | solution.py:165
  637.5 20.1 %dynamic_update_slice.301 = f32[4,128,24,64]{1,0,3,2:T(4,128)} dynamic-update-slice(f32[4,128,24,64]{1,0,3,2:T(4,128)} %get-tuple-element.3522, f32[1,128,24,64]{1,0,3,2:T(1,128)S(1)} %bitcast.784, s32[]{:T(128)S(6)} %sub.347, s32[]{:T(128)} %constant.336.clone.1..sunk, s32[]{:T(128)} %constant.336.clone.1..sunk, s32[]{:T(128)} %constant.336.clone.1..sunk) | dynamic-update-slice | bytes 1572868 | tf_op jit(solution)/shard_map/transpose(jvp())/while/body/jit(dynamic_update_index_in_dim)/dynamic_update_slice | solution.py:165
  662.5 4.8 fusion.373
  697.2 20.1 %dynamic_update_slice.301 = f32[4,128,24,64]{1,0,3,2:T(4,128)} dynamic-update-slice(f32[4,128,24,64]{1,0,3,2:T(4,128)} %get-tuple-element.3522, f32[1,128,24,64]{1,0,3,2:T(1,128)S(1)} %bitcast.784, s32[]{:T(128)S(6)} %sub.347, s32[]{:T(128)} %constant.336.clone.1..sunk, s32[]{:T(128)} %constant.336.clone.1..sunk, s32[]{:T(128)} %constant.336.clone.1..sunk) | dynamic-update-slice | bytes 1572868 | tf_op jit(solution)/shard_map/transpose(jvp())/while/body/jit(dynamic_update_index_in_dim)/dynamic_update_slice | solution.py:165
  722.2 4.8 fusion.373
  756.8 20.1 %dynamic_update_slice.301 = f32[4,128,24,64]{1,0,3,2:T(4,128)} dynamic-update-slice(f32[4,128,24,64]{1,0,3,2:T(4,128)} %get-tuple-element.3522, f32[1,128,24,64]{1,0,3,2:T(1,128)S(1)} %bitcast.784, s32[]{:T(128)S(6)} %sub.347, s32[]{:T(128)} %constant.336.clone.1..sunk, s32[]{:T(128)} %constant.336.clone.1..sunk, s32[]{:T(128)} %constant.336.clone.1..sunk) | dynamic-update-slice | bytes 1572868 | tf_op jit(solution)/shard_map/transpose(jvp())/while/body/jit(dynamic_update_index_in_dim)/dynamic_update_slice | solution.py:165
  781.8 4.8 fusion.373
  816.4 20.1 %dynamic_update_slice.301 = f32[4,128,24,64]{1,0,3,2:T(4,128)} dynamic-update-slice(f32[4,128,24,64]{1,0,3,2:T(4,128)} %get-tuple-element.3522, f32[1,128,24,64]{1,0,3,2:T(1,128)S(1)} %bitcast.784, s32[]{:T(128)S(6)} %sub.347, s32[]{:T(128)} %constant.336.clone.1..sunk, s32[]{:T(128)} %constant.336.clone.1..sunk, s32[]{:T(128)} %constant.336.clone.1..sunk) | dynamic-update-slice | bytes 1572868 | tf_op jit(solution)/shard_map/transpose(jvp())/while/body/jit(dynamic_update_index_in_dim)/dynamic_update_slice | solution.py:165
  841.4 4.8 fusion.373
  860.2 4.5 fusion.210
  870.8 11.1 multiply_reduce_fusion.2
  882.0 5.5 broadcast_multiply_fusion.1
  887.5 7.8 pad_add_fusion
  901.0 11.0 collective-permute-done.2
  917.1 10.5 convolution_convert_fusion.1
  927.6 9.6 copy.276
  946.5 4.8 convolution_convert_fusion.3
  959.1 11.0 convolution_convert_fusion
  971.0 55.3 %reduce-scatter.25.cloned.1.call-done = bf16[128,3352]{1,0:T(8,128)(2,1)} async-done(((bf16[1024,3352]{1,0:T(8,128)(2,1)}), bf16[128,3352]{1,0:T(8,128)(2,1)}) %reduce-scatter.25.cloned.1.call-update) | async-done | bytes 858128
  1028.5 37.2 %reduce-scatter.19.cloned.1.call-done = bf16[64,1024]{1,0:T(8,128)(2,1)} async-done(((bf16[512,1024]{1,0:T(8,128)(2,1)}), bf16[64,1024]{1,0:T(8,128)(2,1)}) %reduce-scatter.19.cloned.1.call-update) | async-done | bytes 131088 | tf_op jit(solution)/shard_map/reduce_scatter | solution.py:538
  1065.7 42.7 %reduce-scatter.17.cloned.1.call-done = bf16[128,768]{1,0:T(8,128)(2,1)} async-done(((bf16[1024,768]{1,0:T(8,128)(2,1)}), bf16[128,768]{1,0:T(8,128)(2,1)}) %reduce-scatter.17.cloned.1.call-update) | async-done | bytes 196624 | tf_op jit(solution)/shard_map/reduce_scatter | solution.py:535
  1108.5 49.9 %reduce-scatter.15.cloned.1.call-done = bf16[192,1024]{1,0:T(8,128)(2,1)} async-done(((bf16[1536,1024]{1,0:T(8,128)(2,1)}), bf16[192,1024]{1,0:T(8,128)(2,1)}) %reduce-scatter.15.cloned.1.call-update) | async-done | bytes 393232 | tf_op jit(solution)/shard_map/reduce_scatter | solution.py:532
  1158.3 54.6 %reduce-scatter.23.cloned.1.call-done = bf16[256,1024]{1,0:T(8,128)(2,1)} async-done(((bf16[2048,1024]{1,0:T(8,128)(2,1)}), bf16[256,1024]{1,0:T(8,128)(2,1)}) %reduce-scatter.23.cloned.1.call-update) | async-done | bytes 524304 | tf_op jit(solution)/shard_map/reduce_scatter | solution.py:544
  1212.9 75.0 %reduce-scatter.21.cloned.1.call-done = bf16[128,4096]{1,0:T(8,128)(2,1)} async-done(((bf16[1024,4096]{1,0:T(8,128)(2,1)}), bf16[128,4096]{1,0:T(8,128)(2,1)}) %reduce-scatter.21.cloned.1.call-update) | async-done | bytes 1048592 | tf_op jit(solution)/shard_map/reduce_scatter | solution.py:541
  1288.0 6.3 fusion.203
  1296.6 8.9 fusion.195
  1305.5 45.9 %all-reduce.18 = (f32[1024]{0:T(1024)}, f32[1024]{0:T(1024)}, f32[1536]{0:T(1024)}, f32[4,1792]{1,0:T(4,128)}, f32[1792]{0:T(1024)}, /*index=5*/f32[24]{0:T(128)}, f32[24]{0:T(128)}, f32[24]{0:T(128)}) all-reduce(f32[1024]{0:T(1024)S(1)} %get-tuple-element.2124, ...), channel_id=1, replica_groups=mesh['fsdp'=8,'seq'=4] {'fsdp','seq'}, use_global_device_ids=true, to_apply=%region_42.44 | all-reduce | flops 12616 | bytes 100928 | tf_op jit(solution)/shard_map/psum | solution.py:556
  1351.5 4.9 fusion.198
  1356.3 59.3 %all-reduce.22.cloned.1.call-done = (bf16[128,3352]{0,1:T(8,128)(2,1)}, bf16[192,1024]{1,0:T(8,128)(2,1)}, bf16[128,768]{1,0:T(8,128)(2,1)}, bf16[64,1024]{1,0:T...) async-done(((bf16[128,3352]{0,1:T(8,128)(2,1)}, bf16[192,1024]{1,0:T(8,128)(2,1)}, bf16[128,768]{1,0:T(8,128)(2,1)}, bf16[64,1024]{1,0:T(8,128)(2,1)}, ...) | async-done | bytes 3151888 | tf_op jit(solution)/shard_map/psum | solution.py:549
  (917 shorter events, 428.0 us)
Async XLA Ops:
  7.2 55.2 %copy-start.122 = (f32[1024]{0:T(1024)S(1)}, f32[1024]{0:T(1024)}, u32[]{:S(2)}) copy-start(f32[1024]{0:T(1024)} %param.35) | copy-start | bytes 12292
  7.2 55.2 %all-gather.17.cloned.1.call-start = ((), (), s32[]{:S(2)}) async-start(), calls=%async_computation.10 | async-start | bytes 7723008 | tf_op jit(solution)/shard_map/all_gather | solution.py:226
  9.8 348.9 %all-gather.13.cloned.1.call-start = ((), (), s32[]{:S(2)}) async-start(), calls=%async_computation.8 | async-start | bytes 1769472 | tf_op jit(solution)/shard_map/all_gather | solution.py:228
  10.6 6.4 collective-permute-start
  16.3 446.9 %all-gather.25.cloned.1.call-start = ((), (), s32[]{:S(2)}) async-start(), calls=%async_computation.21 | async-start | bytes 1966080 | tf_op jit(solution)/shard_map/all_gather | solution.py:34
  16.8 51.8 %copy-start.108 = (f32[512]{0:T(512)}, f32[512]{0:T(512)S(1)}, u32[]{:S(2)}) copy-start(f32[512]{0:T(512)S(1)} %fusion.199) | copy-start | bytes 6148
  16.8 51.8 %copy-start.115 = (f32[512]{0:T(512)}, f32[512]{0:T(512)S(1)}, u32[]{:S(2)}) copy-start(f32[512]{0:T(512)S(1)} %fusion.234) | copy-start | bytes 6148
  16.9 58.5 %copy-start.120 = (f32[24]{0:T(128)}, f32[24]{0:T(128)S(1)}, u32[]{:S(2)}) copy-start(f32[24]{0:T(128)S(1)} %exp.187) | copy-start | bytes 292
  17.0 68.4 %copy-start.78 = (f32[1792]{0:T(1024)}, f32[1792]{0:T(1024)S(1)}, u32[]{:S(2)}) copy-start(f32[1792]{0:T(1024)S(1)} %get-tuple-element.2129) | copy-start | bytes 21508
  17.0 68.4 %copy-start.80 = (f32[1792]{0:T(1024)}, f32[1792]{0:T(1024)S(1)}, u32[]{:S(2)}) copy-start(f32[1792]{0:T(1024)S(1)} %get-tuple-element.2130) | copy-start | bytes 21508
  17.0 68.4 %copy-start.82 = (f32[1792]{0:T(1024)}, f32[1792]{0:T(1024)S(1)}, u32[]{:S(2)}) copy-start(f32[1792]{0:T(1024)S(1)} %get-tuple-element.2131) | copy-start | bytes 21508
  17.0 68.4 %copy-start.84 = (f32[1792]{0:T(1024)}, f32[1792]{0:T(1024)S(1)}, u32[]{:S(2)}) copy-start(f32[1792]{0:T(1024)S(1)} %get-tuple-element.2132) | copy-start | bytes 21508
  22.3 63.1 %copy-start.93 = (f32[512]{0:T(512)}, f32[512]{0:T(512)S(1)}, u32[]{:S(2)}) copy-start(f32[512]{0:T(512)S(1)} %get-tuple-element.2436) | copy-start | bytes 6148
  22.3 63.1 %copy-start.96 = (f32[512]{0:T(512)}, f32[512]{0:T(512)S(1)}, u32[]{:S(2)}) copy-start(f32[512]{0:T(512)S(1)} %get-tuple-element.2437) | copy-start | bytes 6148
  22.3 63.1 %copy-start.99 = (f32[512]{0:T(512)}, f32[512]{0:T(512)S(1)}, u32[]{:S(2)}) copy-start(f32[512]{0:T(512)S(1)} %get-tuple-element.2438) | copy-start | bytes 6148
  68.7 16.8 %copy-start.119 = (f32[1792]{0:T(1024)S(1)}, f32[1792]{0:T(1024)}, u32[]{:S(2)}) copy-start(f32[1792]{0:T(1024)} %param.39) | copy-start | bytes 21508
  71.7 13.6 collective-permute-start.1
  76.1 20.9 %copy-start.61 = (f32[512,24]{0,1:T(8,128)}, f32[512,24]{0,1:T(8,128)S(1)}, u32[]{:S(2)}) copy-start(f32[512,24]{0,1:T(8,128)S(1)} %get-tuple-element.2379) | copy-start | bytes 147460
  85.4 11.7 copy-start.30
  110.9 14.5 %copy-start.22 = (f32[4,128,128]{2,1,0:T(8,128)}, f32[4,128,128]{2,1,0:T(8,128)S(1)}, u32[]{:S(2)}) copy-start(f32[4,128,128]{2,1,0:T(8,128)S(1)} %get-tuple-element.3295) | copy-start | bytes 786436 | tf_op jit(solution)/shard_map/jvp()/while
  110.9 14.5 %copy-start.25 = (f32[4,128,128]{2,1,0:T(8,128)}, f32[4,128,128]{2,1,0:T(8,128)S(1)}, u32[]{:S(2)}) copy-start(f32[4,128,128]{2,1,0:T(8,128)S(1)} %get-tuple-element.3296) | copy-start | bytes 786436 | tf_op jit(solution)/shard_map/jvp()/while
  153.2 12.5 copy-start.136
  153.2 13.1 copy-start.26
  166.3 14.5 %copy-start.22 = (f32[4,128,128]{2,1,0:T(8,128)}, f32[4,128,128]{2,1,0:T(8,128)S(1)}, u32[]{:S(2)}) copy-start(f32[4,128,128]{2,1,0:T(8,128)S(1)} %get-tuple-element.3295) | copy-start | bytes 786436 | tf_op jit(solution)/shard_map/jvp()/while
  166.3 14.5 %copy-start.25 = (f32[4,128,128]{2,1,0:T(8,128)}, f32[4,128,128]{2,1,0:T(8,128)S(1)}, u32[]{:S(2)}) copy-start(f32[4,128,128]{2,1,0:T(8,128)S(1)} %get-tuple-element.3296) | copy-start | bytes 786436 | tf_op jit(solution)/shard_map/jvp()/while
  208.6 12.5 copy-start.136
  208.6 13.1 copy-start.26
  221.7 14.6 %copy-start.22 = (f32[4,128,128]{2,1,0:T(8,128)}, f32[4,128,128]{2,1,0:T(8,128)S(1)}, u32[]{:S(2)}) copy-start(f32[4,128,128]{2,1,0:T(8,128)S(1)} %get-tuple-element.3295) | copy-start | bytes 786436 | tf_op jit(solution)/shard_map/jvp()/while
  221.7 14.6 %copy-start.25 = (f32[4,128,128]{2,1,0:T(8,128)}, f32[4,128,128]{2,1,0:T(8,128)S(1)}, u32[]{:S(2)}) copy-start(f32[4,128,128]{2,1,0:T(8,128)S(1)} %get-tuple-element.3296) | copy-start | bytes 786436 | tf_op jit(solution)/shard_map/jvp()/while
  264.1 12.5 copy-start.136
  264.1 13.1 copy-start.26
  277.3 14.6 %copy-start.22 = (f32[4,128,128]{2,1,0:T(8,128)}, f32[4,128,128]{2,1,0:T(8,128)S(1)}, u32[]{:S(2)}) copy-start(f32[4,128,128]{2,1,0:T(8,128)S(1)} %get-tuple-element.3295) | copy-start | bytes 786436 | tf_op jit(solution)/shard_map/jvp()/while
  277.3 14.6 %copy-start.25 = (f32[4,128,128]{2,1,0:T(8,128)}, f32[4,128,128]{2,1,0:T(8,128)S(1)}, u32[]{:S(2)}) copy-start(f32[4,128,128]{2,1,0:T(8,128)S(1)} %get-tuple-element.3296) | copy-start | bytes 786436 | tf_op jit(solution)/shard_map/jvp()/while
  319.7 11.4 copy-start.114
  319.7 12.7 copy-start.136
  319.7 13.3 copy-start.26
  333.9 148.0 %all-gather.19.cloned.1.call-start = ((), (), s32[]{:S(2)}) async-start(), calls=%async_computation.11 | async-start | bytes 3538944 | tf_op jit(solution)/shard_map/all_gather | solution.py:227
  336.0 152.2 %all-gather.15.cloned.1.call-start = ((), (), s32[]{:S(2)}) async-start(), calls=%async_computation.9 | async-start | bytes 1179648 | tf_op jit(solution)/shard_map/all_gather | solution.py:229
  336.7 19.1 %copy-start.135 = (u32[32]{0:T(128)S(1)}, u32[32]{0:T(128)}, u32[]{:S(2)}) copy-start(u32[32]{0:T(128)} %constant.392) | copy-start | bytes 388
  336.7 22.0 %copy-start.116 = (f32[512]{0:T(512)S(1)}, f32[512]{0:T(512)}, u32[]{:S(2)}) copy-start(f32[512]{0:T(512)} %copy-done.115) | copy-start | bytes 6148
  336.8 22.0 %copy-start.123 = (f32[1024]{0:T(1024)S(1)}, f32[1024]{0:T(1024)}, u32[]{:S(2)}) copy-start(f32[1024]{0:T(1024)} %param.35) | copy-start | bytes 12292
  336.8 158.9 %all-gather.21.cloned.1.call-start = ((), (), s32[]{:S(2)}) async-start(), calls=%async_computation.12 | async-start | bytes 9437184 | tf_op jit(solution)/shard_map/all_gather | solution.py:230
  339.5 195.4 %all-gather.23.cloned.1.call-start = ((), (), s32[]{:S(2)}) async-start(), calls=%async_computation.13 | async-start | bytes 4718592 | tf_op jit(solution)/shard_map/all_gather | solution.py:231
  340.5 270.1 %all-gather.27.cloned.1.call-start = ((), (), s32[]{:S(2)}) async-start(), calls=%async_computation.22 | async-start | bytes 1966080 | tf_op jit(solution)/shard_map/all_gather | solution.py:57
  357.4 25.4 %copy-start.47 = (f32[512,32]{0,1:T(8,128)}, f32[512,32]{0,1:T(8,128)S(1)}, u32[]{:S(2)}) copy-start(f32[512,32]{0,1:T(8,128)S(1)} %get-tuple-element.2439) | copy-start | bytes 196612
  357.4 25.4 %copy-start.49 = (f32[512,32]{0,1:T(8,128)}, f32[512,32]{0,1:T(8,128)S(1)}, u32[]{:S(2)}) copy-start(f32[512,32]{0,1:T(8,128)S(1)} %get-tuple-element.2440) | copy-start | bytes 196612
  410.6 47.5 %copy-start.20 = (f32[512,2,4,64]{0,3,2,1:T(8,128)}, f32[512,2,4,64]{0,3,2,1:T(8,128)S(1)}, u32[]{:S(2)}) copy-start(f32[512,2,4,64]{0,3,2,1:T(8,128)S(1)} %get-tuple-element.1573) | copy-start | bytes 3145732
  411.3 76.9 %copy-start.42 = (bf16[512,2,4,64]{0,3,2,1:T(8,128)(2,1)}, bf16[512,2,4,64]{0,3,2,1:T(8,128)(2,1)S(1)}, u32[]{:S(2)}) copy-start(bf16[512,2,4,64]{0,3,2,1:T(8,128)(2,1)S(1)} %convert_element_type.337) | copy-start | bytes 1572868
  468.1 147.4 %copy-start.6 = (f32[24,64,128]{2,1,0:T(8,128)}, f32[24,64,128]{2,1,0:T(8,128)S(1)}, u32[]{:S(2)}) copy-start(f32[24,64,128]{2,1,0:T(8,128)S(1)} %get-tuple-element.1577) | copy-start | bytes 2359300
  481.8 80.3 %copy-start.76 = (f32[512]{0:T(512)}, f32[512]{0:T(512)S(1)}, u32[]{:S(2)}) copy-start(f32[512]{0:T(512)S(1)} %fusion.235) | copy-start | bytes 6148
  492.4 63.1 %copy-start.105 = (f32[512]{0:T(512)}, f32[512]{0:T(512)S(1)}, u32[]{:S(2)}) copy-start(f32[512]{0:T(512)S(1)} %fusion.236) | copy-start | bytes 6148
  495.7 39.2 %copy-start.34 = (bf16[1,512,1024]{2,1,0:T(8,128)(2,1)S(1)}, bf16[1,512,1024]{2,1,0:T(8,128)(2,1)}, u32[]{:S(2)}) copy-start(bf16[1,512,1024]{2,1,0:T(8,128)(2,1)} %param.33) | copy-start | bytes 3145732
  573.4 368.0 %reduce-scatter.11.cloned.1.call-start = ((), (), s32[]{:S(2)}) async-start(), calls=%async_computation.14 | async-start | bytes 655360 | tf_op jit(solution)/shard_map/reduce_scatter | solution.py:474
  590.9 351.5 %reduce-scatter.13.cloned.1.call-start = ((), (), s32[]{:S(2)}) async-start(), calls=%async_computation.15 | async-start | bytes 655360 | tf_op jit(solution)/shard_map/reduce_scatter | solution.py:477
  606.4 419.9 %reduce-scatter.25.cloned.1.call-start = ((), (), s32[]{:S(2)}) async-start(), calls=%async_computation.23 | async-start | bytes 7962624
  898.4 13.5 collective-permute-start.2
  937.2 128.5 %reduce-scatter.19.cloned.1.call-start = ((), (), s32[]{:S(2)}) async-start(), calls=%async_computation.18 | async-start | bytes 1179648 | tf_op jit(solution)/shard_map/reduce_scatter | solution.py:538
  940.3 168.2 %reduce-scatter.17.cloned.1.call-start = ((), (), s32[]{:S(2)}) async-start(), calls=%async_computation.17 | async-start | bytes 1769472 | tf_op jit(solution)/shard_map/reduce_scatter | solution.py:535
  946.4 212.0 %reduce-scatter.15.cloned.1.call-start = ((), (), s32[]{:S(2)}) async-start(), calls=%async_computation.16 | async-start | bytes 3538944 | tf_op jit(solution)/shard_map/reduce_scatter | solution.py:532
  951.3 261.7 %reduce-scatter.23.cloned.1.call-start = ((), (), s32[]{:S(2)}) async-start(), calls=%async_computation.20 | async-start | bytes 4718592 | tf_op jit(solution)/shard_map/reduce_scatter | solution.py:544
  957.5 330.4 %reduce-scatter.21.cloned.1.call-start = ((), (), s32[]{:S(2)}) async-start(), calls=%async_computation.19 | async-start | bytes 9437184 | tf_op jit(solution)/shard_map/reduce_scatter | solution.py:541
  970.1 445.5 %all-reduce.22.cloned.1.call-start = ((), (), s32[]{:S(2)}) async-start(), calls=%async_computation.24 | async-start | bytes 6303744 | tf_op jit(solution)/shard_map/psum | solution.py:549
  1296.6 54.8 %copy-start.109 = (f32[512]{0:T(512)S(1)}, f32[512]{0:T(512)}, u32[]{:S(2)}) copy-start(f32[512]{0:T(512)} %copy-done.108) | copy-start | bytes 6148
  1296.6 54.8 %copy-start.104 = (f32[512]{0:T(512)S(1)}, f32[512]{0:T(512)}, u32[]{:S(2)}) copy-start(f32[512]{0:T(512)} %copy-done.103) | copy-start | bytes 6148
  (153 other events, 747.1 us)
Sparse Core Ops, SparseCore 0:
  10.5 51.8 all-gather.16
  64.9 25.6 all-gather.12
  334.0 45.5 all-gather.24
  381.9 31.7 all-gather.18
  415.4 23.4 all-gather.14
  441.3 54.3 all-gather.20
  498.1 36.7 all-gather.22
  573.5 37.0 all-gather.26
  612.9 37.1 reduce-scatter.10
  652.2 19.7 reduce-scatter.12
  937.3 88.9 reduce-scatter.24
  1029.7 36.0 reduce-scatter.18
  1069.9 38.4 reduce-scatter.16
  1112.1 46.2 reduce-scatter.14
  1161.5 51.3 reduce-scatter.22
  1216.6 71.2 reduce-scatter.20
  1291.2 124.3 all-reduce.21
where the time goes:
time: 1450 us; the launch traced here: 1430 us
  waiting for transfers between devices  468 us (32%)
  local copies, waits for them, and re-layouts  347 us (24%)
  matrix products  244 us (17%)
  other arithmetic  202 us (14%)
  blocking collectives  134 us (9%)
  between operations  18.2 us (1%)
    dynamic_update_slice x72, local copies, waits for them, and re-layouts, ssd_local(): lax.scan(ssd_block, start_state, (values_in.reshape(block_count, SUB, MH,...  187 us
    reduce_scatter x1, waiting for transfers between devices, on_device(): lax.psum_scatter(weight_grads[4].astype(jnp.bfloat16), 'fsdp', scatter_di...  75 us
    psum x1, waiting for transfers between devices, on_device(): lax.psum(pieces[0].astype(jnp.bfloat16), 'seq').astype(jnp.float32)  59.3 us
    unnamed x18, waiting for transfers between devices  55.6 us
    reduce_scatter x1, waiting for transfers between devices, on_device(): lax.psum_scatter(weight_grads[5].astype(jnp.bfloat16), 'fsdp', scatter_di...  54.6 us
    dynamic_slice x44, local copies, waits for them, and re-layouts, ssd_local(): lax.scan(ssd_block, start_state, (values_in.reshape(block_count, SUB, MH,...  54.3 us
    reduce_scatter x1, waiting for transfers between devices, on_device(): lax.psum_scatter(weight_grads[1].astype(jnp.bfloat16), 'fsdp', scatter_di...  49.9 us
    psum x1, blocking collectives, on_device(): lax.psum((norm_gain_grad, ffn_gain_grad, mixer_gain_grad, conv_weight_gra...  45.9 us
  transfers between devices with their start and end apart: 20, of which 13 were waited for; matrix products, arithmetic and copies ran while one was open for 51% of the time, Pallas kernels for 0%

commit v1 on v0

v1 whole, which is shorter than its diff:
```python
import jax
import jax.numpy as jnp
from jax import lax
from jax.experimental import pallas as pl
from jax.experimental.pallas import tpu as pltpu
from jax.sharding import PartitionSpec as P

FF = 2048
QUERY_HEADS = 8
KEY_VALUE_HEADS = 2
HEAD_WIDTH = 64
MH = 24
MP = 64
NS = 128
KC = 4
SUB = 128
DI = 1536
CW = 1792
EDGE = 8

epsilon = 1e-05
rope_base = 100000000000.0
highest = lax.Precision.HIGHEST
f32 = jnp.float32
bf16 = jnp.bfloat16


def dot_nn(left, right):
    return jnp.dot(left, right, preferred_element_type=jnp.float32)


def dot_nt(left, right):
    return lax.dot_general(
        left, right, (((1,), (1,)), ((), ())), preferred_element_type=jnp.float32
    )


def dot_tn(left, right):
    return lax.dot_general(
        left, right, (((0,), (0,)), ((), ())), preferred_element_type=jnp.float32
    )


def exact(left, right):
    return jnp.dot(left, right, precision=highest, preferred_element_type=jnp.float32)


def low(values):
    return values.astype(jnp.bfloat16)


def split(values):
    top = low(values)
    return top, low(values - top.astype(jnp.float32))


def iota(shape, axis):
    return lax.broadcasted_iota(jnp.int32, shape, axis)


def spreader():
    return low(jnp.where(iota((128, DI), 1) // MP == iota((128, DI), 0), 1.0, 0.0))


def widen(values, spread):
    top, rest = split(values)
    return dot_nn(top, spread) + dot_nn(rest, spread)


def widen_row(row, spread):
    return widen(jnp.broadcast_to(row, (8, 128)), spread)[0:1]


def head_sums(values, spread):
    top, rest = split(values)
    return dot_nt(top, spread) + dot_nt(rest, spread)


def softplus(values):
    return jnp.maximum(values, 0.0) + jnp.log1p(jnp.exp(-jnp.abs(values)))


def sigmoid(values):
    return 1.0 / (1.0 + jnp.exp(-values))


def lane_halves(rows):
    lane = iota((rows, 128), 1)
    return lane < MP


def rounded_to(values):
    return low(values).astype(jnp.float32)


def front_kernel(conv_ref, seg_ref, raw_ref, bias_ref, rate_ref, weight_ref, cbias_ref,
                 act_ref, dt_ref, cum_ref, end_ref, pass_ref):
    chunks = raw_ref.shape[0] // SUB

    def tile(j, carry):
        col = pl.ds(pl.multiple_of(j * 128, 128), 128)
        for c in range(chunks):
            r0 = c * SUB
            seg = seg_ref[pl.ds(r0 + 8, SUB), :]
            total = jnp.broadcast_to(cbias_ref[0:1, col], (SUB, 128))
            for k in range(KC):
                x = rounded_to(conv_ref[pl.ds(r0 + 9 - KC + k, SUB), col])
                if k < KC - 1:
                    x = jnp.where(seg_ref[pl.ds(r0 + 9 - KC + k, SUB), :] == seg, x, 0.0)
                total = total + weight_ref[k : k + 1, col] * x
            act_ref[pl.ds(r0, SUB), col] = low(total * sigmoid(total))
        return carry

    lax.fori_loop(0, CW // 128, tile, 0)
    spread = spreader()
    lower = jnp.where(iota((SUB, SUB), 0) >= iota((SUB, SUB), 1), 1.0, 0.0)
    end_ref[...] = jnp.zeros_like(end_ref)
    gain = jnp.ones((1, 128), jnp.float32)
    for c in range(chunks):
        rows = pl.ds(c * SUB, SUB)
        dt = softplus(raw_ref[rows, :] + bias_ref[...])
        cum = exact(lower, -dt * jnp.exp(rate_ref[...]))
        dt_ref[rows, :] = dt
        cum_ref[rows, :] = cum
        seg = seg_ref[pl.ds(c * SUB + 8, SUB), :]
        before = seg_ref[pl.ds(c * SUB + 7, 1), :]
        last = seg[SUB - 1 :, :]
        end = cum[SUB - 1 :, :]
        weight = jnp.where(seg == last, jnp.exp(end - cum), 0.0) * dt
        passing = jnp.where(last == before, jnp.exp(end), 0.0)
        gain = gain * passing
        values = act_ref[rows, 0:DI].astype(jnp.float32)
        fresh = dot_tn(act_ref[rows, DI : DI + NS], low(widen(weight, spread) * values))
        end_ref[...] = widen_row(passing, spread) * end_ref[...] + fresh
    pass_ref[...] = widen_row(gain, spread)


def mid_kernel(act_ref, dt_ref, cum_ref, seg_ref, segrow_ref, state_ref, z_ref, gain_ref, skip_ref,
               y_ref, gated_ref, kept_ref, carry_ref):
    chunks = act_ref.shape[0] // SUB
    spread = spreader()
    carry_ref[...] = state_ref[...]
    half = lane_halves(SUB)

    def chunk(c, nothing):
        r0 = pl.multiple_of(c * SUB, SUB)
        rows = pl.ds(r0, SUB)
        dt, cum = dt_ref[rows, :], cum_ref[rows, :]
        cum_t = cum.T
        seg = seg_ref[pl.ds(pl.multiple_of(r0 + 8, 8), SUB), :]
        before = seg_ref[pl.ds(pl.multiple_of(r0, 8), 8), :][7:8]
        last, end = seg[SUB - 1 :, :], cum[SUB - 1 :, :]
        keys, reads = act_ref[rows, DI : DI + NS], act_ref[rows, DI + NS : CW]
        affinity = dot_nt(reads, keys)
        allowed = (iota((SUB, SUB), 0) >= iota((SUB, SUB), 1)) & (seg == segrow_ref[0:1, rows])
        state = low(carry_ref[...])
        kept_ref[pl.ds(c, 1)] = state[None]
        entry = widen(jnp.where(seg == before, jnp.exp(cum), 0.0), spread)
        y_ref[rows, :] = dot_nn(reads, state) * entry
        values = act_ref[rows, 0:DI].astype(jnp.float32)
        scaled = values * widen(dt, spread)
        weight = jnp.where(seg == last, jnp.exp(end - cum), 0.0)
        passing = jnp.where(last == before, jnp.exp(end), 0.0)
        fresh = dot_tn(keys, low(widen(weight, spread) * scaled))
        carry_ref[...] = widen_row(passing, spread) * carry_ref[...] + fresh
        for pair in range(MH // 2):
            cols = slice(pair * 128, pair * 128 + 128)
            parts = []
            for h in (2 * pair, 2 * pair + 1):
                gap = jnp.where(allowed, cum[:, h : h + 1] - cum_t[h : h + 1, :], -1e30)
                parts.append(low(jnp.exp(gap) * affinity))
            v = scaled[:, cols]
            right = jnp.concatenate([low(jnp.where(half, v, 0.0)), low(jnp.where(half, 0.0, v))], 0)
            y_ref[rows, cols] = y_ref[rows, cols] + dot_nn(jnp.concatenate(parts, 1), right)
        z = z_ref[rows, :]
        g = (y_ref[rows, :] + skip_ref[...] * values) * (z * sigmoid(z))
        scale = lax.rsqrt(jnp.mean(g * g, axis=1, keepdims=True) + epsilon)
        gated_ref[rows, :] = low(g * scale * gain_ref[...])
        return nothing

    lax.fori_loop(0, chunks, chunk, 0)


def gate_back_kernel(grad_ref, y_ref, act_ref, z_ref, dt_ref, cum_ref, seg_ref, gain_ref, skip_ref,
                     ygrad_ref, zgrad_ref, gain_grad_ref, state_grad_ref):
    chunks = act_ref.shape[0] // SUB
    spread = spreader()
    gain_grad_ref[...] = jnp.zeros_like(gain_grad_ref)
    state_grad_ref[...] = jnp.zeros_like(state_grad_ref)

    def chunk(i, nothing):
        c = chunks - 1 - i
        r0 = pl.multiple_of(c * SUB, SUB)
        rows = pl.ds(r0, SUB)
        values = act_ref[rows, 0:DI].astype(jnp.float32)
        z = z_ref[rows, :]
        sig = sigmoid(z)
        silu = z * sig
        u = y_ref[rows, :] + skip_ref[...] * values
        g = u * silu
        grad = grad_ref[rows, :].astype(jnp.float32)
        scale = lax.rsqrt(jnp.mean(g * g, axis=1, keepdims=True) + epsilon)
        unit = g * scale
        gain_grad_ref[...] += jnp.sum(grad * unit, axis=0, keepdims=True)
        h = grad * gain_ref[...]
        dg = scale * (h - unit * jnp.mean(h * unit, axis=1, keepdims=True))
        dy = dg * silu
        ygrad_ref[rows, :] = dy
        zgrad_ref[rows, :] = low(dg * u * (sig * (1.0 + z * (1.0 - sig))))
        cum = cum_ref[rows, :]
        seg = seg_ref[pl.ds(pl.multiple_of(r0 + 8, 8), SUB), :]
        before = seg_ref[pl.ds(pl.multiple_of(r0, 8), 8), :][7:8]
        last, end = seg[SUB - 1 :, :], cum[SUB - 1 :, :]
        entry = widen(jnp.where(seg == before, jnp.exp(cum), 0.0), spread)
        passing = jnp.where(last == before, jnp.exp(end), 0.0)
        fresh = dot_tn(act_ref[rows, DI + NS : CW], low(entry * dy))
        state_grad_ref[...] = widen_row(passing, spread) * state_grad_ref[...] + fresh
        return nothing

    lax.fori_loop(0, chunks, chunk, 0)


def back_kernel(act_ref, dt_ref, cum_ref, seg_ref, segrow_ref, raw_ref, bias_ref, rate_ref, kept_ref,
                y_ref, ygrad_ref, later_ref, conv_ref, weight_ref, cbias_ref, skip_ref,
                raw_grad_ref, conv_grad_ref, weight_grad_ref, cbias_grad_ref, rate_grad_ref,
                bias_grad_ref, skip_grad_ref, act_grad_ref, carry_ref, pre_ref):
    rows_total = act_ref.shape[0]
    chunks = rows_total // SUB
    spread = spreader()
    half = lane_halves(SUB)
    upper = jnp.where(iota((SUB, SUB), 1) >= iota((SUB, SUB), 0), 1.0, 0.0)
    rate = jnp.exp(rate_ref[...])
    carry_ref[...] = later_ref[...]
    rate_grad_ref[...] = jnp.zeros_like(rate_grad_ref)
    bias_grad_ref[...] = jnp.zeros_like(bias_grad_ref)
    skip_grad_ref[...] = jnp.zeros_like(skip_grad_ref)

    def chunk(i, nothing):
        c = chunks - 1 - i
        r0 = pl.multiple_of(c * SUB, SUB)
        rows = pl.ds(r0, SUB)
        dt, cum = dt_ref[rows, :], cum_ref[rows, :]
        cum_t = cum.T
        seg = seg_ref[pl.ds(pl.multiple_of(r0 + 8, 8), SUB), :]
        before = seg_ref[pl.ds(pl.multiple_of(r0, 8), 8), :][7:8]
        last, end = seg[SUB - 1 :, :], cum[SUB - 1 :, :]
        keys, reads = act_ref[rows, DI : DI + NS], act_ref[rows, DI + NS : CW]
        affinity = dot_nt(keys, reads)
        allowed = (iota((SUB, SUB), 1) >= iota((SUB, SUB), 0)) & (seg == segrow_ref[0:1, rows])
        values = act_ref[rows, 0:DI].astype(jnp.float32)
        wide_dt = widen(dt, spread)
        scaled = values * wide_dt
        scaled_low = low(scaled)
        dy = ygrad_ref[rows, :]
        dy_low = low(dy)
        state, carry = kept_ref[pl.ds(c, 1)][0], carry_ref[...]
        carry_low = low(carry)
        wide_weight = widen(jnp.where(seg == last, jnp.exp(end - cum), 0.0), spread)
        wide_entry = widen(jnp.where(seg == before, jnp.exp(cum), 0.0), spread)
        wide_pass = widen_row(jnp.where(last == before, jnp.exp(end), 0.0), spread)
        from_state = dot_nn(keys, carry_low) * wide_weight
        mixed_grad = jnp.zeros((SUB, SUB), jnp.float32)
        for pair in range(MH // 2):
            cols = slice(pair * 128, pair * 128 + 128)
            v, d = scaled[:, cols], dy[:, cols]
            left = jnp.concatenate([low(jnp.where(half, v, 0.0)), low(jnp.where(half, 0.0, v))], 0)
            right = jnp.concatenate([low(jnp.where(half, d, 0.0)), low(jnp.where(half, 0.0, d))], 0)
            weight_grad = dot_nt(left, dy_low[:, cols])
            parts = []
            for n, h in enumerate((2 * pair, 2 * pair + 1)):
                gap = jnp.where(allowed, cum_t[h : h + 1, :] - cum[:, h : h + 1], -1e30)
                decay = jnp.exp(gap)
                parts.append(low(decay * affinity))
                mixed_grad = mixed_grad + decay * weight_grad[n * SUB : (n + 1) * SUB]
            act_grad_ref[rows, cols] = dot_nn(jnp.concatenate(parts, 1), right)
        x = act_grad_ref[rows, 0:DI] + from_state
        act_grad_ref[rows, 0:DI] = wide_dt * x + skip_ref[...] * dy
        mixed_low = low(mixed_grad)
        act_grad_ref[rows, DI : DI + NS] = dot_nn(mixed_low, reads) + dot_nt(
            low(wide_weight * scaled), carry_low
        )
        entered = low(wide_entry * dy)
        act_grad_ref[rows, DI + NS : CW] = dot_tn(mixed_low, keys) + dot_nt(entered, state)
        scaled_exact = scaled_low.astype(jnp.float32)
        direct = head_sums(values * x, spread)
        given = head_sums(scaled_exact * x, spread)
        taken = head_sums(dy_low.astype(jnp.float32) * y_ref[rows, :], spread)
        tail = jnp.sum(scaled_exact * from_state, axis=0, keepdims=True) + jnp.sum(
            wide_pass * carry * state.astype(jnp.float32), axis=0, keepdims=True
        )
        tail = head_sums(jnp.broadcast_to(tail, (8, DI)), spread)[0:1]
        decay_grad = exact(upper, taken - given) + tail
        rate_grad_ref[...] += jnp.sum(decay_grad * (-dt * rate), axis=0, keepdims=True)
        dt_grad = direct - decay_grad * rate
        raw_grad = dt_grad * sigmoid(raw_ref[rows, :] + bias_ref[...])
        raw_grad_ref[rows, :] = raw_grad
        bias_grad_ref[...] += jnp.sum(raw_grad, axis=0, keepdims=True)
        skip_sum = jnp.sum(dy * values, axis=0, keepdims=True)
        skip_grad_ref[...] += head_sums(jnp.broadcast_to(skip_sum, (8, DI)), spread)[0:1]
        carry_ref[...] = wide_pass * carry + dot_tn(reads, entered)
        return nothing

    lax.fori_loop(0, chunks, chunk, 0)
    weight_grad_ref[...] = jnp.zeros_like(weight_grad_ref)
    pre_ref[0:8, :] = jnp.zeros((8, 128), jnp.float32)
    pre_ref[rows_total + 8 : rows_total + 16, :] = jnp.zeros((8, 128), jnp.float32)

    def tile(j, carry):
        col = pl.ds(pl.multiple_of(j * 128, 128), 128)
        sums = [jnp.zeros((1, 128), jnp.float32) for _ in range(KC + 1)]
        for c in range(chunks):
            r0 = c * SUB
            seg = seg_ref[pl.ds(r0 + 8, SUB), :]
            total = jnp.broadcast_to(cbias_ref[0:1, col], (SUB, 128))
            taps = []
            for k in range(KC):
                x = rounded_to(conv_ref[pl.ds(r0 + 9 - KC + k, SUB), col])
                if k < KC - 1:
                    x = jnp.where(seg_ref[pl.ds(r0 + 9 - KC + k, SUB), :] == seg, x, 0.0)
                taps.append(x)
                total = total + weight_ref[k : k + 1, col] * x
            sig = sigmoid(total)
            pre = act_grad_ref[pl.ds(r0, SUB), col] * (sig * (1.0 + total * (1.0 - sig)))
            pre_ref[pl.ds(r0 + 8, SUB), :] = pre
            for k in range(KC):
                sums[k] = sums[k] + jnp.sum(pre * taps[k], axis=0, keepdims=True)
            sums[KC] = sums[KC] + jnp.sum(pre, axis=0, keepdims=True)
        for k in range(KC):
            weight_grad_ref[k : k + 1, col] = sums[k]
        cbias_grad_ref[0:1, col] = sums[KC]
        for c in range(chunks + 1):
            r0 = c * SUB
            size = SUB if c < chunks else 8
            seg = seg_ref[pl.ds(r0, size), :]
            total = jnp.zeros((size, 128), jnp.float32)
            for back in range(KC):
                x = pre_ref[pl.ds(r0 + back, size), :]
                if back:
                    x = jnp.where(seg_ref[pl.ds(r0 + back, size), :] == seg, x, 0.0)
                total = total + weight_ref[KC - 1 - back : KC - back, col] * x
            conv_grad_ref[pl.ds(r0, size), col] = total
        return carry

    lax.fori_loop(0, CW // 128, tile, 0)


def partner(values):
    lane = iota(values.shape, 1)
    half = HEAD_WIDTH // 2
    return jnp.where(
        lane % HEAD_WIDTH < half, pltpu.roll(values, 128 - half, 1), pltpu.roll(values, half, 1)
    )


def rotate_kernel(qkv_ref, cos_ref, sin_ref, query_ref, kv_ref):
    cos, sin = cos_ref[...], sin_ref[...]
    for g in range(5):
        x = qkv_ref[:, g * 128 : g * 128 + 128]
        x = low(x * cos + partner(x) * sin)
        if g < 4:
            query_ref[:, g * 128 : g * 128 + 128] = x * jnp.bfloat16(HEAD_WIDTH**-0.5)
        else:
            kv_ref[:, 0:128] = x
    kv_ref[:, 128:256] = low(qkv_ref[:, 640:768])


def lane_variants(block, out_ref):
    other = pltpu.roll(block, 64, 1)
    half = iota(block.shape, 1) < HEAD_WIDTH
    out_ref[0] = low(jnp.where(half, block, 0.0))
    out_ref[1] = low(jnp.where(half, 0.0, other))
    out_ref[2] = low(jnp.where(half, other, 0.0))
    out_ref[3] = low(jnp.where(half, 0.0, block))


def attend_bias(b, own, rows, segcol_ref, segrow_ref, bias_ref):
    seg = segcol_ref[pl.ds(pl.multiple_of(b * rows, rows), rows), :]
    seg = jnp.concatenate([seg] * (rows // 128), 1)
    causal = (iota((rows, rows), 0) - iota((rows, rows), 1)) <= jnp.where(b < own, rows, 0)
    bias_ref[...] = jnp.where(causal & (seg == segrow_ref[...]), 0.0, -1e30)


def attend_kernel(own_ref, query_ref, kv_ref, segcol_ref, segrow_ref, out_ref, out_t_ref, total_ref,
                  bias_ref, keys_ref, top_ref, sum_ref):
    rows = query_ref.shape[0]
    own = own_ref[0]
    top_ref[...] = jnp.full_like(top_ref, -1e30)
    sum_ref[...] = jnp.zeros_like(sum_ref)
    out_t_ref[...] = jnp.zeros_like(out_t_ref)

    def block(i, nothing):
        b = own - i
        at = pl.ds(pl.multiple_of(b * rows, rows), rows)
        attend_bias(b, own, rows, segcol_ref, segrow_ref, bias_ref)
        lane_variants(kv_ref[at, 0:128].astype(jnp.float32), keys_ref)
        values_t = low(kv_ref[at, 128:256].astype(jnp.float32).T)
        for h in range(QUERY_HEADS):
            g, kv = h // 2, h // 4
            scores = dot_nt(keys_ref[kv * 2 + h % 2], query_ref[:, g * 128 : g * 128 + 128])
            scores = scores + bias_ref[...]
            old = top_ref[h : h + 1, :]
            top = jnp.maximum(old, jnp.max(scores, axis=0, keepdims=True))
            p = jnp.exp(scores - top)
            fade = jnp.exp(old - top)
            top_ref[h : h + 1, :] = top
            sum_ref[h : h + 1, :] = sum_ref[h : h + 1, :] * fade + jnp.sum(p, 0, keepdims=True)
            at_h = slice(h * 64, h * 64 + 64)
            out_t_ref[at_h, :] = out_t_ref[at_h, :] * fade + dot_nn(
                values_t[kv * 64 : kv * 64 + 64, :], low(p)
            )
        return nothing

    lax.fori_loop(0, own + 1, block, 0)
    total_ref[...] = top_ref[...] + jnp.log(sum_ref[...])
    for h in range(QUERY_HEADS):
        at_h = slice(h * 64, h * 64 + 64)
        out_t_ref[at_h, :] = out_t_ref[at_h, :] / sum_ref[h : h + 1, :]
    out_ref[...] = low(out_t_ref[...].T)


def attend_back_kernel(own_ref, query_ref, kv_ref, segcol_ref, segrow_ref, grad_ref, out_t_ref,
                       total_ref, cos_ref, sin_ref, query_grad_ref, kv_grad_ref,
                       bias_ref, keys_ref, values_ref, dkeys_ref, dvalues_ref, spread_ref, dq_ref,
                       query_half_ref, grad_half_ref):
    rows = query_ref.shape[0]
    own = own_ref[0]
    kv_grad_ref[...] = jnp.zeros_like(kv_grad_ref)
    dq_ref[...] = jnp.zeros_like(dq_ref)
    grad_t = grad_ref[...].astype(jnp.float32).T
    product = grad_t * out_t_ref[...]
    for h in range(QUERY_HEADS):
        spread_ref[h : h + 1, :] = jnp.sum(product[h * 64 : h * 64 + 64, :], 0, keepdims=True)
        g = h // 2
        half = (iota((rows, 128), 1) < HEAD_WIDTH) == (h % 2 == 0)
        for src, dst in ((query_ref, query_half_ref), (grad_ref, grad_half_ref)):
            dst[h] = low(jnp.where(half, src[:, g * 128 : g * 128 + 128].astype(jnp.float32), 0.0))

    def block(b, nothing):
        at = pl.ds(pl.multiple_of(b * rows, rows), rows)
        attend_bias(b, own, rows, segcol_ref, segrow_ref, bias_ref)
        keys = kv_ref[at, 0:128].astype(jnp.float32)
        lane_variants(keys, keys_ref)
        lane_variants(kv_ref[at, 128:256].astype(jnp.float32), values_ref)
        keys_t = low(keys.T)
        dkeys_ref[...] = jnp.zeros_like(dkeys_ref)
        dvalues_ref[...] = jnp.zeros_like(dvalues_ref)
        for h in range(QUERY_HEADS):
            g, kv = h // 2, h // 4
            lanes = slice(g * 128, g * 128 + 128)
            scores = dot_nt(keys_ref[kv * 2 + h % 2], query_ref[:, lanes]) + bias_ref[...]
            p = jnp.exp(scores - total_ref[h : h + 1, :])
            dp = dot_nt(values_ref[kv * 2 + h % 2], grad_ref[:, lanes])
            ds = low(p * (dp - spread_ref[h : h + 1, :]))
            dkeys_ref[kv] += dot_nn(ds, query_half_ref[h])
            dvalues_ref[kv] += dot_nn(low(p), grad_half_ref[h])
            dq_ref[h * 64 : h * 64 + 64, :] += dot_nn(keys_t[kv * 64 : kv * 64 + 64, :], ds)
        half = iota((rows, 128), 1) < HEAD_WIDTH
        for src, lanes in ((dkeys_ref, slice(0, 128)), (dvalues_ref, slice(128, 256))):
            first, second = src[0], src[1]
            kv_grad_ref[at, lanes] = low(
                jnp.where(half, first + pltpu.roll(first, 64, 1), second + pltpu.roll(second, 64, 1))
            )
        return nothing

    lax.fori_loop(0, own + 1, block, 0)
    dq = dq_ref[...].T * (HEAD_WIDTH**-0.5)
    cos, sin = cos_ref[...], sin_ref[...]
    for g in range(4):
        x = dq[:, g * 128 : g * 128 + 128]
        query_grad_ref[:, g * 128 : g * 128 + 128] = low(x * cos + partner(x * sin))


vmem = pl.BlockSpec(memory_space=pltpu.VMEM)
smem = pl.BlockSpec(memory_space=pltpu.SMEM)


def call(kernel, outs, args, scratch=(), first=vmem, flops=10**9):
    return pl.pallas_call(
        kernel,
        out_shape=[jax.ShapeDtypeStruct(shape, kind) for shape, kind in outs],
        in_specs=[first] + [vmem] * (len(args) - 1),
        out_specs=[vmem] * len(outs),
        scratch_shapes=[pltpu.VMEM(shape, kind) for shape, kind in scratch],
        compiler_params=pltpu.CompilerParams(vmem_limit_bytes=56 * 2**20),
        cost_estimate=pl.CostEstimate(flops=flops, bytes_accessed=10**7, transcendentals=10**6),
    )(*args)


def shifted(array, axis, by):
    devices = lax.axis_size(axis)
    pairs = [(i, i + by) for i in range(devices) if 0 <= i + by < devices]
    return lax.ppermute(array, axis, pairs)


def contract(left, right):
    return dot_tn(left, right)


def rms_scale(values, gain_vec):
    return (
        values * lax.rsqrt(jnp.mean(values * values, axis=-1, keepdims=True) + epsilon) * gain_vec
    )


def gathered(shard):
    return lax.all_gather(low(shard), "fsdp", axis=0, tiled=True)


def reduced(gradient):
    piece = lax.psum_scatter(low(gradient), "fsdp", scatter_dimension=0, tiled=True)
    return piece


def padded(vector):
    return jnp.pad(vector, (0, 128 - vector.shape[0]))[None]


def on_device(
    tokens,
    cotangent,
    segment_ids,
    norm_gain,
    ffn_gain,
    mixer_gain,
    conv_weight,
    conv_bias,
    decay_log,
    step_bias,
    skip_gain,
    in_proj,
    mixer_out,
    qkv_proj,
    attn_proj,
    gate_up,
    down_proj,
):
    place, devices = lax.axis_index("seq"), lax.axis_size("seq")
    count = tokens.shape[1]
    seg_all = lax.all_gather(segment_ids[0], "seq", axis=0, tiled=True).astype(f32)
    edge_tokens = shifted(tokens[0, count - EDGE :], "seq", 1)
    qkv_full = gathered(qkv_proj)
    in_full = gathered(in_proj)
    mix_full = gathered(mixer_out)
    attn_full = gathered(attn_proj)
    gate_full = gathered(gate_up)
    down_full = gathered(down_proj)

    seg_padded = jnp.pad(seg_all, (EDGE, EDGE), constant_values=-1.0)
    seg_ext = lax.dynamic_slice_in_dim(seg_padded, place * count, count + 2 * EDGE, 0)
    seg_wide = jnp.broadcast_to(seg_ext[:, None], (count + 2 * EDGE, 128))
    seg_row = segment_ids.astype(f32)
    seg_col = jnp.broadcast_to(seg_all[:, None], (seg_all.shape[0], 128))
    own = place.astype(jnp.int32)[None]

    position = place * count + jnp.arange(count, dtype=jnp.int32)
    half = HEAD_WIDTH // 2
    lane = jnp.arange(128, dtype=jnp.int32)
    exponent = (lane % half).astype(f32) * (2.0 / HEAD_WIDTH)
    frequencies = jnp.power(rope_base, -exponent)
    angles = position.astype(f32)[:, None] * frequencies[None, :]
    cosine = jnp.cos(angles)
    signed = jnp.sin(angles) * jnp.where(lane % HEAD_WIDTH < half, -1.0, 1.0)[None]

    token_rows = tokens[0].astype(f32)
    normed32, norm_pull = jax.vjp(rms_scale, token_rows, norm_gain)
    normed = low(normed32)
    normed_edge = low(rms_scale(edge_tokens.astype(f32), norm_gain))
    normed_ext = jnp.concatenate([normed_edge, normed], axis=0)

    qkv = dot_nn(normed, qkv_full)
    query, kv = call(
        rotate_kernel,
        [((count, 512), bf16), ((count, 256), bf16)],
        (qkv, cosine, signed),
    )
    kv_all = lax.all_gather(kv, "seq", axis=0, tiled=True)
    length = kv_all.shape[0]

    step_weights = jnp.pad(in_full[:, DI + CW :], ((0, 0), (0, 128 - MH)))
    conv_ext = dot_nn(normed_ext, in_full[:, DI : DI + CW])
    step_raw = dot_nn(normed, step_weights)
    gate_z = dot_nn(normed, in_full[:, :DI])
    bias_row, rate_row = padded(step_bias), padded(decay_log)
    act, dt, cum, end_state, passing = call(
        front_kernel,
        [
            ((count, CW), bf16),
            ((count, 128), f32),
            ((count, 128), f32),
            ((NS, DI), f32),
            ((1, DI), f32),
        ],
        (conv_ext, seg_wide, step_raw, bias_row, rate_row, conv_weight, conv_bias[None]),
    )
    pass_top, pass_rest = split(passing)
    states = lax.all_gather(
        jnp.concatenate([low(end_state), pass_top, pass_rest, jnp.zeros((14, DI), bf16)], 0), "seq"
    ).astype(f32)
    passings = states[:, NS : NS + 1] + states[:, NS + 1 : NS + 2]
    state_in = jnp.zeros((NS, DI), f32)
    for k in range(devices):
        state_in = jnp.where(k < place, passings[k] * state_in + states[k, :NS], state_in)

    attended, attended_t, log_total = call(
        attend_kernel,
        [((count, 512), bf16), ((512, count), f32), ((QUERY_HEADS, count), f32)],
        (own, query, kv_all, seg_col, seg_row),
        (
            ((count, count), f32),
            ((4, count, 128), bf16),
            ((QUERY_HEADS, count), f32),
            ((QUERY_HEADS, count), f32),
        ),
        smem,
    )
    skip_row = jnp.repeat(skip_gain, MP)[None]
    mixer_y, gated, kept = call(
        mid_kernel,
        [((count, DI), f32), ((count, DI), bf16), ((count // SUB, NS, DI), bf16)],
        (act, dt, cum, seg_wide, seg_row, state_in, gate_z, mixer_gain[None], skip_row),
        (((NS, DI), f32),),
    )
    hidden = token_rows + (dot_nn(attended, attn_full) + dot_nn(gated, mix_full))
    ffn_in32, ffn_pull = jax.vjp(rms_scale, hidden, ffn_gain)
    ffn_in = low(ffn_in32)
    gates = dot_nn(ffn_in, gate_full)

    def swiglu(values):
        return jax.nn.silu(values[:, :FF]) * values[:, FF:]

    act32, act_pull = jax.vjp(swiglu, gates)
    inner = low(act32)
    result = hidden + dot_nn(inner, down_full)
    back_rows = cotangent[0]
    down_piece = reduced(contract(inner, back_rows))
    (gates_grad,) = act_pull(dot_nt(back_rows, down_full))
    gates_grad = low(gates_grad)
    gate_piece = reduced(contract(ffn_in, gates_grad))
    hidden_extra, ffn_gain_grad = ffn_pull(dot_nt(gates_grad, gate_full))
    hidden_grad = back_rows.astype(f32) + hidden_extra
    branch = low(hidden_grad)
    attn_piece = reduced(contract(attended, branch))
    attended_grad = low(dot_nt(branch, attn_full))
    mixer_piece = reduced(contract(gated, branch))
    gated_grad = low(dot_nt(branch, mix_full))

    y_grad, gate_z_grad, mixer_gain_grad, state_grad = call(
        gate_back_kernel,
        [((count, DI), f32), ((count, DI), bf16), ((1, DI), f32), ((NS, DI), f32)],
        (gated_grad, mixer_y, act, gate_z, dt, cum, seg_wide, mixer_gain[None], skip_row),
    )
    grads = lax.all_gather(low(state_grad), "seq").astype(f32)
    later = jnp.zeros((NS, DI), f32)
    for k in reversed(range(devices)):
        later = jnp.where(k > place, passings[k] * later + grads[k], later)

    query_grad, kv_grad = call(
        attend_back_kernel,
        [((count, 512), bf16), ((length, 256), bf16)],
        (own, query, kv_all, seg_col, seg_row, attended_grad, attended_t, log_total, cosine, signed),
        (
            ((count, count), f32),
            ((4, count, 128), bf16),
            ((4, count, 128), bf16),
            ((2, count, 128), f32),
            ((2, count, 128), f32),
            ((QUERY_HEADS, count), f32),
            ((512, count), f32),
            ((QUERY_HEADS, count, 128), bf16),
            ((QUERY_HEADS, count, 128), bf16),
        ),
        smem,
    )
    kv_own = lax.psum_scatter(kv_grad, "seq", scatter_dimension=0, tiled=True).astype(f32)

    def swap(values):
        shaped = values.reshape(count, 2, 2, half)
        return shaped[:, :, ::-1].reshape(count, 128)

    key_grad = kv_own[:, :128]
    key_grad = key_grad * cosine + swap(key_grad * signed)
    qkv_grad = jnp.concatenate([query_grad, low(key_grad), low(kv_own[:, 128:])], axis=1)
    qkv_piece = reduced(contract(normed, qkv_grad))
    normed_grad = dot_nt(qkv_grad, qkv_full)

    raw_grad, conv_grad, conv_weight_grad, conv_bias_grad, rate_grad, bias_grad, skip_grad = call(
        back_kernel,
        [
            ((count, 128), f32),
            ((count + EDGE, CW), f32),
            ((KC, CW), f32),
            ((1, CW), f32),
            ((1, 128), f32),
            ((1, 128), f32),
            ((1, 128), f32),
        ],
        (
            act, dt, cum, seg_wide, seg_row, step_raw, bias_row, rate_row, kept,
            mixer_y, y_grad, later, conv_ext, conv_weight, conv_bias[None], skip_row,
        ),
        (((count, CW), f32), ((NS, DI), f32), ((count + 2 * EDGE, 128), f32)),
    )
    edge_back = shifted(conv_grad[:EDGE], "seq", -1)
    conv_grad = conv_grad[EDGE:] + jnp.pad(edge_back, ((count - EDGE, 0), (0, 0)))
    mixed_grad = jnp.concatenate([gate_z_grad, low(conv_grad), low(raw_grad[:, :MH])], axis=1)
    in_piece = reduced(contract(normed, mixed_grad))
    normed_grad = normed_grad + dot_nt(mixed_grad, in_full)
    rows_extra, norm_gain_grad = norm_pull(normed_grad)
    input_grad = hidden_grad + rows_extra
    pieces = (in_piece, mixer_piece, qkv_piece, attn_piece, gate_piece, down_piece)
    shards = [lax.psum(piece, "seq").astype(f32) for piece in pieces]
    small = lax.psum(
        (
            norm_gain_grad,
            ffn_gain_grad,
            mixer_gain_grad[0],
            conv_weight_grad,
            conv_bias_grad[0],
            rate_grad[0, :MH],
            bias_grad[0, :MH],
            skip_grad[0, :MH],
        ),
        ("fsdp", "seq"),
    )
    return (low(result)[None], input_grad[None], *small, *shards)


def solution(mesh):
    rows, whole, split_rows = P("fsdp", "seq", None), P(), P("fsdp", None)
    return jax.shard_map(
        on_device,
        mesh=mesh,
        in_specs=(rows, rows, P("fsdp", "seq"), *[whole] * 8, *[split_rows] * 6),
        out_specs=(rows, rows, *[whole] * 8, *[split_rows] * 6),
        check_vma=False,
    )
```

time: 1450 us -> 931 us (0.64)
  local copies, waits for them, and re-layouts: 347 us -> 30.2 us
  other arithmetic: 202 us -> 43.6 us
  matrix products: 244 us -> 119 us
  waiting for transfers between devices: 468 us -> 564 us
  Pallas kernels: 0 us -> 86.6 us
  blocking collectives: 134 us -> 57.1 us
    dynamic_update_slice x73 -> x0, local copies, waits for them, and re-layouts: 187 us -> none  [the longest x72 187 us: ssd_local(): lax.scan(ssd_block, start_state, (values_in.reshape(block_count, SUB, MH,...]
    all_gather x8 -> x9, waiting for transfers between devices: 74.9 us -> 221 us  [the longest x6 170 us: gathered(): return lax.all_gather(low(shard), 'fsdp', axis=0, tiled=True)]
    dot_general x76 -> x20, matrix products: 244 us -> 119 us  [the longest x6 43.5 us: dot_nt(): lax.dot_general(left, right, (((1,), (1,)), ((), ())), preferred_element_...]
    pallas_call x0 -> x7, Pallas kernels: none -> 86.6 us  [call(): pl.pallas_call(kernel, out_shape=[jax.ShapeDtypeStruct(shape, kind) for s...]
    dynamic_slice x47 -> x1, local copies, waits for them, and re-layouts: 55.2 us -> 0.09 us  [on_device(): lax.dynamic_slice_in_dim(seg_padded, place * count, count + 2 * EDGE, 0)]
    dynamic_update_slice x24 -> x0, other arithmetic: 43.8 us -> none  [ssd_local(): lax.scan(ssd_block, start_state, (values_in.reshape(block_count, SUB, MH,...]
    reduce_sum x22 -> x0, other arithmetic: 41.4 us -> none  [the longest x1 11.1 us: conv_apply(): weight[offset][None, :] * padded[offset:offset + count_of_rows]]
    unnamed x1 -> x0, blocking collectives: 39.8 us -> none
  transfers between devices with their start and end apart: 20 -> 19, of which waited for: 13 -> 17; matrix products, arithmetic and copies ran while one was open for 51% -> 16% of each run, Pallas kernels for 0% -> 8%
where the time goes in v1:
time: 931 us; the launch traced here: 923 us
  waiting for transfers between devices  564 us (61%)
  matrix products  119 us (13%)
  Pallas kernels  86.6 us (9%)
  blocking collectives  57.1 us (6%)
  other arithmetic  43.6 us (5%)
  local copies, waits for them, and re-layouts  30.2 us (3%)
  between operations  14.7 us (2%)
    reduce_scatter x5, waiting for transfers between devices, reduced(): lax.psum_scatter(low(gradient), 'fsdp', scatter_dimension=0, tiled=True)  258 us
    all_gather x6, waiting for transfers between devices, gathered(): return lax.all_gather(low(shard), 'fsdp', axis=0, tiled=True)  170 us
    pallas_call x7, Pallas kernels, call(): pl.pallas_call(kernel, out_shape=[jax.ShapeDtypeStruct(shape, kind) for s...  86.6 us
    psum x1, waiting for transfers between devices, on_device(): shards = [lax.psum(piece, 'seq').astype(f32) for piece in pieces]  54.9 us
    psum x1, blocking collectives, on_device(): lax.psum((norm_gain_grad, ffn_gain_grad, mixer_gain_grad[0], conv_weight_...  45 us
    dot_general x6, matrix products, dot_nt(): lax.dot_general(left, right, (((1,), (1,)), ((), ())), preferred_element_...  43.5 us
    dot_general x8, matrix products, dot_nn(): return jnp.dot(left, right, preferred_element_type=jnp.float32)  40.9 us
    dot_general x6, matrix products, dot_tn(): lax.dot_general(left, right, (((0,), (0,)), ((), ())), preferred_element_...  34.9 us
  transfers between devices with their start and end apart: 19, of which 17 were waited for; matrix products, arithmetic and copies ran while one was open for 16% of the time, Pallas kernels for 8%

profile of v1, /device:TPU:0, one launch (start us, length us, event | category | flops | bytes accessed | tf_op | source)
XLA Modules:
  0.0 922.7 jit_solution(7883580727739384142)
XLA Ops:
  7.2 1.8 convert_element_type.153
  9.1 2.4 convert_element_type.161
  11.7 4.9 collective-permute-start
  16.6 12.1 %all-gather = s32[1,2048]{1,0:T(1,128)S(1)} all-gather(s32[1,512]{1,0:T(1,128)S(1)} %copy-done.31), channel_id=2, replica_groups=mesh['fsdp'=8,'seq'=4] {'seq'}, dimensions={1}, use_global_device_ids=true | all-gather | bytes 10240 | tf_op jit(solution)/shard_map/all_gather | solution.py:539
  29.2 1.8 fusion.40
  32.8 6.1 all-gather.13.cloned.1.call-done
  38.9 3.5 fusion.63.qkv_ref
  42.5 3.0 shard_map.288
  45.5 45.1 %all-gather.19.cloned.1.call-done = bf16[1024,3352]{0,1:T(8,128)(2,1)} async-done(((bf16[128,3352]{0,1:T(8,128)(2,1)}), bf16[1024,3352]{0,1:T(8,128)(2,1)}) %all-gather.19.cloned.1.call-update) | async-done | bytes 6864912 | tf_op jit(solution)/shard_map/all_gather | solution.py:506
  92.5 6.0 fusion.3.conv_ref
  99.4 10.3 %shard_map.290 = (bf16[512,1792]{1,0:T(8,128)(2,1)}, f32[512,128]{1,0:T(8,128)}, f32[512,128]{1,0:T(8,128)}, f32[128,1536]{1,0:T(8,128)}, f32[1,1536]{1,0:T(1,128)}) custom-call(f32[520,1792]{1,0:T(8,128)} %fusion.3.conv_ref, f32[528,128]{1,0:T(8,128)} %broadcast_in_dim.68.seg_ref, f32[512,128]{1,0:T(8,128)} %fusion.41.raw_ref, ...), custom_call_target="tpu_custom_call" | custom-call | flops 1000000000 | bytes 10000000 | tf_op jit(solution)/shard_map/pallas_call | solution.py:478
  114.4 2.8 convert_element_type.169
  120.7 1.3 broadcast_in_dim.67.segcol_ref
  122.0 7.9 shard_map.289
  129.9 5.5 fusion.5.z_ref
  135.4 27.1 %all-gather.27.cloned.1.call-done = bf16[576,1536]{1,0:T(8,128)(2,1)} async-done(((bf16[144,1536]{1,0:T(8,128)(2,1)}), bf16[576,1536]{1,0:T(8,128)(2,1)}) %all-gather.27.cloned.1.call-update) | async-done | bytes 1769488 | tf_op jit(solution)/shard_map/all_gather | solution.py:596
  162.6 1.9 convert.8
  165.8 13.3 %shard_map.291 = (f32[512,1536]{1,0:T(8,128)}, bf16[512,1536]{1,0:T(8,128)(2,1)}, bf16[4,128,1536]{2,1,0:T(8,128)(2,1)}) custom-call(bf16[512,1792]{1,0:T(8,128)(2,1)} %get-tuple-element.45.act_ref, f32[512,128]{1,0:T(8,128)} %get-tuple-element.46.dt_ref, f32[512,128]{1,0:T(8,128)} %get-tuple-element.47.cum_ref, f32[528,128]{1,0:T(8,128)} %broadcast_in_dim.68.seg_ref, ...), custom_call_target="tpu_custom_call" | custom-call | flops 1000000000 | bytes 10000000 | tf_op jit(solution)/shard_map/pallas_call | solution.py:478
  179.1 17.0 %all-gather.21.cloned.1.call-done = bf16[1536,1024]{1,0:T(8,128)(2,1)} async-done(((bf16[192,1024]{1,0:T(8,128)(2,1)}), bf16[1536,1024]{1,0:T(8,128)(2,1)}) %all-gather.21.cloned.1.call-update) | async-done | bytes 3145744 | tf_op jit(solution)/shard_map/all_gather | solution.py:506
  196.1 5.5 fusion.64
  201.6 19.8 %all-gather.17.cloned.1.call-done = bf16[512,1024]{1,0:T(8,128)(2,1)} async-done(((bf16[64,1024]{1,0:T(8,128)(2,1)}), bf16[512,1024]{1,0:T(8,128)(2,1)}) %all-gather.17.cloned.1.call-update) | async-done | bytes 1048592 | tf_op jit(solution)/shard_map/all_gather | solution.py:506
  221.4 2.9 multiply_reduce_fusion.2
  224.3 53.9 %all-gather.23.cloned.1.call-done = bf16[1024,4096]{1,0:T(8,128)(2,1)} async-done(((bf16[128,4096]{1,0:T(8,128)(2,1)}), bf16[1024,4096]{1,0:T(8,128)(2,1)}) %all-gather.23.cloned.1.call-update) | async-done | bytes 8388624 | tf_op jit(solution)/shard_map/all_gather | solution.py:506
  278.3 10.2 %fusion.60 = f32[512,4096]{1,0:T(8,128)} fusion(bf16[1024,4096]{1,0:T(8,128)(2,1)} %all-gather.23.cloned.1.call-done, f32[512,1024]{1,0:T(8,128)S(1)} %get-tuple-element.98, f32[1024]{0:T(1024)S(1)} %copy-done.27, f32[512]{0:T(512)S(1)} %fusion.47), kind=kOutput, calls=%fused_computation.128 | convolution fusion | flops 4296540160 | bytes 18880512 | tf_op jit(solution)/shard_map/dot_general | solution.py:29
  288.4 28.4 %all-gather.25.cloned.1.call-done = bf16[2048,1024]{1,0:T(8,128)(2,1)} async-done(((bf16[256,1024]{1,0:T(8,128)(2,1)}), bf16[2048,1024]{1,0:T(8,128)(2,1)}) %all-gather.25.cloned.1.call-update) | async-done | bytes 4194320 | tf_op jit(solution)/shard_map/all_gather | solution.py:506
  316.9 12.6 %fusion.36 = (f32[512,2048]{1,0:T(8,128)}, f32[512,2048]{1,0:T(8,128)}, bf16[512,2048]{1,0:T(8,128)(2,1)}) fusion(f32[512,4096]{1,0:T(8,128)} %fusion.60, bf16[2048,1024]{1,0:T(8,128)(2,1)} %all-gather.25.cloned.1.call-done, bf16[1,512,1024]{2,1,0:T(8,128)(2,1)} %param.18), kind=kOutput, calls=%fused_computation.72 | convolution fusion | flops 2162163712 | bytes 24117248 | tf_op jit(solution)/shard_map/dot_general | solution.py:33
  329.5 10.6 %multiply_reduce_fusion = (f32[1024]{0:T(1024)}, f32[512]{0:T(512)S(1)}, f32[512,1024]{1,0:T(8,128)S(1)}) fusion(f32[512,1024]{1,0:T(8,128)S(1)} %get-tuple-element.98, f32[512]{0:T(512)S(1)} %fusion.47, f32[1024]{0:T(1024)S(1)} %copy-done.27, bf16[1024,4096]{1,0:T(8,128)(2,1)} %all-gather.23.cloned.1.call-done, f32[512,2048]{1,0:T(8,128)} %get-tuple-element.91, ...), kind=kOutput, calls=%fused_computation.34 | convolution fusion | flops 4302305792 | bytes 20983808 | tf_op jit(solution)/shard_map/dot_general | solution.py:33
  341.5 1.3 copy-done.39
  342.8 2.9 convolution_convert_fusion.4.grad_ref
  345.8 11.4 %shard_map.293 = (f32[512,1536]{1,0:T(8,128)}, bf16[512,1536]{1,0:T(8,128)(2,1)}, f32[1,1536]{1,0:T(1,128)}, f32[128,1536]{1,0:T(8,128)}) custom-call(bf16[512,1536]{1,0:T(8,128)(2,1)} %convolution_convert_fusion.4.grad_ref, f32[512,1536]{1,0:T(8,128)} %get-tuple-element.55.y_ref, bf16[512,1792]{1,0:T(8,128)(2,1)} %get-tuple-element.45.act_ref, ...), custom_call_target="tpu_custom_call" | custom-call | flops 1000000000 | bytes 10000000 | tf_op jit(solution)/shard_map/pallas_call | solution.py:478
  357.2 1.9 convert_element_type.179
  359.2 3.1 convolution_convert_fusion.7.grad_ref
  362.3 10.9 %shard_map.292 = (bf16[512,512]{1,0:T(8,128)(2,1)}, bf16[2048,256]{1,0:T(8,128)(2,1)}) custom-call(s32[1]{0:T(128)} %bitcast.1.own_ref, bf16[512,512]{1,0:T(8,128)(2,1)} %get-tuple-element.42.query_ref, bf16[2048,256]{1,0:T(8,128)(2,1)} %all-gather.15.cloned.1.call-done.kv_ref, f32[2048,128]{1,0:T(8,128)} %broadcast_in_dim.67.segcol_ref, ...), custom_call_target="tpu_custom_call" | custom-call | flops 1000000000 | bytes 10000000 | tf_op jit(solution)/shard_map/pallas_call | solution.py:478
  373.3 23.2 %all-gather.29.cloned.1.call-done = bf16[512,1536]{1,0:T(8,128)(2,1)} async-done(((bf16[128,1536]{1,0:T(8,128)(2,1)}), bf16[512,1536]{1,0:T(8,128)(2,1)}) %all-gather.29.cloned.1.call-update) | async-done | bytes 1572880 | tf_op jit(solution)/shard_map/all_gather | solution.py:652
  396.4 1.8 convert_element_type.197
  399.5 29.8 %shard_map.294 = (f32[512,128]{1,0:T(8,128)}, f32[520,1792]{1,0:T(8,128)}, f32[4,1792]{1,0:T(4,128)}, f32[1,1792]{1,0:T(1,128)}, f32[1,128]{1,0:T(1,128)}, /*index=5*/f32[1,128]{1,0:T(1,128)}, f32[1,128]{1,0:T(1,128)}) custom-call(bf16[512,1792]{1,0:T(8,128)(2,1)} %get-tuple-element.45.act_ref, f32[512,128]{1,0:T(8,128)} %get-tuple-element.46.dt_ref, ...), custom_call_target="tpu_custom_call" | custom-call | flops 1000000000 | bytes 10000000 | tf_op jit(solution)/shard_map/pallas_call | solution.py:478
  430.1 1.3 collective-permute-start.1
  432.4 3.8 collective-permute-done.1
  436.2 2.2 add_convert_fusion.1
  439.6 5.9 convolution_convert_fusion.1
  445.5 9.9 %copy.37 = bf16[1024,3352]{1,0:T(8,128)(2,1)} copy(bf16[1024,3352]{0,1:T(8,128)(2,1)} %convolution_convert_fusion.1) | data formatting | bytes 13729792
  455.5 3.1 convolution_convert_fusion.6
  458.7 1.9 convert_multiply_fusion.4
  461.5 1.7 rev.3
  465.3 1.9 fusion.39
  467.2 3.8 convolution_convert_fusion.5
  471.1 5.2 convolution_convert_fusion.3
  476.8 6.4 convolution_convert_fusion.2
  483.9 10.5 %convolution_convert_fusion = bf16[1024,4096]{1,0:T(8,128)(2,1)} fusion(f32[512,2048]{1,0:T(8,128)} %get-tuple-element.91, f32[512,2048]{1,0:T(8,128)} %get-tuple-element.90, f32[512,1024]{1,0:T(8,128)S(1)} %get-tuple-element.98, f32[1024]{0:T(1024)S(1)} %copy-done.28, f32[512]{0:T(512)S(1)} %fusion.47), kind=kOutput, calls=%fused_computation.1 | convolution fusion | flops 4304928768 | bytes 18880512 | tf_op jit(solution)/shard_map/dot_general | solution.py:39
  494.4 25.4 %reduce-scatter.22.cloned.1.call-done = bf16[128,3352]{1,0:T(8,128)(2,1)} async-done(((bf16[1024,3352]{1,0:T(8,128)(2,1)}), bf16[128,3352]{1,0:T(8,128)(2,1)}) %reduce-scatter.22.cloned.1.call-update) | async-done | bytes 858128
  519.8 2.2 copy.38
  522.0 37.5 %reduce-scatter.16.cloned.1.call-done = bf16[64,1024]{1,0:T(8,128)(2,1)} async-done(((bf16[512,1024]{1,0:T(8,128)(2,1)}), bf16[64,1024]{1,0:T(8,128)(2,1)}) %reduce-scatter.16.cloned.1.call-update) | async-done | bytes 131088 | tf_op jit(solution)/shard_map/reduce_scatter | solution.py:510
  559.5 41.8 %reduce-scatter.14.cloned.1.call-done = bf16[128,768]{1,0:T(8,128)(2,1)} async-done(((bf16[1024,768]{1,0:T(8,128)(2,1)}), bf16[128,768]{1,0:T(8,128)(2,1)}) %reduce-scatter.14.cloned.1.call-update) | async-done | bytes 196624 | tf_op jit(solution)/shard_map/reduce_scatter | solution.py:510
  601.3 49.5 %reduce-scatter.12.cloned.1.call-done = bf16[192,1024]{1,0:T(8,128)(2,1)} async-done(((bf16[1536,1024]{1,0:T(8,128)(2,1)}), bf16[192,1024]{1,0:T(8,128)(2,1)}) %reduce-scatter.12.cloned.1.call-update) | async-done | bytes 393232 | tf_op jit(solution)/shard_map/reduce_scatter | solution.py:510
  650.8 54.9 %reduce-scatter.20.cloned.1.call-done = bf16[256,1024]{1,0:T(8,128)(2,1)} async-done(((bf16[2048,1024]{1,0:T(8,128)(2,1)}), bf16[256,1024]{1,0:T(8,128)(2,1)}) %reduce-scatter.20.cloned.1.call-update) | async-done | bytes 524304 | tf_op jit(solution)/shard_map/reduce_scatter | solution.py:510
  705.7 74.6 %reduce-scatter.18.cloned.1.call-done = bf16[128,4096]{1,0:T(8,128)(2,1)} async-done(((bf16[1024,4096]{1,0:T(8,128)(2,1)}), bf16[128,4096]{1,0:T(8,128)(2,1)}) %reduce-scatter.18.cloned.1.call-update) | async-done | bytes 1048592 | tf_op jit(solution)/shard_map/reduce_scatter | solution.py:510
  780.4 6.2 fusion.16
  786.6 3.9 fusion.37
  793.2 10.2 %fusion.10 = (f32[1024]{0:T(1024)S(1)}, f32[512]{0:T(512)S(1)}, f32[512,1024]{1,0:T(8,128)}) fusion(bf16[1,512,1024]{2,1,0:T(8,128)(2,1)S(1)} %copy-done, f32[512]{0:T(512)} %copy-done.21, f32[1024]{0:T(1024)S(1)} %copy-done.19, f32[512,1024]{1,0:T(8,128)} %fusion.37, bf16[1024,3352]{0,1:T(8,128)(2,1)} %all-gather.19.cloned.1.call-done, ...), kind=kOutput, calls=%fused_computation.28 | convolution fusion | flops 3529316864 | bytes 15552512 | tf_op jit(solution)/shard_map/dot_general | solution.py:33
  803.4 45.0 %all-reduce.7 = (f32[1024]{0:T(1024)}, f32[1024]{0:T(1024)}, f32[1536]{0:T(1024)}, f32[4,1792]{1,0:T(4,128)}, f32[1792]{0:T(1024)}, /*index=5*/f32[24]{0:T(128)}, f32[24]{0:T(128)}, f32[24]{0:T(128)}) all-reduce(f32[1024]{0:T(1024)S(1)} %get-tuple-element.70, ...), channel_id=1, replica_groups=mesh['fsdp'=8,'seq'=4] {'fsdp','seq'}, use_global_device_ids=true, to_apply=%region_7.8 | all-reduce | flops 12616 | bytes 100928 | tf_op jit(solution)/shard_map/psum | solution.py:712
  848.5 4.9 fusion.13
  853.4 54.9 %all-reduce.11.cloned.1.call-done = (bf16[128,3352]{0,1:T(8,128)(2,1)}, bf16[192,1024]{1,0:T(8,128)(2,1)}, bf16[128,768]{1,0:T(8,128)(2,1)}, bf16[64,1024]{1,0:T...) async-done(((bf16[128,3352]{0,1:T(8,128)(2,1)}, bf16[192,1024]{1,0:T(8,128)(2,1)}, bf16[128,768]{1,0:T(8,128)(2,1)}, bf16[64,1024]{1,0:T(8,128)(2,1)}, ...) | async-done | bytes 3151888 | tf_op jit(solution)/shard_map/psum | solution.py:711
  908.3 2.6 convert_element_type.183
  913.4 1.5 convert_element_type.191
  (171 shorter events, 30.8 us)
Async XLA Ops:
  7.2 4.5 copy-start
  7.2 9.4 %copy-start.31 = (s32[1,512]{1,0:T(1,128)S(1)}, s32[1,512]{1,0:T(1,128)}, u32[]{:S(2)}) copy-start(s32[1,512]{1,0:T(1,128)} %param.19) | copy-start | bytes 6148
  7.2 31.7 %all-gather.13.cloned.1.call-start = ((), (), s32[]{:S(2)}) async-start(), calls=%async_computation.7 | async-start | bytes 1769472 | tf_op jit(solution)/shard_map/all_gather | solution.py:506
  9.0 22.0 %copy-start.19 = (f32[1024]{0:T(1024)S(1)}, f32[1024]{0:T(1024)}, u32[]{:S(2)}) copy-start(f32[1024]{0:T(1024)} %param.20) | copy-start | bytes 12292
  9.1 81.6 %all-gather.19.cloned.1.call-start = ((), (), s32[]{:S(2)}) async-start(), calls=%async_computation.10 | async-start | bytes 7723008 | tf_op jit(solution)/shard_map/all_gather | solution.py:506
  11.6 19.8 %copy-start.37 = (f32[24]{0:T(128)S(1)}, f32[24]{0:T(128)}, u32[]{:S(2)}) copy-start(f32[24]{0:T(128)} %param.25) | copy-start | bytes 292
  11.6 19.8 %copy-start.38 = (f32[24]{0:T(128)S(1)}, f32[24]{0:T(128)}, u32[]{:S(2)}) copy-start(f32[24]{0:T(128)} %param.26) | copy-start | bytes 292
  11.6 20.3 %copy-start.32 = (f32[1792]{0:T(1024)S(1)}, f32[1792]{0:T(1024)}, u32[]{:S(2)}) copy-start(f32[1792]{0:T(1024)} %param.24) | copy-start | bytes 21508
  11.6 109.1 %all-gather.15.cloned.1.call-start = ((), (), s32[]{:S(2)}) async-start(), calls=%async_computation.8 | async-start | bytes 1310720 | tf_op jit(solution)/shard_map/all_gather | solution.py:576
  11.7 20.9 %collective-permute-start = (bf16[8,1024]{1,0:T(8,128)(2,1)S(1)}, bf16[8,1024]{1,0:T(8,128)(2,1)S(1)}, u32[]{:S(2)}, u32[]{:S(2)}) collective-permute-start(bf16[8,1024]{1,0:T(8,128)(2,1)S(1)} %slice_bitcast_fusion.4), channel_id=1, source_target_pairs={{0,1},{1,2},{2,3},{4,5},{5,6},{6,7},{8,9},{9,10},{10,11},{12,13},{... | collective-permute-start | bytes 49160 | tf_op jit(solution)/shard_map/ppermute | solution.py:492
  28.8 430.0 %copy-start.34 = (f32[128]{0:T(128)}, f32[128]{0:T(128)S(1)}, u32[]{:S(2)}) copy-start(f32[128]{0:T(128)S(1)} %fusion.51) | copy-start | bytes 1540
  29.2 13.3 %copy-start.25 = (f32[512]{0:T(512)}, f32[512]{0:T(512)S(1)}, u32[]{:S(2)}) copy-start(f32[512]{0:T(512)S(1)} %fusion.14) | copy-start | bytes 6148
  29.2 13.3 %copy-start.21 = (f32[512]{0:T(512)}, f32[512]{0:T(512)S(1)}, u32[]{:S(2)}) copy-start(f32[512]{0:T(512)S(1)} %fusion.46) | copy-start | bytes 6148
  31.4 98.6 %copy-start.2 = (bf16[512,1024]{1,0:T(8,128)(2,1)}, bf16[512,1024]{1,0:T(8,128)(2,1)S(1)}, u32[]{:S(2)}) copy-start(bf16[512,1024]{1,0:T(8,128)(2,1)S(1)} %fusion.9) | copy-start | bytes 3145732
  45.5 117.1 %all-gather.27.cloned.1.call-start = ((), (), s32[]{:S(2)}) async-start(), calls=%async_computation.20 | async-start | bytes 2211840 | tf_op jit(solution)/shard_map/all_gather | solution.py:596
  109.7 3.0 copy-start.9
  109.7 3.9 copy-start.12
  112.7 83.4 %all-gather.21.cloned.1.call-start = ((), (), s32[]{:S(2)}) async-start(), calls=%async_computation.11 | async-start | bytes 3538944 | tf_op jit(solution)/shard_map/all_gather | solution.py:506
  113.6 107.8 %all-gather.17.cloned.1.call-start = ((), (), s32[]{:S(2)}) async-start(), calls=%async_computation.9 | async-start | bytes 1179648 | tf_op jit(solution)/shard_map/all_gather | solution.py:506
  114.4 2.9 copy-start.7
  114.4 163.9 %all-gather.23.cloned.1.call-start = ((), (), s32[]{:S(2)}) async-start(), calls=%async_computation.12 | async-start | bytes 9437184 | tf_op jit(solution)/shard_map/all_gather | solution.py:506
  117.2 1.6 copy-start.30
  117.2 2.2 copy-start.36
  117.2 199.6 %all-gather.25.cloned.1.call-start = ((), (), s32[]{:S(2)}) async-start(), calls=%async_computation.13 | async-start | bytes 4718592 | tf_op jit(solution)/shard_map/all_gather | solution.py:506
  118.2 278.2 %all-gather.29.cloned.1.call-start = ((), (), s32[]{:S(2)}) async-start(), calls=%async_computation.21 | async-start | bytes 1966080 | tf_op jit(solution)/shard_map/all_gather | solution.py:652
  221.4 56.9 %copy-start.27 = (f32[1024]{0:T(1024)S(1)}, f32[1024]{0:T(1024)}, u32[]{:S(2)}) copy-start(f32[1024]{0:T(1024)} %param.21) | copy-start | bytes 12292
  224.3 259.0 %copy-start.23 = (f32[512]{0:T(512)}, f32[512]{0:T(512)S(1)}, u32[]{:S(2)}) copy-start(f32[512]{0:T(512)S(1)} %fusion.47) | copy-start | bytes 6148
  329.5 10.7 %copy-start.4 = (bf16[1,512,1024]{2,1,0:T(8,128)(2,1)S(1)}, bf16[1,512,1024]{2,1,0:T(8,128)(2,1)}, u32[]{:S(2)}) copy-start(bf16[1,512,1024]{2,1,0:T(8,128)(2,1)} %param.18) | copy-start | bytes 3145732
  340.2 1.3 copy-start.1
  340.2 2.6 copy-start.39
  342.8 3.0 copy-start.8
  359.2 99.6 %reduce-scatter.10.cloned.1.call-start = ((), (), s32[]{:S(2)}) async-start(), calls=%async_computation.14 | async-start | bytes 1310720 | tf_op jit(solution)/shard_map/reduce_scatter | solution.py:674
  373.2 146.6 %reduce-scatter.22.cloned.1.call-start = ((), (), s32[]{:S(2)}) async-start(), calls=%async_computation.22 | async-start | bytes 7962624
  430.1 6.1 collective-permute-start.1
  432.4 6.0 copy-start.15
  432.4 7.2 copy-start.3
  432.4 7.2 copy-start.40
  438.4 1.2 copy-start.5
  455.5 104.0 %reduce-scatter.16.cloned.1.call-start = ((), (), s32[]{:S(2)}) async-start(), calls=%async_computation.17 | async-start | bytes 1179648 | tf_op jit(solution)/shard_map/reduce_scatter | solution.py:510
  458.7 142.6 %reduce-scatter.14.cloned.1.call-start = ((), (), s32[]{:S(2)}) async-start(), calls=%async_computation.16 | async-start | bytes 1769472 | tf_op jit(solution)/shard_map/reduce_scatter | solution.py:510
  465.3 1.9 copy-start.17
  471.1 179.7 %reduce-scatter.12.cloned.1.call-start = ((), (), s32[]{:S(2)}) async-start(), calls=%async_computation.15 | async-start | bytes 3538944 | tf_op jit(solution)/shard_map/reduce_scatter | solution.py:510
  476.4 229.3 %reduce-scatter.20.cloned.1.call-start = ((), (), s32[]{:S(2)}) async-start(), calls=%async_computation.19 | async-start | bytes 4718592 | tf_op jit(solution)/shard_map/reduce_scatter | solution.py:510
  483.2 0.7 copy-start.28
  483.3 297.1 %reduce-scatter.18.cloned.1.call-start = ((), (), s32[]{:S(2)}) async-start(), calls=%async_computation.18 | async-start | bytes 9437184 | tf_op jit(solution)/shard_map/reduce_scatter | solution.py:510
  494.4 413.9 %all-reduce.11.cloned.1.call-start = ((), (), s32[]{:S(2)}) async-start(), calls=%async_computation.23 | async-start | bytes 6303744 | tf_op jit(solution)/shard_map/psum | solution.py:711
  780.3 6.2 copy-start.33
  780.4 6.2 copy-start.18
  786.6 6.6 copy-start.16
  793.2 10.3 %copy-start.20 = (f32[4,1792]{1,0:T(4,128)S(1)}, f32[4,1792]{1,0:T(4,128)}, u32[]{:S(2)}) copy-start(f32[4,1792]{1,0:T(4,128)} %get-tuple-element.63) | copy-start | bytes 86020
  793.2 10.3 %copy-start.35 = (f32[1024]{0:T(1024)S(1)}, f32[1024]{0:T(1024)}, u32[]{:S(2)}) copy-start(f32[1024]{0:T(1024)} %get-tuple-element.68) | copy-start | bytes 12292
  793.2 55.3 %copy-start.26 = (f32[512]{0:T(512)S(1)}, f32[512]{0:T(512)}, u32[]{:S(2)}) copy-start(f32[512]{0:T(512)} %copy-done.25) | copy-start | bytes 6148
  793.2 55.3 %copy-start.22 = (f32[512]{0:T(512)S(1)}, f32[512]{0:T(512)}, u32[]{:S(2)}) copy-start(f32[512]{0:T(512)} %copy-done.21) | copy-start | bytes 6148
  793.2 55.3 %copy-start.24 = (f32[512]{0:T(512)S(1)}, f32[512]{0:T(512)}, u32[]{:S(2)}) copy-start(f32[512]{0:T(512)} %copy-done.23) | copy-start | bytes 6148
  793.2 55.3 %copy-start.29 = (f32[1024]{0:T(1024)S(1)}, f32[1024]{0:T(1024)}, u32[]{:S(2)}) copy-start(f32[1024]{0:T(1024)} %param.21) | copy-start | bytes 12292
  908.3 2.6 copy-start.11
  908.3 3.6 copy-start.13
  908.3 4.3 copy-start.14
  908.3 5.1 copy-start.6
  911.9 3.0 copy-start.10
Sparse Core Ops, SparseCore 0:
  10.5 28.3 all-gather.12
  41.4 49.1 all-gather.18
  92.8 27.9 all-gather.14
  122.7 39.8 all-gather.26
  164.9 31.1 all-gather.20
  197.8 23.4 all-gather.16
  223.8 54.3 all-gather.22
  280.1 36.7 all-gather.24
  359.3 37.0 all-gather.28
  398.6 25.9 reduce-scatter.9
  455.6 64.1 reduce-scatter.21
  523.4 36.0 reduce-scatter.15
  562.8 38.4 reduce-scatter.13
  604.5 46.2 reduce-scatter.11
  654.4 51.3 reduce-scatter.19
  709.0 71.2 reduce-scatter.17
  783.8 124.4 all-reduce.10

commit v2 on v1

--- a/solution.py
+++ b/solution.py
@@ -93,9 +93,8 @@
     return low(values).astype(jnp.float32)
 
 
-def front_kernel(conv_ref, seg_ref, raw_ref, bias_ref, rate_ref, weight_ref, cbias_ref,
-                 act_ref, dt_ref, cum_ref, end_ref, pass_ref):
-    chunks = raw_ref.shape[0] // SUB
+def front_conv(conv_ref, seg_ref, weight_ref, cbias_ref, act_ref):
+    chunks = act_ref.shape[0] // SUB
 
     def tile(j, carry):
         col = pl.ds(pl.multiple_of(j * 128, 128), 128)
@@ -112,6 +111,10 @@
         return carry
 
     lax.fori_loop(0, CW // 128, tile, 0)
+
+
+def front_state(seg_ref, raw_ref, bias_ref, rate_ref, act_ref, dt_ref, cum_ref, end_ref, pass_ref):
+    chunks = raw_ref.shape[0] // SUB
     spread = spreader()
     lower = jnp.where(iota((SUB, SUB), 0) >= iota((SUB, SUB), 1), 1.0, 0.0)
     end_ref[...] = jnp.zeros_like(end_ref)
@@ -136,10 +139,10 @@
 
 
 def mid_kernel(act_ref, dt_ref, cum_ref, seg_ref, segrow_ref, state_ref, z_ref, gain_ref, skip_ref,
-               y_ref, gated_ref, kept_ref, carry_ref):
-    chunks = act_ref.shape[0] // SUB
+               y_ref, gated_ref, kept_ref, carry_ref, first, until):
     spread = spreader()
-    carry_ref[...] = state_ref[...]
+    if first == 0:
+        carry_ref[...] = state_ref[...]
     half = lane_halves(SUB)
 
     def chunk(c, nothing):
@@ -178,7 +181,7 @@
         gated_ref[rows, :] = low(g * scale * gain_ref[...])
         return nothing
 
-    lax.fori_loop(0, chunks, chunk, 0)
+    lax.fori_loop(first, until, chunk, 0)
 
 
 def gate_back_kernel(grad_ref, y_ref, act_ref, z_ref, dt_ref, cum_ref, seg_ref, gain_ref, skip_ref,
@@ -380,41 +383,48 @@
     bias_ref[...] = jnp.where(causal & (seg == segrow_ref[...]), 0.0, -1e30)
 
 
-def attend_kernel(own_ref, query_ref, kv_ref, segcol_ref, segrow_ref, out_ref, out_t_ref, total_ref,
-                  bias_ref, keys_ref, top_ref, sum_ref):
-    rows = query_ref.shape[0]
-    own = own_ref[0]
+def attend_start(top_ref, sum_ref, out_t_ref):
     top_ref[...] = jnp.full_like(top_ref, -1e30)
     sum_ref[...] = jnp.zeros_like(sum_ref)
     out_t_ref[...] = jnp.zeros_like(out_t_ref)
 
-    def block(i, nothing):
-        b = own - i
-        at = pl.ds(pl.multiple_of(b * rows, rows), rows)
-        attend_bias(b, own, rows, segcol_ref, segrow_ref, bias_ref)
-        lane_variants(kv_ref[at, 0:128].astype(jnp.float32), keys_ref)
-        values_t = low(kv_ref[at, 128:256].astype(jnp.float32).T)
-        for h in range(QUERY_HEADS):
-            g, kv = h // 2, h // 4
-            scores = dot_nt(keys_ref[kv * 2 + h % 2], query_ref[:, g * 128 : g * 128 + 128])
+
+def attend_block(b, own, query_ref, kv_ref, segcol_ref, segrow_ref, out_t_ref, bias_ref, keys_ref,
+                 values_t_ref, top_ref, sum_ref):
+    rows = query_ref.shape[0]
+    at = pl.ds(pl.multiple_of(b * rows, rows), rows)
+    attend_bias(b, own, rows, segcol_ref, segrow_ref, bias_ref)
+    lane_variants(kv_ref[at, 0:128].astype(jnp.float32), keys_ref)
+    values_t_ref[...] = low(kv_ref[at, 128:256].astype(jnp.float32).T)
+
+    def pair(g, nothing):
+        kv = g // 2
+        query = query_ref[:, pl.ds(pl.multiple_of(g * 128, 128), 128)]
+        for side in range(2):
+            h = g * 2 + side
+            row = pl.ds(pl.multiple_of(h * 8, 8), 8)
+            scores = dot_nt(keys_ref[kv * 2 + side], query)
             scores = scores + bias_ref[...]
-            old = top_ref[h : h + 1, :]
+            old = top_ref[row, :][0:1]
             top = jnp.maximum(old, jnp.max(scores, axis=0, keepdims=True))
             p = jnp.exp(scores - top)
             fade = jnp.exp(old - top)
-            top_ref[h : h + 1, :] = top
-            sum_ref[h : h + 1, :] = sum_ref[h : h + 1, :] * fade + jnp.sum(p, 0, keepdims=True)
-            at_h = slice(h * 64, h * 64 + 64)
-            out_t_ref[at_h, :] = out_t_ref[at_h, :] * fade + dot_nn(
-                values_t[kv * 64 : kv * 64 + 64, :], low(p)
-            )
+            total = sum_ref[row, :][0:1] * fade + jnp.sum(p, 0, keepdims=True)
+            top_ref[row, :] = jnp.broadcast_to(top, (8, rows))
+            sum_ref[row, :] = jnp.broadcast_to(total, (8, rows))
+            at_h = pl.ds(pl.multiple_of(h * 64, 64), 64)
+            values_t = values_t_ref[pl.ds(pl.multiple_of(kv * 64, 64), 64), :]
+            out_t_ref[at_h, :] = out_t_ref[at_h, :] * fade + dot_nn(values_t, low(p))
         return nothing
 
-    lax.fori_loop(0, own + 1, block, 0)
-    total_ref[...] = top_ref[...] + jnp.log(sum_ref[...])
+    lax.fori_loop(0, QUERY_HEADS // 2, pair, 0)
+
+
+def attend_finish(out_ref, out_t_ref, total_ref, top_ref, sum_ref):
     for h in range(QUERY_HEADS):
         at_h = slice(h * 64, h * 64 + 64)
-        out_t_ref[at_h, :] = out_t_ref[at_h, :] / sum_ref[h : h + 1, :]
+        total_ref[h : h + 1, :] = top_ref[h * 8 : h * 8 + 1, :] + jnp.log(sum_ref[h * 8 : h * 8 + 1, :])
+        out_t_ref[at_h, :] = out_t_ref[at_h, :] / sum_ref[h * 8 : h * 8 + 1, :]
     out_ref[...] = low(out_t_ref[...].T)
 
 
@@ -486,6 +496,837 @@
     )(*args)
 
 
+MESH = pl.DeviceIdType.MESH
+
+
+def position_bits(count):
+    index = lax.axis_index("fsdp")
+    return [(index // (1 << b)) % 2 for b in reversed(range(count))]
+
+
+def across(bits, axis):
+    count = len(bits)
+    index = lax.axis_index("fsdp")
+    step = 1 << (count - 1 - axis)
+    return (index + step * (1 - 2 * bits[axis]), lax.axis_index("seq"))
+
+
+def along(by):
+    return (lax.axis_index("fsdp"), lax.axis_index("seq") + by)
+
+
+class Item:
+    def __init__(self, number, weight, start, size, order):
+        self.number, self.weight, self.start, self.size, self.order = number, weight, start, size, order
+
+
+def plan_items(shapes, parts, bit_count):
+    items = []
+    for w, ((rows, _), count) in enumerate(zip(shapes, parts)):
+        for p in range(count):
+            turn = p % max(bit_count - 1, 1)
+            ici = list(range(bit_count - 1))
+            order = [bit_count - 1] + ici[turn:] + ici[:turn]
+            items.append(Item(len(items), w, p * (rows // count), rows // count, order))
+    return items
+
+
+class Reducer:
+    def __init__(self, bit_count, depth, items, whole, own, landed, zin, zmid, total, out, send, recv, own_sem):
+        self.bit_count, self.depth, self.items = bit_count, depth, items
+        self.whole, self.own, self.landed = whole, own, landed
+        self.zin, self.zmid, self.total, self.out = zin, zmid, total, out
+        self.send, self.recv, self.own_sem = send, recv, own_sem
+        self.bits = position_bits(bit_count)
+        self.place = lax.axis_index("seq")
+
+    def rows(self, item):
+        return pl.ds(item.start, item.size)
+
+    def left(self, item, stage):
+        return sorted(item.order[stage:])
+
+    def pick(self, item, stage, mine):
+        axis = item.order[stage]
+        at = self.left(item, stage).index(axis)
+        bit = self.bits[axis] if mine else 1 - self.bits[axis]
+        lead = [slice(None)] * (self.bit_count - stage)
+        lead[at] = bit
+        return (*lead, self.rows(item))
+
+    def source(self, item, stage):
+        if stage == 0:
+            return self.whole[item.weight]
+        return self.own[item.weight] if stage == 1 else self.landed[stage - 1][item.weight]
+
+    def copy(self, item, stage):
+        lead = (slice(None),) * (self.bit_count - stage - 1)
+        return pltpu.make_async_remote_copy(
+            self.source(item, stage).at[self.pick(item, stage, False)],
+            self.landed[stage][item.weight].at[(*lead, self.rows(item))],
+            self.send.at[item.number, stage],
+            self.recv.at[item.number, stage],
+            device_id=across(self.bits, item.order[stage]),
+            device_id_type=MESH,
+        )
+
+    def own_copy(self, item):
+        lead = (slice(None),) * (self.bit_count - 1)
+        return pltpu.make_async_copy(
+            self.whole[item.weight].at[self.pick(item, 0, True)],
+            self.own[item.weight].at[(*lead, self.rows(item))],
+            self.own_sem.at[item.number],
+        )
+
+    def begin(self, item):
+        self.copy(item, 0).start()
+        self.own_copy(item).start()
+
+    def add(self, dst, dst_lead, other, other_lead, item):
+        group = 16
+
+        def step(i, nothing):
+            at = pl.ds(pl.multiple_of(item.start + i * group, group), group)
+            dst[(*dst_lead, at)] = low(
+                dst[(*dst_lead, at)].astype(f32) + other[(*other_lead, at)].astype(f32)
+            )
+            return nothing
+
+        lax.fori_loop(0, item.size // group, step, 0)
+
+    def advance(self, item, stage):
+        self.copy(item, stage).wait_recv()
+        landed = self.landed[stage][item.weight]
+        kept = self.bit_count - stage - 1
+        places = [[(i >> (kept - 1 - b)) & 1 for b in range(kept)] for i in range(1 << kept)]
+        if stage == 0:
+            self.own_copy(item).wait()
+            for lead in places:
+                self.add(self.own[item.weight], lead, landed, lead, item)
+        else:
+            source = self.source(item, stage)
+            axis = item.order[stage]
+            at = self.left(item, stage).index(axis)
+            for lead in places:
+                from_lead = [*lead[:at], self.bits[axis], *lead[at:]]
+                self.add(landed, lead, source, from_lead, item)
+        if stage + 1 < self.bit_count:
+            self.copy(item, stage + 1).start()
+
+    def z_copy(self, item, kind, by):
+        w, rows = item.weight, self.rows(item)
+        last = self.landed[self.bit_count - 1][w]
+        src, dst = {
+            "in": (last, self.zin[w]),
+            "mid": (last, self.zmid[w]),
+            "out": (self.total[w], self.total[w]),
+        }[kind]
+        slot = self.bit_count + {"in": 0, "mid": 1, "out": 2}[kind]
+        return pltpu.make_async_remote_copy(
+            src.at[rows],
+            dst.at[rows],
+            self.send.at[item.number, slot],
+            self.recv.at[item.number, slot],
+            device_id=along(by),
+            device_id_type=MESH,
+        )
+
+    def sides(self):
+        half = self.depth // 2
+        outermost = (self.place == 0) | (self.place == self.depth - 1)
+        middle = (self.place == half - 1) | (self.place == half)
+        inward = 1 - 2 * (self.place // half)
+        return outermost, middle, inward
+
+    def z_first(self, item):
+        outermost, middle, inward = self.sides()
+
+        @pl.when(outermost & jnp.logical_not(middle))
+        def _():
+            self.z_copy(item, "in", inward).start()
+
+    def z_second(self, item):
+        outermost, middle, inward = self.sides()
+
+        @pl.when(jnp.logical_not(outermost))
+        def _():
+            self.z_copy(item, "in", -inward).wait_recv()
+            self.add(self.landed[self.bit_count - 1][item.weight], (), self.zin[item.weight], (), item)
+
+            @pl.when(jnp.logical_not(middle))
+            def _():
+                self.z_copy(item, "in", inward).start()
+
+        @pl.when(middle)
+        def _():
+            self.z_copy(item, "mid", inward).start()
+
+    def z_third(self, item):
+        outermost, middle, inward = self.sides()
+
+        @pl.when(middle)
+        def _():
+            self.z_copy(item, "mid", inward).wait_recv()
+            group = 16
+            last, other = self.landed[self.bit_count - 1][item.weight], self.zmid[item.weight]
+
+            def step(i, nothing):
+                at = pl.ds(pl.multiple_of(item.start + i * group, group), group)
+                self.total[item.weight][at] = low(last[at].astype(f32) + other[at].astype(f32))
+                return nothing
+
+            lax.fori_loop(0, item.size // group, step, 0)
+
+            @pl.when(jnp.logical_not(outermost))
+            def _():
+                self.z_copy(item, "out", -inward).start()
+
+    def z_fourth(self, item):
+        outermost, middle, inward = self.sides()
+
+        @pl.when(jnp.logical_not(middle))
+        def _():
+            self.z_copy(item, "out", inward).wait_recv()
+
+            @pl.when(jnp.logical_not(outermost))
+            def _():
+                self.z_copy(item, "out", -inward).start()
+
+        group = 16
+
+        def step(i, nothing):
+            at = pl.ds(pl.multiple_of(item.start + i * group, group), group)
+            self.out[item.weight][at] = self.total[item.weight][at]
+            return nothing
+
+        lax.fori_loop(0, item.size // group, step, 0)
+
+    def finish(self, item):
+        outermost, middle, inward = self.sides()
+        for stage in range(self.bit_count):
+            self.copy(item, stage).wait_send()
+
+        @pl.when(jnp.logical_not(middle))
+        def _():
+            self.z_copy(item, "in", inward).wait_send()
+
+        @pl.when(middle)
+        def _():
+            self.z_copy(item, "mid", inward).wait_send()
+
+        @pl.when(jnp.logical_not(outermost))
+        def _():
+            self.z_copy(item, "out", -inward).wait_send()
+
+    def actions(self, lag, z_lag):
+        steps = []
+        for i, item in enumerate(self.items):
+            for stage in range(self.bit_count):
+                steps.append((i + lag * stage, stage, lambda item=item, s=stage: self.advance(item, s)))
+            t = i + lag * (self.bit_count - 1)
+            for n, run in enumerate((self.z_first, self.z_second, self.z_third, self.z_fourth)):
+                steps.append((t + n * z_lag, self.bit_count + n, lambda item=item, run=run: run(item)))
+        return [action for _, _, action in sorted(steps, key=lambda s: s[:2])]
+
+
+def enter(bit_count, depth):
+    bits = position_bits(bit_count)
+    place = lax.axis_index("seq")
+    barrier = pltpu.get_barrier_semaphore()
+    for axis in range(bit_count):
+        pl.semaphore_signal(barrier, inc=1, device_id=across(bits, axis), device_id_type=MESH)
+
+    @pl.when(place > 0)
+    def _():
+        pl.semaphore_signal(barrier, inc=1, device_id=along(-1), device_id_type=MESH)
+
+    @pl.when(place < depth - 1)
+    def _():
+        pl.semaphore_signal(barrier, inc=1, device_id=along(1), device_id_type=MESH)
+
+    ends = jnp.where(place == 0, 1, 0) + jnp.where(place == depth - 1, 1, 0)
+    pl.semaphore_wait(barrier, bit_count + 2 - ends)
+
+
+def small_sum(bit_count, depth, src, buf, out, send, recv):
+    bits = position_bits(bit_count)
+    place = lax.axis_index("seq")
+    half = depth // 2
+    outermost = (place == 0) | (place == depth - 1)
+    middle = (place == half - 1) | (place == half)
+    inward = 1 - 2 * (place // half)
+
+    def flip(stage):
+        return pltpu.make_async_remote_copy(
+            (src if stage == 0 else out.at[stage - 1]),
+            buf.at[stage],
+            send.at[stage],
+            recv.at[stage],
+            device_id=across(bits, bit_count - 1 - stage),
+            device_id_type=MESH,
+        )
+
+    def z_copy(kind, by):
+        n = bit_count + kind
+        return pltpu.make_async_remote_copy(
+            out.at[(bit_count - 1, bit_count, bit_count + 1)[kind]],
+            (buf.at[bit_count], buf.at[bit_count + 1], out.at[bit_count + 1])[kind],
+            send.at[n],
+            recv.at[n],
+            device_id=along(by),
+            device_id_type=MESH,
+        )
+
+    def flip_done(stage):
+        flip(stage).wait_recv()
+        mine = src[...] if stage == 0 else out[stage - 1]
+        out[stage] = mine + buf[stage]
+        if stage + 1 < bit_count:
+            flip(stage + 1).start()
+
+    def z_in():
+        @pl.when(jnp.logical_not(middle))
+        def _():
+            @pl.when(jnp.logical_not(outermost))
+            def _():
+                z_copy(0, -inward).wait_recv()
+                out[bit_count - 1] = out[bit_count - 1] + buf[bit_count]
+
+            z_copy(0, inward).start()
+
+        @pl.when(middle)
+        def _():
+            out[bit_count] = out[bit_count - 1]
+
+            @pl.when(jnp.logical_not(outermost))
+            def _():
+                z_copy(0, -inward).wait_recv()
+                out[bit_count] = out[bit_count] + buf[bit_count]
+
+            z_copy(1, inward).start()
+
+    def z_mid():
+        @pl.when(middle)
+        def _():
+            z_copy(1, inward).wait_recv()
+            out[bit_count + 1] = out[bit_count] + buf[bit_count + 1]
+
+    def z_out():
+        @pl.when(jnp.logical_not(middle))
+        def _():
+            z_copy(2, inward).wait_recv()
+
+        @pl.when(jnp.logical_not(outermost))
+        def _():
+            z_copy(2, -inward).start()
+
+    def finish():
+        for stage in range(bit_count):
+            flip(stage).wait_send()
+
+        @pl.when(jnp.logical_not(middle))
+        def _():
+            z_copy(0, inward).wait_send()
+
+        @pl.when(middle)
+        def _():
+            z_copy(1, inward).wait_send()
+
+        @pl.when(jnp.logical_not(outermost))
+        def _():
+            z_copy(2, -inward).wait_send()
+
+    begin = lambda: flip(0).start()
+    steps = [lambda s=s: flip_done(s) for s in range(bit_count)] + [z_in, z_mid, z_out]
+    return begin, steps, finish
+
+
+def bit_length(count):
+    return count.bit_length() - 1
+
+
+def reduce_all(gradients, small, parts):
+    fsdp, depth = lax.axis_size("fsdp"), lax.axis_size("seq")
+    bit_count = bit_length(fsdp)
+    shapes = [(g.shape[0] // fsdp, g.shape[1]) for g in gradients]
+    items = plan_items(shapes, parts, bit_count)
+    count = len(shapes)
+
+    def kernel(*refs):
+        at = 0
+
+        def take(n):
+            nonlocal at
+            at += n
+            return refs[at - n : at]
+
+        whole, (small_ref,) = take(count), take(1)
+        out, (small_out,) = take(count), take(1)
+        own = take(count)
+        landed = [take(count) for _ in range(bit_count)]
+        zin, zmid, total = take(count), take(count), take(count)
+        (small_buf, small_work) = take(2)
+        send, recv, own_sem, small_send, small_recv = take(5)
+        enter(bit_count, depth)
+        work = Reducer(bit_count, depth, items, whole, own, landed, zin, zmid, total, out, send, recv, own_sem)
+        begin, steps, finish = small_sum(
+            bit_count, depth, small_ref, small_buf, small_work, small_send, small_recv
+        )
+        begin()
+        for item in items:
+            work.begin(item)
+        for n, action in enumerate(work.actions(2, 3)):
+            action()
+            if n % 2 == 1 and steps:
+                steps.pop(0)()
+        for step in steps:
+            step()
+        small_out[...] = small_work[bit_count + 1]
+        for item in items:
+            work.finish(item)
+        finish()
+
+    two = (2,) * bit_count
+    stacks = [[pltpu.VMEM((*two[: bit_count - 1 - s], *shape), bf16) for shape in shapes] for s in range(bit_count)]
+    flat = [pltpu.VMEM(shape, bf16) for shape in shapes]
+    scratch = [*stacks[0], *[b for stage in stacks for b in stage], *flat, *flat, *flat]
+    scratch += [pltpu.VMEM((bit_count + 2, *small.shape), f32)] * 2
+    scratch += [
+        pltpu.SemaphoreType.DMA((len(items), bit_count + 3)),
+        pltpu.SemaphoreType.DMA((len(items), bit_count + 3)),
+        pltpu.SemaphoreType.DMA((len(items),)),
+        pltpu.SemaphoreType.DMA((bit_count + 3,)),
+        pltpu.SemaphoreType.DMA((bit_count + 3,)),
+    ]
+    return pl.pallas_call(
+        kernel,
+        out_shape=[jax.ShapeDtypeStruct(shape, bf16) for shape in shapes]
+        + [jax.ShapeDtypeStruct(small.shape, f32)],
+        in_specs=[pl.BlockSpec(memory_space=pl.ANY)] * count + [vmem],
+        out_specs=[vmem] * (count + 1),
+        scratch_shapes=scratch,
+        compiler_params=pltpu.CompilerParams(
+            collective_id=0, has_side_effects=True, vmem_limit_bytes=60 * 2**20
+        ),
+    )(*[g.reshape(*two, *shape) for g, shape in zip(gradients, shapes)], small)
+
+
+class Gatherer:
+    def __init__(self, bit_count, items, shards, whole, loads, load_sem, cast_to, own_sem, send, recv):
+        self.bit_count, self.items = bit_count, items
+        self.shards, self.whole, self.loads, self.load_sem = shards, whole, loads, load_sem
+        self.cast_to, self.own_sem, self.send, self.recv = cast_to, own_sem, send, recv
+        self.bits = position_bits(bit_count)
+        self.index = lax.axis_index("fsdp")
+        self.ready = set()
+        self.todo = []
+        self.done = set()
+
+    def block(self, axes):
+        at = self.index
+        for axis in axes:
+            at = at + (1 << (self.bit_count - 1 - axis)) * (1 - 2 * self.bits[axis])
+        return at
+
+    def subsets(self, order):
+        sets = [()]
+        for axis in order:
+            sets = sets + [(*s, axis) for s in sets]
+        return sets
+
+    def rows(self, item, axes):
+        shard_rows = self.cast_to[item.weight].shape[0]
+        return pl.ds(pl.multiple_of(self.block(axes) * shard_rows + item.start, 16), item.size)
+
+    def copy(self, item, stage, number, axes):
+        whole = self.whole[item.weight]
+        at = self.rows(item, axes)
+        src = self.cast_to[item.weight].at[pl.ds(item.start, item.size)] if not axes else whole.at[at]
+        slot = (1 << stage) - 1 + number
+        return pltpu.make_async_remote_copy(
+            src,
+            whole.at[at],
+            self.send.at[item.number, slot],
+            self.recv.at[item.number, slot],
+            device_id=across(self.bits, item.order[stage]),
+            device_id_type=MESH,
+        )
+
+    def landed(self, item, stage, number, axes):
+        whole = self.whole[item.weight]
+        at = self.rows(item, (*axes, item.order[stage]))
+        slot = (1 << stage) - 1 + number
+        return pltpu.make_async_remote_copy(
+            whole.at[at],
+            whole.at[at],
+            self.send.at[item.number, slot],
+            self.recv.at[item.number, slot],
+            device_id=across(self.bits, item.order[stage]),
+            device_id_type=MESH,
+        )
+
+    def load(self, weight):
+        return pltpu.make_async_copy(self.shards[weight], self.loads[weight], self.load_sem.at[weight])
+
+    def own(self, weight):
+        rows = self.cast_to[weight].shape[0]
+        return pltpu.make_async_copy(
+            self.cast_to[weight],
+            self.whole[weight].at[pl.ds(pl.multiple_of(self.index * rows, 16), rows)],
+            self.own_sem.at[weight],
+        )
+
+    def begin(self, item):
+        w = item.weight
+        if w not in self.ready:
+            self.ready.add(w)
+            self.load(w).wait()
+            group = 16
+
+            def step(i, nothing):
+                at = pl.ds(pl.multiple_of(i * group, group), group)
+                self.cast_to[w][at] = low(self.loads[w][at])
+                return nothing
+
+            lax.fori_loop(0, self.cast_to[w].shape[0] // group, step, 0)
+            self.own(w).start()
+        for stage in range(self.bit_count):
+            self.copy(item, stage, 0, ()).start()
+
+    def advance(self, item, stage):
+        before = self.subsets(item.order[:stage])
+        for number, axes in enumerate(before):
+            self.landed(item, stage, number, axes).wait_recv()
+        for later in range(stage + 1, self.bit_count):
+            sets = self.subsets(item.order[:later])
+            for number, axes in enumerate(before):
+                mine = (*axes, item.order[stage])
+                self.copy(item, later, sets.index(mine), mine).start()
+        if stage == self.bit_count - 1:
+            self.done.add(item.number)
+
+    def plan(self, lag):
+        steps = []
+        for i, item in enumerate(self.items):
+            steps.append((i, 0, lambda item=item: self.begin(item)))
+            for stage in range(self.bit_count):
+                steps.append((i + lag * (stage + 1), stage + 1, lambda item=item, s=stage: self.advance(item, s)))
+        self.todo = [action for _, _, action in sorted(steps, key=lambda s: s[:2])]
+
+    def pump(self, count):
+        for _ in range(min(count, len(self.todo))):
+            self.todo.pop(0)()
+
+    def until(self, weight):
+        numbers = {item.number for item in self.items if item.weight == weight}
+        while not numbers <= self.done:
+            self.todo.pop(0)()
+        self.own(weight).wait()
+
+    def finish(self):
+        for item in self.items:
+            for stage in range(self.bit_count):
+                for number, axes in enumerate(self.subsets(item.order[:stage])):
+                    self.copy(item, stage, number, axes).wait_send()
+
+
+def multiply(out_ref, out_rows, left, right_ref, first, width, tile):
+    def step(j, nothing):
+        at = pl.ds(pl.multiple_of(j * tile, tile), tile)
+        from_at = pl.ds(pl.multiple_of(first + j * tile, 128), tile)
+        out_ref[out_rows, at] = dot_nn(left[...], right_ref[:, from_at])
+        return nothing
+
+    lax.fori_loop(0, width // tile, step, 0)
+
+
+def forward_part(tokens, seg_rows, norm_gain, cosine, signed, bias_row, rate_row, conv_weight,
+                 conv_bias, mixer_gain, skip_row, shards, parts):
+    fsdp, depth = lax.axis_size("fsdp"), lax.axis_size("seq")
+    bit_count = bit_length(fsdp)
+    shapes = [s.shape for s in shards]
+    items = plan_items(shapes, parts, bit_count)
+    count = tokens.shape[0]
+    weights = len(shards)
+    pieces = 2
+    kept_shape = (count // SUB, NS, DI)
+    results = dict(
+        normed=((count, 1024), bf16),
+        conv=((count + EDGE, CW), f32),
+        raw=((count, 128), f32),
+        z=((count, DI), f32),
+        act=((count, CW), bf16),
+        dt=((count, 128), f32),
+        cum=((count, 128), f32),
+        passing=((1, DI), f32),
+        query=((count, 512), bf16),
+        kv=((depth * count, 256), bf16),
+        attended=((count, 512), bf16),
+        attended_t=((512, count), f32),
+        log_total=((QUERY_HEADS, count), f32),
+        y=((count, DI), f32),
+        gated=((count, DI), bf16),
+        kept=(kept_shape, bf16),
+        seg_wide=((count + 2 * EDGE, 128), f32),
+        seg_col=((depth * count, 128), f32),
+    )
+    names = list(results)
+    local = dict(
+        normed_edge=((16, 1024), bf16),
+        edge=((16, 1024), bf16),
+        seg_all=((depth * 8, count), f32),
+        qkv=((count, 768), f32),
+        end=((NS, DI), f32),
+        state=((NS, DI), f32),
+        carry=((NS, DI), f32),
+        state_send=((NS, DI), bf16),
+        state_recv=((NS, DI), bf16),
+        bias=((count, count), f32),
+        keys=((4, count, 128), bf16),
+        values_t=((128, count), bf16),
+        top=((QUERY_HEADS * 8, count), f32),
+        total=((QUERY_HEADS * 8, count), f32),
+    )
+    in_vmem = (0, 1)
+
+    def kernel(*refs):
+        at = 0
+
+        def take(n):
+            nonlocal at
+            at += n
+            return refs[at - n : at]
+
+        (tokens_ref, segrow_ref, gain_ref, cos_ref, sin_ref, bias_ref, rate_ref, weight_ref, cbias_ref,
+         mixer_gain_ref, skip_ref) = take(11)
+        shard_refs = take(weights)
+        out = dict(zip(names, take(len(names))))
+        whole_out = take(weights)
+        v = dict(zip(names, take(len(names))))
+        v.update(zip(local, take(len(local))))
+        loads, cast_to = take(weights), take(weights)
+        whole_vmem = take(len(in_vmem))
+        send, recv, load_sem, own_sem, save_sem, z_send, z_recv = take(7)
+        place = lax.axis_index("seq")
+        whole = [whole_vmem[in_vmem.index(w)] if w in in_vmem else whole_out[w] for w in range(weights)]
+        gather = Gatherer(bit_count, items, shard_refs, whole, loads, load_sem, cast_to, own_sem, send, recv)
+        for w in range(weights):
+            gather.load(w).start()
+        enter(bit_count, depth)
+        gather.plan(2)
+        saved = []
+
+        def save(src, dst):
+            copy = pltpu.make_async_copy(src, dst, save_sem.at[len(saved)])
+            copy.start()
+            saved.append(copy)
+
+        def keep(*which):
+            for name in which:
+                save(v[name], out[name])
+
+        def to_next(src, dst, slot):
+            return pltpu.make_async_remote_copy(
+                src, dst, z_send.at[slot], z_recv.at[slot], device_id=along(1), device_id_type=MESH
+            )
+
+        started = []
+
+        def send_on(condition, src, dst, slot):
+            @pl.when(condition)
+            def _():
+                to_next(src, dst, slot).start()
+
+            started.append((condition, src, dst, slot))
+
+        def ring(ref, rows, hop, slot):
+            b = place - hop + 1
+            part = ref.at[pl.ds(pl.multiple_of(jnp.maximum(b, 0) * rows, 8), rows)]
+            send_on((b >= 0) & (place < depth - 1), part, part, slot)
+
+        def ring_wait(ref, rows, hop, slot):
+            b = place - hop
+            part = ref.at[pl.ds(pl.multiple_of(jnp.maximum(b, 0) * rows, 8), rows)]
+
+            @pl.when(b >= 0)
+            def _():
+                to_next(part, part, slot).wait_recv()
+
+        tail = tokens_ref.at[pl.ds(count - 16, 16)]
+        gather.pump(2)
+        send_on(place < depth - 1, tail, v["edge"], 0)
+        v["seg_all"][pl.ds(pl.multiple_of(place * 8, 8), 8)] = jnp.broadcast_to(segrow_ref[...], (8, count))
+        ring(v["seg_all"], 8, 1, 1)
+
+        def normalise(src, dst, rows, group):
+            def step(i, nothing):
+                at = pl.ds(pl.multiple_of(i * group, group), group)
+                x = src[at].astype(f32)
+                scale = lax.rsqrt(jnp.mean(x * x, axis=1, keepdims=True) + epsilon)
+                dst[at] = low(x * scale * gain_ref[...])
+                return nothing
+
+            lax.fori_loop(0, rows // group, step, 0)
+
+        normalise(tokens_ref, v["normed"], count, 64)
+        gather.pump(1)
+
+        @pl.when(place == 0)
+        def _():
+            v["edge"][...] = jnp.zeros((16, 1024), bf16)
+
+        @pl.when(place > 0)
+        def _():
+            to_next(tail, v["edge"], 0).wait_recv()
+
+        normalise(v["edge"], v["normed_edge"], 16, 16)
+        gather.pump(1)
+        for hop in range(1, depth):
+            ring_wait(v["seg_all"], 8, hop, hop)
+            if hop < depth - 1:
+                ring(v["seg_all"], 8, hop + 1, hop + 1)
+
+        def column(row):
+            return jnp.broadcast_to(row, (128, count)).T
+
+        for b in range(depth):
+
+            @pl.when(b <= place)
+            def _(b=b):
+                v["seg_col"][b * count : (b + 1) * count, :] = column(v["seg_all"][b * 8 : b * 8 + 1, :])
+
+            @pl.when(b > place)
+            def _(b=b):
+                v["seg_col"][b * count : (b + 1) * count, :] = jnp.full((count, 128), -2.0, f32)
+
+        own_rows = pl.ds(pl.multiple_of(place * count, 8), count)
+        v["seg_wide"][EDGE : EDGE + count, :] = v["seg_col"][own_rows, :]
+        v["seg_wide"][EDGE + count :, :] = jnp.full((EDGE, 128), -2.0, f32)
+        before = pl.ds(pl.multiple_of(jnp.maximum(place * count - EDGE, 0), 8), EDGE)
+        v["seg_wide"][0:EDGE, :] = jnp.where(place == 0, -1.0, v["seg_col"][before, :])
+        v["raw"][...] = jnp.zeros((count, 128), f32)
+        gather.until(0)
+        save(whole[0], whole_out[0])
+        multiply(v["conv"], pl.ds(EDGE, count), v["normed"], whole[0], DI, CW, 256)
+        v["conv"][0:EDGE, :] = dot_nn(v["normed_edge"][...], whole[0][:, DI : DI + CW])[EDGE:]
+        v["raw"][:, 0:MH] = dot_nn(v["normed"][...], whole[0][:, DI + CW : DI + CW + MH])
+        gather.pump(4)
+        front_conv(v["conv"], v["seg_wide"], weight_ref, cbias_ref, v["act"])
+        gather.pump(4)
+        front_state(v["seg_wide"], v["raw"], bias_ref, rate_ref, v["act"], v["dt"], v["cum"], v["end"], v["passing"])
+        keep("normed", "conv", "raw", "act", "dt", "cum", "passing", "seg_wide", "seg_col")
+        width = DI // pieces
+        state_slot, kv_slot = depth, depth + pieces
+
+        def chain(j):
+            for p in range(pieces):
+                cols = pl.ds(p * width, width)
+
+                @pl.when(place == j)
+                def _():
+                    if j == 0:
+                        v["state"][:, cols] = jnp.zeros((NS, width), f32)
+                    else:
+                        to_next(
+                            v["state_send"].at[:, cols], v["state_recv"].at[:, cols], state_slot + p
+                        ).wait_recv()
+                        v["state"][:, cols] = v["state_recv"][:, cols].astype(f32)
+                    if j < depth - 1:
+                        v["state_send"][:, cols] = low(
+                            v["passing"][:, cols] * v["state"][:, cols] + v["end"][:, cols]
+                        )
+                        to_next(
+                            v["state_send"].at[:, cols], v["state_recv"].at[:, cols], state_slot + p
+                        ).start()
+
+        chain(0)
+        gather.until(1)
+        save(whole[1], whole_out[1])
+        multiply(v["qkv"], slice(None), v["normed"], whole[1], 0, 768, 256)
+        rotate_kernel(v["qkv"], cos_ref, sin_ref, v["query"], v["kv"].at[own_rows])
+        ring(v["kv"], count, 1, kv_slot + 1)
+        keep("query")
+        gather.pump(4)
+        multiply(v["z"], slice(None), v["normed"], whole[0], 0, DI, 256)
+        keep("z")
+        gather.pump(4)
+        chain(1)
+        attend_start(v["top"], v["total"], v["attended_t"])
+
+        def attend(b):
+            attend_block(b, place, v["query"], v["kv"], v["seg_col"], segrow_ref, v["attended_t"], v["bias"],
+                         v["keys"], v["values_t"], v["top"], v["total"])
+
+        attend(place)
+        gather.pump(4)
+        for hop in range(1, depth):
+            ring_wait(v["kv"], count, hop, kv_slot + hop)
+            if hop < depth - 1:
+                ring(v["kv"], count, hop + 1, kv_slot + hop + 1)
+
+            @pl.when(place >= hop)
+            def _(hop=hop):
+                attend(place - hop)
+
+            gather.pump(4)
+            if hop < depth - 1:
+                chain(hop + 1)
+
+        attend_finish(v["attended"], v["attended_t"], v["log_total"], v["top"], v["total"])
+        keep("attended", "attended_t", "log_total", "kv")
+        for first in range(0, count // SUB, 2):
+            gather.pump(4)
+            mid_kernel(v["act"], v["dt"], v["cum"], v["seg_wide"], segrow_ref, v["state"], v["z"], mixer_gain_ref,
+                       skip_ref, v["y"], v["gated"], v["kept"], v["carry"], first, first + 2)
+        keep("y", "gated", "kept")
+        for w in range(2, weights):
+            gather.until(w)
+        gather.finish()
+        for condition, src, dst, slot in started:
+
+            @pl.when(condition)
+            def _(src=src, dst=dst, slot=slot):
+                to_next(src, dst, slot).wait_send()
+
+        @pl.when(place < depth - 1)
+        def _():
+            for p in range(pieces):
+                cols = pl.ds(p * width, width)
+                to_next(v["state_send"].at[:, cols], v["state_recv"].at[:, cols], state_slot + p).wait_send()
+
+        for copy in saved:
+            copy.wait()
+
+    wholes = [((fsdp * rows, cols), bf16) for rows, cols in shapes]
+    scratch = [pltpu.VMEM(*results[n]) for n in names] + [pltpu.VMEM(*a) for a in local.values()]
+    scratch += [pltpu.VMEM(shape, f32) for shape in shapes] + [pltpu.VMEM(shape, bf16) for shape in shapes]
+    scratch += [pltpu.VMEM(*wholes[w]) for w in in_vmem]
+    slots = (1 << bit_count) - 1
+    z_slots = depth + pieces + depth
+    scratch += [
+        pltpu.SemaphoreType.DMA((len(items), slots)),
+        pltpu.SemaphoreType.DMA((len(items), slots)),
+        pltpu.SemaphoreType.DMA((weights,)),
+        pltpu.SemaphoreType.DMA((weights,)),
+        pltpu.SemaphoreType.DMA((len(names) + 2,)),
+        pltpu.SemaphoreType.DMA((z_slots,)),
+        pltpu.SemaphoreType.DMA((z_slots,)),
+    ]
+    hbm = pl.BlockSpec(memory_space=pl.ANY)
+    made = pl.pallas_call(
+        kernel,
+        out_shape=[jax.ShapeDtypeStruct(*a) for a in list(results.values()) + wholes],
+        in_specs=[vmem] * 11 + [hbm] * weights,
+        out_specs=[hbm] * (len(names) + weights),
+        scratch_shapes=scratch,
+        compiler_params=pltpu.CompilerParams(
+            collective_id=1, has_side_effects=True, vmem_limit_bytes=62 * 2**20
+        ),
+    )(tokens, seg_rows, norm_gain, cosine, signed, bias_row, rate_row, conv_weight, conv_bias, mixer_gain,
+      skip_row, *shards)
+    return dict(zip(names, made)), made[len(names) :]
+
+
 def shifted(array, axis, by):
     devices = lax.axis_size(axis)
     pairs = [(i, i + by) for i in range(devices) if 0 <= i + by < devices]
@@ -502,13 +1343,8 @@
     )
 
 
-def gathered(shard):
-    return lax.all_gather(low(shard), "fsdp", axis=0, tiled=True)
-
-
 def reduced(gradient):
-    piece = lax.psum_scatter(low(gradient), "fsdp", scatter_dimension=0, tiled=True)
-    return piece
+    return low(gradient)
 
 
 def padded(vector):
@@ -536,22 +1372,6 @@
 ):
     place, devices = lax.axis_index("seq"), lax.axis_size("seq")
     count = tokens.shape[1]
-    seg_all = lax.all_gather(segment_ids[0], "seq", axis=0, tiled=True).astype(f32)
-    edge_tokens = shifted(tokens[0, count - EDGE :], "seq", 1)
-    qkv_full = gathered(qkv_proj)
-    in_full = gathered(in_proj)
-    mix_full = gathered(mixer_out)
-    attn_full = gathered(attn_proj)
-    gate_full = gathered(gate_up)
-    down_full = gathered(down_proj)
-
-    seg_padded = jnp.pad(seg_all, (EDGE, EDGE), constant_values=-1.0)
-    seg_ext = lax.dynamic_slice_in_dim(seg_padded, place * count, count + 2 * EDGE, 0)
-    seg_wide = jnp.broadcast_to(seg_ext[:, None], (count + 2 * EDGE, 128))
-    seg_row = segment_ids.astype(f32)
-    seg_col = jnp.broadcast_to(seg_all[:, None], (seg_all.shape[0], 128))
-    own = place.astype(jnp.int32)[None]
-
     position = place * count + jnp.arange(count, dtype=jnp.int32)
     half = HEAD_WIDTH // 2
     lane = jnp.arange(128, dtype=jnp.int32)
@@ -560,66 +1380,25 @@
     angles = position.astype(f32)[:, None] * frequencies[None, :]
     cosine = jnp.cos(angles)
     signed = jnp.sin(angles) * jnp.where(lane % HEAD_WIDTH < half, -1.0, 1.0)[None]
-
+    seg_row = segment_ids.astype(f32)
+    bias_row, rate_row = padded(step_bias), padded(decay_log)
+    skip_row = jnp.repeat(skip_gain, MP)[None]
+    own = place.astype(jnp.int32)[None]
+    v, (in_full, qkv_full, mix_full, attn_full, gate_full, down_full) = forward_part(
+        tokens[0], seg_row, norm_gain[None], cosine, signed, bias_row, rate_row, conv_weight, conv_bias[None],
+        mixer_gain[None], skip_row, (in_proj, qkv_proj, mixer_out, attn_proj, gate_up, down_proj),
+        (4, 2, 2, 2, 4, 4),
+    )
+    normed, attended, gated, mixer_y, act, dt, cum = (
+        v[n] for n in ("normed", "attended", "gated", "y", "act", "dt", "cum")
+    )
+    gate_z, seg_wide, seg_col, kept, kv_all, query = (
+        v[n] for n in ("z", "seg_wide", "seg_col", "kept", "kv", "query")
+    )
+    attended_t, log_total, conv_ext, step_raw = (v[n] for n in ("attended_t", "log_total", "conv", "raw"))
+    length = kv_all.shape[0]
     token_rows = tokens[0].astype(f32)
-    normed32, norm_pull = jax.vjp(rms_scale, token_rows, norm_gain)
-    normed = low(normed32)
-    normed_edge = low(rms_scale(edge_tokens.astype(f32), norm_gain))
-    normed_ext = jnp.concatenate([normed_edge, normed], axis=0)
-
-    qkv = dot_nn(normed, qkv_full)
-    query, kv = call(
-        rotate_kernel,
-        [((count, 512), bf16), ((count, 256), bf16)],
-        (qkv, cosine, signed),
-    )
-    kv_all = lax.all_gather(kv, "seq", axis=0, tiled=True)
-    length = kv_all.shape[0]
-
-    step_weights = jnp.pad(in_full[:, DI + CW :], ((0, 0), (0, 128 - MH)))
-    conv_ext = dot_nn(normed_ext, in_full[:, DI : DI + CW])
-    step_raw = dot_nn(normed, step_weights)
-    gate_z = dot_nn(normed, in_full[:, :DI])
-    bias_row, rate_row = padded(step_bias), padded(decay_log)
-    act, dt, cum, end_state, passing = call(
-        front_kernel,
-        [
-            ((count, CW), bf16),
-            ((count, 128), f32),
-            ((count, 128), f32),
-            ((NS, DI), f32),
-            ((1, DI), f32),
-        ],
-        (conv_ext, seg_wide, step_raw, bias_row, rate_row, conv_weight, conv_bias[None]),
-    )
-    pass_top, pass_rest = split(passing)
-    states = lax.all_gather(
-        jnp.concatenate([low(end_state), pass_top, pass_rest, jnp.zeros((14, DI), bf16)], 0), "seq"
-    ).astype(f32)
-    passings = states[:, NS : NS + 1] + states[:, NS + 1 : NS + 2]
-    state_in = jnp.zeros((NS, DI), f32)
-    for k in range(devices):
-        state_in = jnp.where(k < place, passings[k] * state_in + states[k, :NS], state_in)
-
-    attended, attended_t, log_total = call(
-        attend_kernel,
-        [((count, 512), bf16), ((512, count), f32), ((QUERY_HEADS, count), f32)],
-        (own, query, kv_all, seg_col, seg_row),
-        (
-            ((count, count), f32),
-            ((4, count, 128), bf16),
-            ((QUERY_HEADS, count), f32),
-            ((QUERY_HEADS, count), f32),
-        ),
-        smem,
-    )
-    skip_row = jnp.repeat(skip_gain, MP)[None]
-    mixer_y, gated, kept = call(
-        mid_kernel,
-        [((count, DI), f32), ((count, DI), bf16), ((count // SUB, NS, DI), bf16)],
-        (act, dt, cum, seg_wide, seg_row, state_in, gate_z, mixer_gain[None], skip_row),
-        (((NS, DI), f32),),
-    )
+    _, norm_pull = jax.vjp(rms_scale, token_rows, norm_gain)
     hidden = token_rows + (dot_nn(attended, attn_full) + dot_nn(gated, mix_full))
     ffn_in32, ffn_pull = jax.vjp(rms_scale, hidden, ffn_gain)
     ffn_in = low(ffn_in32)
@@ -650,6 +1429,7 @@
         (gated_grad, mixer_y, act, gate_z, dt, cum, seg_wide, mixer_gain[None], skip_row),
     )
     grads = lax.all_gather(low(state_grad), "seq").astype(f32)
+    passings = lax.all_gather(v["passing"], "seq")
     later = jnp.zeros((NS, DI), f32)
     for k in reversed(range(devices)):
         later = jnp.where(k > place, passings[k] * later + grads[k], later)
@@ -708,20 +1488,26 @@
     rows_extra, norm_gain_grad = norm_pull(normed_grad)
     input_grad = hidden_grad + rows_extra
     pieces = (in_piece, mixer_piece, qkv_piece, attn_piece, gate_piece, down_piece)
-    shards = [lax.psum(piece, "seq").astype(f32) for piece in pieces]
-    small = lax.psum(
-        (
-            norm_gain_grad,
-            ffn_gain_grad,
-            mixer_gain_grad[0],
-            conv_weight_grad,
-            conv_bias_grad[0],
-            rate_grad[0, :MH],
-            bias_grad[0, :MH],
-            skip_grad[0, :MH],
-        ),
-        ("fsdp", "seq"),
+    rows = (
+        norm_gain_grad,
+        ffn_gain_grad,
+        mixer_gain_grad,
+        conv_weight_grad,
+        conv_bias_grad,
+        rate_grad,
+        bias_grad,
+        skip_grad,
     )
+    flat = jnp.concatenate([row.reshape(-1) for row in rows])
+    flat = jnp.pad(flat, (0, 16384 - flat.shape[0])).reshape(16, 1024)
+    *shards, flat = reduce_all(pieces, flat, (4, 2, 2, 2, 4, 4))
+    shards = [shard.astype(f32) for shard in shards]
+    flat, small, at = flat.reshape(-1), [], 0
+    for row, keep in zip(rows, (None, None, None, None, None, MH, MH, MH)):
+        part = flat[at : at + row.size].reshape(row.shape)
+        at += row.size
+        part = part[:, :keep] if keep else part
+        small.append(part if part.shape[0] == KC else part.reshape(-1))
     return (low(result)[None], input_grad[None], *small, *shards)
 
 

time: 931 us -> 627 us (0.67)
  waiting for transfers between devices: 564 us -> 2.69 us
  Pallas kernels: 86.6 us -> 420 us
  matrix products: 119 us -> 80.9 us
  blocking collectives: 57.1 us -> 30.5 us
  other arithmetic: 43.6 us -> 29.8 us
    pallas_call x0 -> x2, Pallas kernels: none -> 368 us  [the longest x1 217 us: forward_part(): pl.pallas_call(kernel, out_shape=[jax.ShapeDtypeStruct(*a) for a in list(...]
    reduce_scatter x5 -> x0, waiting for transfers between devices: 258 us -> none  [reduced(): lax.psum_scatter(low(gradient), 'fsdp', scatter_dimension=0, tiled=True)]
    all_gather x8 -> x0, waiting for transfers between devices: 198 us -> none  [the longest x6 170 us: gathered(): return lax.all_gather(low(shard), 'fsdp', axis=0, tiled=True)]
    psum x1 -> x0, waiting for transfers between devices: 54.9 us -> none  [on_device(): shards = [lax.psum(piece, 'seq').astype(f32) for piece in pieces]]
    psum x1 -> x0, blocking collectives: 45 us -> none  [on_device(): lax.psum((norm_gain_grad, ffn_gain_grad, mixer_gain_grad[0], conv_weight_...]
    pallas_call x7 -> x3, Pallas kernels: 86.6 us -> 52.2 us  [call(): pl.pallas_call(kernel, out_shape=[jax.ShapeDtypeStruct(shape, kind) for s...]
    unnamed x18 -> x2, waiting for transfers between devices: 25.7 us -> 0.03 us
    dot_general x8 -> x4, matrix products: 40.9 us -> 16 us  [dot_nn(): return jnp.dot(left, right, preferred_element_type=jnp.float32)]
  transfers between devices with their start and end apart: 19 -> 3, of which waited for: 17 -> 1; matrix products, arithmetic and copies ran while one was open for 16% -> 8% of each run, Pallas kernels for 8% -> 2%
where the time goes in v2:
time: 627 us; the launch traced here: 618 us
  Pallas kernels  420 us (67%)
  matrix products  80.9 us (13%)
  local copies, waits for them, and re-layouts  37.7 us (6%)
  blocking collectives  30.5 us (5%)
  other arithmetic  29.8 us (5%)
  between operations  14.9 us (2%)
    pallas_call x1, Pallas kernels, forward_part(): pl.pallas_call(kernel, out_shape=[jax.ShapeDtypeStruct(*a) for a in list(...  217 us
    pallas_call x1, Pallas kernels, reduce_all(): pl.pallas_call(kernel, out_shape=[jax.ShapeDtypeStruct(shape, bf16) for s...  151 us
    pallas_call x3, Pallas kernels, call(): pl.pallas_call(kernel, out_shape=[jax.ShapeDtypeStruct(shape, kind) for s...  52.2 us
    dot_general x6, matrix products, dot_nt(): lax.dot_general(left, right, (((1,), (1,)), ((), ())), preferred_element_...  34 us
    dot_general x6, matrix products, dot_tn(): lax.dot_general(left, right, (((0,), (0,)), ((), ())), preferred_element_...  30.9 us
    all_gather x1, blocking collectives, on_device(): passings = lax.all_gather(v['passing'], 'seq')  30.5 us
    dot_general x4, matrix products, dot_nn(): return jnp.dot(left, right, preferred_element_type=jnp.float32)  16 us
  transfers between devices with their start and end apart: 3, of which 1 were waited for; matrix products, arithmetic and copies ran while one was open for 8% of the time, Pallas kernels for 2%

profile of v2, /device:TPU:0, one launch (start us, length us, event | category | flops | bytes accessed | tf_op | source)
XLA Modules:
  0.0 617.9 jit_solution(1561003945664368168)
XLA Ops:
  7.3 0.7 broadcast_in_dim.62
  8.0 0.7 broadcast_in_dim_reshape.3.refs_10_.skip_ref
  8.7 1.3 convert_element_type.103.refs_1_.segrow_ref
  9.9 1.3 broadcast_in_dim.60.refs_8_.cbias_ref
  11.2 1.3 broadcast_in_dim.61.refs_9_.gain_ref
  12.5 2.7 copy.43.refs_11_
  15.8 1.8 fusion.22
  17.6 216.9 %shard_map.288 = (bf16[512,1024]{1,0:T(8,128)(2,1)}, f32[520,1792]{1,0:T(8,128)}, f32[512,128]{1,0:T(8,128)}, f32[512,1536]{1,0:T(8,128)}, bf16[512,1792]{1,0:T(...) custom-call(bf16[512,1024]{1,0:T(8,128)(2,1)} %bitcast.87, ...), custom_call_target="tpu_custom_call" | custom-call | tf_op jit(solution)/shard_map/pallas_call | solution.py:1316
  234.5 4.3 fusion.39
  238.9 0.9 multiply_reduce_fusion.2
  240.1 4.7 fusion.36
  244.8 6.4 %bitcast_multiply_fusion.1 = (f32[512,2048]{1,0:T(8,128)}, f32[512,2048]{1,0:T(8,128)}, bf16[512,2048]{1,0:T(8,128)(2,1)}) fusion(f32[512,4096]{1,0:T(8,128)S(1)} %fusion.36, bf16[2048,1024]{1,0:T(8,128)(2,1)S(1)} %copy-done.33, bf16[1,512,1024]{2,1,0:T(8,128)(2,1)S(1)} %copy-done.2), kind=kOutput, calls=%fused_computation.7 | convolution fusion | flops 2162163712 | bytes 24117248 | tf_op jit(solution)/shard_map/dot_general | solution.py:33
  251.2 10.6 %multiply_reduce_fusion = (f32[1024]{0:T(1024)}, f32[512]{0:T(512)S(1)}, f32[512,1024]{1,0:T(8,128)S(1)}) fusion(f32[512,1024]{1,0:T(8,128)S(1)} %get-tuple-element.171, f32[512]{0:T(512)S(1)} %fusion.24, f32[1024]{0:T(1024)S(1)} %copy-done.23, bf16[1024,4096]{1,0:T(8,128)(2,1)} %get-tuple-element.64, f32[512,2048]{1,0:T(8,128)} %get-tuple-element.161, ...), kind=kOutput, calls=%fused_computation.30 | convolution fusion | flops 4302305792 | bytes 20983808 | tf_op jit(solution)/shard_map/dot_general | solution.py:33
  261.8 1.3 copy-done.1
  263.8 1.5 convolution_convert_fusion.7.grad_ref
  265.3 10.8 %shard_map.289 = (bf16[512,512]{1,0:T(8,128)(2,1)}, bf16[2048,256]{1,0:T(8,128)(2,1)}) custom-call(s32[1]{0:T(128)} %bitcast.7.own_ref, bf16[512,512]{1,0:T(8,128)(2,1)} %get-tuple-element.66.query_ref, bf16[2048,256]{1,0:T(8,128)(2,1)} %get-tuple-element.67.kv_ref, f32[2048,128]{1,0:T(8,128)} %get-tuple-element.68.segcol_ref, ...), custom_call_target="tpu_custom_call" | custom-call | flops 1000000000 | bytes 10000000 | tf_op jit(solution)/shard_map/pallas_call | solution.py:488
  276.2 5.2 convolution_convert_fusion.4.grad_ref
  281.4 11.8 %shard_map.290 = (f32[512,1536]{1,0:T(8,128)}, bf16[512,1536]{1,0:T(8,128)(2,1)}, f32[1,1536]{1,0:T(1,128)}, f32[128,1536]{1,0:T(8,128)}) custom-call(bf16[512,1536]{1,0:T(8,128)(2,1)} %convolution_convert_fusion.4.grad_ref, f32[512,1536]{1,0:T(8,128)} %get-tuple-element.74.y_ref, bf16[512,1792]{1,0:T(8,128)(2,1)} %get-tuple-element.75.act_ref, ...), custom_call_target="tpu_custom_call" | custom-call | flops 1000000000 | bytes 10000000 | tf_op jit(solution)/shard_map/pallas_call | solution.py:488
  293.3 1.9 convert_element_type.115
  295.5 3.3 convolution_convert_fusion.6
  298.8 3.5 convolution_convert_fusion.3
  302.3 30.5 %all-gather.2 = f32[4,1,1536]{2,1,0:T(1,128)S(1)} all-gather(f32[1,1,1536]{2,1,0:T(1,128)S(1)} %bitcast.101), channel_id=2, replica_groups=mesh['fsdp'=8,'seq'=4] {'seq'}, dimensions={0}, use_global_device_ids=true | all-gather | bytes 30720 | tf_op jit(solution)/shard_map/all_gather | solution.py:1432
  332.8 0.6 fusion.25
  333.4 6.2 fusion.10
  339.6 0.6 reduce.4
  340.2 0.7 slice_reduce_fusion.2
  340.9 6.4 %convolution_convert_fusion.2 = bf16[2048,1024]{1,0:T(8,128)(2,1)} fusion(bf16[512,2048]{1,0:T(8,128)(2,1)} %get-tuple-element.162, bf16[1,512,1024]{2,1,0:T(8,128)(2,1)} %param.18), kind=kOutput, calls=%fused_computation.16 | convolution fusion | flops 2149580800 | bytes 7340032 | tf_op jit(solution)/shard_map/dot_general | solution.py:39
  347.3 9.4 %convolution_convert_fusion = bf16[1024,4096]{1,0:T(8,128)(2,1)} fusion(f32[512,2048]{1,0:T(8,128)} %get-tuple-element.161, f32[512,2048]{1,0:T(8,128)S(1)} %copy-done.43, f32[512,1024]{1,0:T(8,128)S(1)} %get-tuple-element.171, f32[1024]{0:T(1024)S(1)} %copy-done.23, f32[512]{0:T(512)S(1)} %fusion.24), kind=kOutput, calls=%fused_computation.1 | convolution fusion | flops 4304928768 | bytes 18880512 | tf_op jit(solution)/shard_map/dot_general | solution.py:39
  356.8 1.8 convert_multiply_fusion.4
  358.6 0.8 copy.45
  359.4 1.7 rev.3
  361.1 1.1 copy.46
  362.2 0.9 slice.133
  363.1 1.9 fusion.21
  365.0 3.9 fusion.19
  369.0 1.8 convert_element_type.130
  370.8 1.2 fusion.14.later_ref
  372.1 29.6 %shard_map.291 = (f32[512,128]{1,0:T(8,128)}, f32[520,1792]{1,0:T(8,128)}, f32[4,1792]{1,0:T(4,128)}, f32[1,1792]{1,0:T(1,128)}, f32[1,128]{1,0:T(1,128)}, /*index=5*/f32[1,128]{1,0:T(1,128)}, f32[1,128]{1,0:T(1,128)}) custom-call(bf16[512,1792]{1,0:T(8,128)(2,1)} %get-tuple-element.75.act_ref, f32[512,128]{1,0:T(8,128)} %get-tuple-element.77.dt_ref, ...), custom_call_target="tpu_custom_call" | custom-call | flops 1000000000 | bytes 10000000 | tf_op jit(solution)/shard_map/pallas_call | solution.py:488
  401.6 1.4 slice.103
  403.1 1.3 collective-permute-start
  404.4 2.2 convolution_convert_fusion.5
  406.7 2.6 collective-permute-done
  409.4 2.4 add_convert_fusion.1
  411.8 6.1 convolution_convert_fusion.1
  418.0 6.3 %fusion.9 = (f32[1024]{0:T(1024)S(1)}, f32[512]{0:T(512)}, f32[512,1024]{1,0:T(8,128)}) fusion(f32[512]{0:T(512)S(1)} %copy-done.24, bf16[1,512,1024]{2,1,0:T(8,128)(2,1)S(1)} %copy-done, f32[1024]{0:T(1024)S(1)} %copy-done.22, f32[512,1024]{1,0:T(8,128)S(1)} %copy-done.42, bf16[1024,3352]{1,0:T(8,128)(2,1)S(1)} %bitcast.105, ...), kind=kOutput, calls=%fused_computation.29 | convolution fusion | flops 3529316864 | bytes 15552512 | tf_op jit(solution)/shard_map/dot_general | solution.py:33
  424.4 0.6 reshape.192.refs_6_
  425.1 9.9 %copy.47 = bf16[1024,3352]{1,0:T(8,128)(2,1)} copy(bf16[1024,3352]{0,1:T(8,128)(2,1)} %convolution_convert_fusion.1) | data formatting | bytes 13729792 | tf_op jit(solution)/shard_map/convert_element_type | solution.py:49
  435.0 150.7 %shard_map.292 = (bf16[128,3352]{1,0:T(8,128)(2,1)}, bf16[192,1024]{1,0:T(8,128)(2,1)}, bf16[128,768]{1,0:T(8,128)(2,1)}, bf16[64,1024]{1,0:T(8,128)(2,1)}, bf16...) custom-call(bf16[2,2,2,128,3352]{4,3,2,1,0:T(8,128)(2,1)} %bitcast.86, ...), custom_call_target="tpu_custom_call" | custom-call | tf_op jit(solution)/shard_map/pallas_call | solution.py:901
  585.8 0.9 copy.50
  586.6 0.6 slice.144
  587.9 0.6 slice.145
  589.0 1.4 fusion.38
  590.5 2.8 convert_element_type.128
  593.2 2.5 copy.48
  595.7 2.2 convert_element_type.129
  597.9 1.0 convert_element_type.125
  598.8 0.8 convert_element_type.126
  599.6 0.7 convert_element_type.127
  600.3 1.4 reshape.194
  601.7 1.2 slice_bitcast_fusion.3
  602.9 1.2 slice_bitcast_fusion.4
  604.0 1.2 slice_bitcast_fusion.5
  605.2 0.7 multiply_multiply_fusion
  605.9 4.9 fusion.5
  (119 shorter events, 3.3 us)
Async XLA Ops:
  7.2 8.1 %copy-start.30 = (f32[24]{0:T(128)S(1)}, f32[24]{0:T(128)}, u32[]{:S(2)}) copy-start(f32[24]{0:T(128)} %param.25) | copy-start | bytes 292
  7.2 8.1 %copy-start.31 = (f32[24]{0:T(128)S(1)}, f32[24]{0:T(128)}, u32[]{:S(2)}) copy-start(f32[24]{0:T(128)} %param.26) | copy-start | bytes 292
  7.2 349.6 %reduce-scatter.2.cloned.1.call-start = ((), (), s32[]{:S(2)}) async-start(), calls=%async_computation.1 | async-start | bytes 1310720 | tf_op jit(solution)/shard_map/reduce_scatter | solution.py:1454
  7.3 349.5 %copy-start.28 = (f32[128]{0:T(128)}, f32[128]{0:T(128)S(1)}, u32[]{:S(2)}) copy-start(f32[128]{0:T(128)S(1)} %get-tuple-element.175) | copy-start | bytes 1540
  234.5 4.3 copy-start
  234.5 4.3 copy-start.3
  234.5 4.3 copy-start.6
  234.5 5.6 copy-start.32
  238.9 1.2 copy-start.23
  239.8 107.5 %copy-start.18 = (f32[512]{0:T(512)}, f32[512]{0:T(512)S(1)}, u32[]{:S(2)}) copy-start(f32[512]{0:T(512)S(1)} %fusion.24) | copy-start | bytes 6148
  240.1 4.7 copy-start.2
  240.1 4.7 copy-start.33
  261.8 1.4 copy-start.1
  263.8 12.4 %copy-start.4 = (bf16[512,1024]{1,0:T(8,128)(2,1)}, bf16[512,1024]{1,0:T(8,128)(2,1)S(1)}, u32[]{:S(2)}) copy-start(bf16[512,1024]{1,0:T(8,128)(2,1)S(1)} %fusion.37) | copy-start | bytes 3145732
  276.2 92.8 %all-gather.5.cloned.1.call-start = ((), (), s32[]{:S(2)}) async-start(), calls=%async_computation.2 | async-start | bytes 1966080 | tf_op jit(solution)/shard_map/all_gather | solution.py:1431
  295.2 3.6 copy-start.5
  295.2 3.6 copy-start.35
  295.5 37.3 %copy-start.20 = (f32[512]{0:T(512)}, f32[512]{0:T(512)S(1)}, u32[]{:S(2)}) copy-start(f32[512]{0:T(512)S(1)} %fusion.6) | copy-start | bytes 6148
  298.8 3.6 copy-start.27
  333.4 6.2 copy-start.26
  340.9 6.4 %copy-start.43 = (f32[512,2048]{1,0:T(8,128)S(1)}, f32[512,2048]{1,0:T(8,128)}, u32[]{:S(2)}) copy-start(f32[512,2048]{1,0:T(8,128)} %get-tuple-element.160) | copy-start | bytes 12582916
  363.1 1.9 copy-start.10
  369.0 1.9 copy-start.13
  369.0 1.9 copy-start.14
  369.0 1.9 copy-start.15
  372.0 32.3 %copy-start.11 = (bf16[512,128]{1,0:T(8,128)(2,1)S(1)}, bf16[512,128]{1,0:T(8,128)(2,1)}, u32[]{:S(2)}) copy-start(bf16[512,128]{1,0:T(8,128)(2,1)} %copy-done.10) | copy-start | bytes 393220
  372.0 32.3 %copy-start.36 = (bf16[512,1024]{1,0:T(8,128)(2,1)S(1)}, bf16[512,1024]{1,0:T(8,128)(2,1)}, u32[]{:S(2)}) copy-start(bf16[512,1024]{1,0:T(8,128)(2,1)} %get-tuple-element.90) | copy-start | bytes 3145732
  372.1 32.4 %copy-start.38 = (bf16[512,512]{1,0:T(8,128)(2,1)S(1)}, bf16[512,512]{1,0:T(8,128)(2,1)}, u32[]{:S(2)}) copy-start(bf16[512,512]{1,0:T(8,128)(2,1)} %get-tuple-element.71) | copy-start | bytes 1572868
  403.1 6.3 %collective-permute-start = (f32[8,1792]{1,0:T(8,128)}, f32[8,1792]{1,0:T(8,128)S(1)}, u32[]{:S(2)}, u32[]{:S(2)}) collective-permute-start(f32[8,1792]{1,0:T(8,128)} %slice.103), channel_id=1, source_target_pairs={{1,0},{2,1},{3,2},{5,4},{6,5},{7,6},{9,8},{10,9},{11,10},{13,12},{... | collective-permute-start | bytes 172040 | tf_op jit(solution)/shard_map/ppermute | solution.py:1333
  404.4 2.2 copy-start.12
  404.4 2.2 copy-start.17
  404.4 2.2 copy-start.25
  406.7 5.0 copy-start.34
  406.7 5.0 copy-start.37
  409.4 8.5 %slice-start = ((s8[7077888]{0:T(1024)(128)(4,1)}), s8[4194304]{0:T(1024)(128)(4,1)S(1)}, s32[]{:S(2)}) async-start(s8[7077888]{0:T(1024)(128)(4,1)} %bitcast.104), calls=%async_computation.3 | async-start | bytes 8388608
  411.8 6.1 copy-start.22
  411.8 6.1 copy-start.24
  411.8 6.1 slice-start.1
  411.8 6.1 copy-start.42
  417.9 6.4 %copy-start.29 = (f32[1024]{0:T(1024)S(1)}, f32[1024]{0:T(1024)}, u32[]{:S(2)}) copy-start(f32[1024]{0:T(1024)} %get-tuple-element.152) | copy-start | bytes 12292
  417.9 6.4 %copy-start.16 = (f32[1536]{0:T(1024)S(1)}, f32[1536]{0:T(1024)}, u32[]{:S(2)}) copy-start(f32[1536]{0:T(1024)} %reduce.4) | copy-start | bytes 18436
  417.9 6.4 %copy-start.41 = (f32[1,128]{1,0:T(1,128)S(1)}, f32[1,128]{1,0:T(1,128)}, u32[]{:S(2)}) copy-start(f32[1,128]{1,0:T(1,128)} %get-tuple-element.94) | copy-start | bytes 1540
  417.9 6.4 %copy-start.40 = (f32[1,128]{1,0:T(1,128)S(1)}, f32[1,128]{1,0:T(1,128)}, u32[]{:S(2)}) copy-start(f32[1,128]{1,0:T(1,128)} %get-tuple-element.95) | copy-start | bytes 1540
  418.0 6.4 %copy-start.39 = (f32[1,128]{1,0:T(1,128)S(1)}, f32[1,128]{1,0:T(1,128)}, u32[]{:S(2)}) copy-start(f32[1,128]{1,0:T(1,128)} %get-tuple-element.96) | copy-start | bytes 1540
  593.2 4.7 copy-start.7
  595.7 3.2 copy-start.8
  595.7 3.9 copy-start.9
  595.7 9.5 %copy-start.21 = (f32[512]{0:T(512)S(1)}, f32[512]{0:T(512)}, u32[]{:S(2)}) copy-start(f32[512]{0:T(512)} %copy-done.20) | copy-start | bytes 6148
  595.7 10.2 %copy-start.19 = (f32[512]{0:T(512)S(1)}, f32[512]{0:T(512)}, u32[]{:S(2)}) copy-start(f32[512]{0:T(512)} %copy-done.18) | copy-start | bytes 6148
Sparse Core Ops, SparseCore 0:
  276.3 43.9 reduce-scatter.1
  322.5 35.8 all-gather.4

commit v3 on v2

--- a/solution.py
+++ b/solution.py
@@ -1046,6 +1046,8 @@
     bit_count = bit_length(fsdp)
     shapes = [s.shape for s in shards]
     items = plan_items(shapes, parts, bit_count)
+    for item in items:
+        item.order = item.order[1:] + item.order[:1]
     count = tokens.shape[0]
     weights = len(shards)
     pieces = 2

time: 627 us -> 533 us (0.85)
  Pallas kernels: 420 us -> 323 us
    pallas_call x1, Pallas kernels: 217 us -> 120 us  [forward_part(): pl.pallas_call(kernel, out_shape=[jax.ShapeDtypeStruct(*a) for a in list(...]
  transfers between devices with their start and end apart: 3 -> 3, of which waited for: 1 -> 1; matrix products, arithmetic and copies ran while one was open for 8% -> 10% of each run, Pallas kernels for 2% -> 2%
where the time goes in v3:
time: 533 us; the launch traced here: 524 us
  Pallas kernels  323 us (61%)
  matrix products  80.9 us (15%)
  local copies, waits for them, and re-layouts  37.7 us (7%)
  blocking collectives  33.6 us (6%)
  other arithmetic  29.8 us (6%)
  between operations  15 us (3%)
    pallas_call x1, Pallas kernels, reduce_all(): pl.pallas_call(kernel, out_shape=[jax.ShapeDtypeStruct(shape, bf16) for s...  151 us
    pallas_call x1, Pallas kernels, forward_part(): pl.pallas_call(kernel, out_shape=[jax.ShapeDtypeStruct(*a) for a in list(...  120 us
    pallas_call x3, Pallas kernels, call(): pl.pallas_call(kernel, out_shape=[jax.ShapeDtypeStruct(shape, kind) for s...  52.2 us
    dot_general x6, matrix products, dot_nt(): lax.dot_general(left, right, (((1,), (1,)), ((), ())), preferred_element_...  34 us
    all_gather x1, blocking collectives, on_device(): passings = lax.all_gather(v['passing'], 'seq')  33.6 us
    dot_general x6, matrix products, dot_tn(): lax.dot_general(left, right, (((0,), (0,)), ((), ())), preferred_element_...  30.9 us
    dot_general x4, matrix products, dot_nn(): return jnp.dot(left, right, preferred_element_type=jnp.float32)  16 us
  transfers between devices with their start and end apart: 3, of which 1 were waited for; matrix products, arithmetic and copies ran while one was open for 10% of the time, Pallas kernels for 2%

profile of v3, /device:TPU:0, one launch (start us, length us, event | category | flops | bytes accessed | tf_op | source)
XLA Modules:
  0.0 524.0 jit_solution(978649310474825826)
XLA Ops:
  7.3 0.7 broadcast_in_dim.62
  8.0 0.7 broadcast_in_dim_reshape.3.refs_10_.skip_ref
  8.7 1.3 convert_element_type.103.refs_1_.segrow_ref
  9.9 1.3 broadcast_in_dim.60.refs_8_.cbias_ref
  11.2 1.3 broadcast_in_dim.61.refs_9_.gain_ref
  12.5 2.7 copy.43.refs_11_
  15.8 1.8 fusion.22
  17.6 120.2 %shard_map.288 = (bf16[512,1024]{1,0:T(8,128)(2,1)}, f32[520,1792]{1,0:T(8,128)}, f32[512,128]{1,0:T(8,128)}, f32[512,1536]{1,0:T(8,128)}, bf16[512,1792]{1,0:T(...) custom-call(bf16[512,1024]{1,0:T(8,128)(2,1)} %bitcast.87, ...), custom_call_target="tpu_custom_call" | custom-call | tf_op jit(solution)/shard_map/pallas_call | solution.py:1318
  137.8 4.3 fusion.39
  142.1 0.9 multiply_reduce_fusion.2
  143.4 4.7 fusion.36
  148.0 6.4 %bitcast_multiply_fusion.1 = (f32[512,2048]{1,0:T(8,128)}, f32[512,2048]{1,0:T(8,128)}, bf16[512,2048]{1,0:T(8,128)(2,1)}) fusion(f32[512,4096]{1,0:T(8,128)S(1)} %fusion.36, bf16[2048,1024]{1,0:T(8,128)(2,1)S(1)} %copy-done.33, bf16[1,512,1024]{2,1,0:T(8,128)(2,1)S(1)} %copy-done.2), kind=kOutput, calls=%fused_computation.7 | convolution fusion | flops 2162163712 | bytes 24117248 | tf_op jit(solution)/shard_map/dot_general | solution.py:33
  154.5 10.6 %multiply_reduce_fusion = (f32[1024]{0:T(1024)}, f32[512]{0:T(512)S(1)}, f32[512,1024]{1,0:T(8,128)S(1)}) fusion(f32[512,1024]{1,0:T(8,128)S(1)} %get-tuple-element.171, f32[512]{0:T(512)S(1)} %fusion.24, f32[1024]{0:T(1024)S(1)} %copy-done.23, bf16[1024,4096]{1,0:T(8,128)(2,1)} %get-tuple-element.64, f32[512,2048]{1,0:T(8,128)} %get-tuple-element.161, ...), kind=kOutput, calls=%fused_computation.30 | convolution fusion | flops 4302305792 | bytes 20983808 | tf_op jit(solution)/shard_map/dot_general | solution.py:33
  165.1 1.3 copy-done.1
  167.0 1.5 convolution_convert_fusion.7.grad_ref
  168.6 10.8 %shard_map.289 = (bf16[512,512]{1,0:T(8,128)(2,1)}, bf16[2048,256]{1,0:T(8,128)(2,1)}) custom-call(s32[1]{0:T(128)} %bitcast.7.own_ref, bf16[512,512]{1,0:T(8,128)(2,1)} %get-tuple-element.66.query_ref, bf16[2048,256]{1,0:T(8,128)(2,1)} %get-tuple-element.67.kv_ref, f32[2048,128]{1,0:T(8,128)} %get-tuple-element.68.segcol_ref, ...), custom_call_target="tpu_custom_call" | custom-call | flops 1000000000 | bytes 10000000 | tf_op jit(solution)/shard_map/pallas_call | solution.py:488
  179.5 5.2 convolution_convert_fusion.4.grad_ref
  184.6 11.8 %shard_map.290 = (f32[512,1536]{1,0:T(8,128)}, bf16[512,1536]{1,0:T(8,128)(2,1)}, f32[1,1536]{1,0:T(1,128)}, f32[128,1536]{1,0:T(8,128)}) custom-call(bf16[512,1536]{1,0:T(8,128)(2,1)} %convolution_convert_fusion.4.grad_ref, f32[512,1536]{1,0:T(8,128)} %get-tuple-element.74.y_ref, bf16[512,1792]{1,0:T(8,128)(2,1)} %get-tuple-element.75.act_ref, ...), custom_call_target="tpu_custom_call" | custom-call | flops 1000000000 | bytes 10000000 | tf_op jit(solution)/shard_map/pallas_call | solution.py:488
  196.5 1.9 convert_element_type.115
  198.7 3.3 convolution_convert_fusion.6
  202.0 3.5 convolution_convert_fusion.3
  205.6 33.6 %all-gather.2 = f32[4,1,1536]{2,1,0:T(1,128)S(1)} all-gather(f32[1,1,1536]{2,1,0:T(1,128)S(1)} %bitcast.101), channel_id=2, replica_groups=mesh['fsdp'=8,'seq'=4] {'seq'}, dimensions={0}, use_global_device_ids=true | all-gather | bytes 30720 | tf_op jit(solution)/shard_map/all_gather | solution.py:1434
  239.1 0.6 fusion.25
  239.7 6.1 %fusion.10 = bf16[1,512,1024]{2,1,0:T(8,128)(2,1)} fusion(f32[512,1024]{1,0:T(8,128)S(1)} %get-tuple-element.171, bf16[512,2048]{1,0:T(8,128)(2,1)} %get-tuple-element.162, bf16[2048,1024]{1,0:T(8,128)(2,1)} %get-tuple-element.65), kind=kOutput, calls=%fused_computation.38 | convolution fusion | flops 2148532224 | bytes 9437184 | tf_op jit(solution)/shard_map/dot_general | solution.py:29
  245.9 0.6 reduce.4
  246.5 0.7 slice_reduce_fusion.2
  247.2 6.4 %convolution_convert_fusion.2 = bf16[2048,1024]{1,0:T(8,128)(2,1)} fusion(bf16[512,2048]{1,0:T(8,128)(2,1)} %get-tuple-element.162, bf16[1,512,1024]{2,1,0:T(8,128)(2,1)} %param.18), kind=kOutput, calls=%fused_computation.16 | convolution fusion | flops 2149580800 | bytes 7340032 | tf_op jit(solution)/shard_map/dot_general | solution.py:39
  253.6 9.4 %convolution_convert_fusion = bf16[1024,4096]{1,0:T(8,128)(2,1)} fusion(f32[512,2048]{1,0:T(8,128)} %get-tuple-element.161, f32[512,2048]{1,0:T(8,128)S(1)} %copy-done.43, f32[512,1024]{1,0:T(8,128)S(1)} %get-tuple-element.171, f32[1024]{0:T(1024)S(1)} %copy-done.23, f32[512]{0:T(512)S(1)} %fusion.24), kind=kOutput, calls=%fused_computation.1 | convolution fusion | flops 4304928768 | bytes 18880512 | tf_op jit(solution)/shard_map/dot_general | solution.py:39
  263.1 1.8 convert_multiply_fusion.4
  264.9 0.8 copy.45
  265.8 1.7 rev.3
  267.4 1.1 copy.46
  268.5 0.9 slice.133
  269.4 1.9 fusion.21
  271.4 3.9 fusion.19
  275.3 1.8 convert_element_type.130
  277.1 1.2 fusion.14.later_ref
  278.4 29.6 %shard_map.291 = (f32[512,128]{1,0:T(8,128)}, f32[520,1792]{1,0:T(8,128)}, f32[4,1792]{1,0:T(4,128)}, f32[1,1792]{1,0:T(1,128)}, f32[1,128]{1,0:T(1,128)}, /*index=5*/f32[1,128]{1,0:T(1,128)}, f32[1,128]{1,0:T(1,128)}) custom-call(bf16[512,1792]{1,0:T(8,128)(2,1)} %get-tuple-element.75.act_ref, f32[512,128]{1,0:T(8,128)} %get-tuple-element.77.dt_ref, ...), custom_call_target="tpu_custom_call" | custom-call | flops 1000000000 | bytes 10000000 | tf_op jit(solution)/shard_map/pallas_call | solution.py:488
  308.0 1.4 slice.103
  309.4 1.3 collective-permute-start
  310.8 2.2 convolution_convert_fusion.5
  313.0 2.7 collective-permute-done
  315.7 2.4 add_convert_fusion.1
  318.1 6.1 %convolution_convert_fusion.1 = bf16[1024,3352]{0,1:T(8,128)(2,1)} fusion(bf16[512,1024]{1,0:T(8,128)(2,1)S(1)} %copy-done.37, bf16[512,24]{1,0:T(8,128)(2,1)S(1)} %slice.197, bf16[512,1792]{1,0:T(8,128)(2,1)S(1)} %add_convert_fusion.1, bf16[512,1536]{1,0:T(8,128)(2,1)S(1)} %copy-done.34), kind=kOutput, calls=%fused_computation.2 | convolution fusion | flops 3528556544 | bytes 11345920 | tf_op jit(solution)/shard_map/dot_general | solution.py:39
  324.3 6.3 %fusion.9 = (f32[1024]{0:T(1024)S(1)}, f32[512]{0:T(512)}, f32[512,1024]{1,0:T(8,128)}) fusion(f32[512]{0:T(512)S(1)} %copy-done.24, bf16[1,512,1024]{2,1,0:T(8,128)(2,1)S(1)} %copy-done, f32[1024]{0:T(1024)S(1)} %copy-done.22, f32[512,1024]{1,0:T(8,128)S(1)} %copy-done.42, bf16[1024,3352]{1,0:T(8,128)(2,1)S(1)} %bitcast.105, ...), kind=kOutput, calls=%fused_computation.29 | convolution fusion | flops 3529316864 | bytes 15552512 | tf_op jit(solution)/shard_map/dot_general | solution.py:33
  330.8 0.6 reshape.192.refs_6_
  331.4 9.9 %copy.47 = bf16[1024,3352]{1,0:T(8,128)(2,1)} copy(bf16[1024,3352]{0,1:T(8,128)(2,1)} %convolution_convert_fusion.1) | data formatting | bytes 13729792 | tf_op jit(solution)/shard_map/convert_element_type | solution.py:49
  341.4 150.6 %shard_map.292 = (bf16[128,3352]{1,0:T(8,128)(2,1)}, bf16[192,1024]{1,0:T(8,128)(2,1)}, bf16[128,768]{1,0:T(8,128)(2,1)}, bf16[64,1024]{1,0:T(8,128)(2,1)}, bf16...) custom-call(bf16[2,2,2,128,3352]{4,3,2,1,0:T(8,128)(2,1)} %bitcast.86, ...), custom_call_target="tpu_custom_call" | custom-call | tf_op jit(solution)/shard_map/pallas_call | solution.py:901
  491.9 0.9 copy.50
  492.8 0.6 slice.144
  494.0 0.6 slice.145
  495.2 1.4 fusion.38
  496.6 2.8 convert_element_type.128
  499.4 2.5 copy.48
  501.9 2.2 convert_element_type.129
  504.0 1.0 convert_element_type.125
  505.0 0.8 convert_element_type.126
  505.8 0.7 convert_element_type.127
  506.5 1.4 reshape.194
  507.9 1.2 slice_bitcast_fusion.3
  509.0 1.2 slice_bitcast_fusion.4
  510.2 1.2 slice_bitcast_fusion.5
  511.4 0.7 multiply_multiply_fusion
  512.1 4.9 fusion.5
  (119 shorter events, 3.3 us)
Async XLA Ops:
  7.2 8.1 %copy-start.30 = (f32[24]{0:T(128)S(1)}, f32[24]{0:T(128)}, u32[]{:S(2)}) copy-start(f32[24]{0:T(128)} %param.25) | copy-start | bytes 292
  7.2 8.1 %copy-start.31 = (f32[24]{0:T(128)S(1)}, f32[24]{0:T(128)}, u32[]{:S(2)}) copy-start(f32[24]{0:T(128)} %param.26) | copy-start | bytes 292
  7.2 255.9 %reduce-scatter.2.cloned.1.call-start = ((), (), s32[]{:S(2)}) async-start(), calls=%async_computation.1 | async-start | bytes 1310720 | tf_op jit(solution)/shard_map/reduce_scatter | solution.py:1456
  7.3 255.8 %copy-start.28 = (f32[128]{0:T(128)}, f32[128]{0:T(128)S(1)}, u32[]{:S(2)}) copy-start(f32[128]{0:T(128)S(1)} %get-tuple-element.175) | copy-start | bytes 1540
  137.7 4.4 copy-start
  137.7 4.3 copy-start.3
  137.8 4.3 copy-start.6
  137.8 5.6 %copy-start.32 = (bf16[1024,4096]{1,0:T(8,128)(2,1)S(1)}, bf16[1024,4096]{1,0:T(8,128)(2,1)}, u32[]{:S(2)}) copy-start(bf16[1024,4096]{1,0:T(8,128)(2,1)} %get-tuple-element.64) | copy-start | bytes 25165828
  142.1 1.2 copy-start.23
  143.0 110.6 %copy-start.18 = (f32[512]{0:T(512)}, f32[512]{0:T(512)S(1)}, u32[]{:S(2)}) copy-start(f32[512]{0:T(512)S(1)} %fusion.24) | copy-start | bytes 6148
  143.4 4.7 copy-start.2
  143.4 4.7 copy-start.33
  165.1 1.4 copy-start.1
  167.0 12.4 %copy-start.4 = (bf16[512,1024]{1,0:T(8,128)(2,1)}, bf16[512,1024]{1,0:T(8,128)(2,1)S(1)}, u32[]{:S(2)}) copy-start(bf16[512,1024]{1,0:T(8,128)(2,1)S(1)} %fusion.37) | copy-start | bytes 3145732
  179.4 95.9 %all-gather.5.cloned.1.call-start = ((), (), s32[]{:S(2)}) async-start(), calls=%async_computation.2 | async-start | bytes 1966080 | tf_op jit(solution)/shard_map/all_gather | solution.py:1433
  198.4 3.6 copy-start.5
  198.4 3.6 copy-start.35
  198.7 40.4 %copy-start.20 = (f32[512]{0:T(512)}, f32[512]{0:T(512)S(1)}, u32[]{:S(2)}) copy-start(f32[512]{0:T(512)S(1)} %fusion.6) | copy-start | bytes 6148
  202.0 3.6 copy-start.27
  239.7 6.2 %copy-start.26 = (f32[1,1536]{1,0:T(1,128)S(1)}, f32[1,1536]{1,0:T(1,128)}, u32[]{:S(2)}) copy-start(f32[1,1536]{1,0:T(1,128)} %get-tuple-element.91) | copy-start | bytes 18436
  247.2 6.5 %copy-start.43 = (f32[512,2048]{1,0:T(8,128)S(1)}, f32[512,2048]{1,0:T(8,128)}, u32[]{:S(2)}) copy-start(f32[512,2048]{1,0:T(8,128)} %get-tuple-element.160) | copy-start | bytes 12582916
  269.4 1.9 copy-start.10
  275.3 1.9 copy-start.13
  275.3 1.9 copy-start.14
  275.3 1.9 copy-start.15
  278.4 32.3 %copy-start.11 = (bf16[512,128]{1,0:T(8,128)(2,1)S(1)}, bf16[512,128]{1,0:T(8,128)(2,1)}, u32[]{:S(2)}) copy-start(bf16[512,128]{1,0:T(8,128)(2,1)} %copy-done.10) | copy-start | bytes 393220
  278.4 32.3 %copy-start.36 = (bf16[512,1024]{1,0:T(8,128)(2,1)S(1)}, bf16[512,1024]{1,0:T(8,128)(2,1)}, u32[]{:S(2)}) copy-start(bf16[512,1024]{1,0:T(8,128)(2,1)} %get-tuple-element.90) | copy-start | bytes 3145732
  278.4 32.4 %copy-start.38 = (bf16[512,512]{1,0:T(8,128)(2,1)S(1)}, bf16[512,512]{1,0:T(8,128)(2,1)}, u32[]{:S(2)}) copy-start(bf16[512,512]{1,0:T(8,128)(2,1)} %get-tuple-element.71) | copy-start | bytes 1572868
  309.4 6.3 %collective-permute-start = (f32[8,1792]{1,0:T(8,128)}, f32[8,1792]{1,0:T(8,128)S(1)}, u32[]{:S(2)}, u32[]{:S(2)}) collective-permute-start(f32[8,1792]{1,0:T(8,128)} %slice.103), channel_id=1, source_target_pairs={{1,0},{2,1},{3,2},{5,4},{6,5},{7,6},{9,8},{10,9},{11,10},{13,12},{... | collective-permute-start | bytes 172040 | tf_op jit(solution)/shard_map/ppermute | solution.py:1335
  310.7 2.2 copy-start.12
  310.7 2.2 copy-start.17
  310.7 2.2 copy-start.25
  313.0 5.1 copy-start.34
  313.0 5.1 copy-start.37
  315.7 8.5 %slice-start = ((s8[7077888]{0:T(1024)(128)(4,1)}), s8[4194304]{0:T(1024)(128)(4,1)S(1)}, s32[]{:S(2)}) async-start(s8[7077888]{0:T(1024)(128)(4,1)} %bitcast.104), calls=%async_computation.3 | async-start | bytes 8388608
  318.1 6.1 %copy-start.22 = (f32[1024]{0:T(1024)S(1)}, f32[1024]{0:T(1024)}, u32[]{:S(2)}) copy-start(f32[1024]{0:T(1024)} %param.20) | copy-start | bytes 12292
  318.1 6.1 %copy-start.24 = (f32[512]{0:T(512)S(1)}, f32[512]{0:T(512)}, u32[]{:S(2)}) copy-start(f32[512]{0:T(512)} %fusion.25) | copy-start | bytes 6148
  318.1 6.1 %slice-start.1 = ((s8[7077888]{0:T(1024)(128)(4,1)}), s8[2883584]{0:T(1024)(128)(4,1)S(1)}, s32[]{:S(2)}) async-start(s8[7077888]{0:T(1024)(128)(4,1)} %bitcast.104), calls=%async_computation.4 | async-start | bytes 5767168
  318.1 6.1 %copy-start.42 = (f32[512,1024]{1,0:T(8,128)S(1)}, f32[512,1024]{1,0:T(8,128)}, u32[]{:S(2)}) copy-start(f32[512,1024]{1,0:T(8,128)} %fusion.19) | copy-start | bytes 6291460
  324.3 6.4 %copy-start.29 = (f32[1024]{0:T(1024)S(1)}, f32[1024]{0:T(1024)}, u32[]{:S(2)}) copy-start(f32[1024]{0:T(1024)} %get-tuple-element.152) | copy-start | bytes 12292
  324.3 6.4 %copy-start.16 = (f32[1536]{0:T(1024)S(1)}, f32[1536]{0:T(1024)}, u32[]{:S(2)}) copy-start(f32[1536]{0:T(1024)} %reduce.4) | copy-start | bytes 18436
  324.3 6.4 %copy-start.41 = (f32[1,128]{1,0:T(1,128)S(1)}, f32[1,128]{1,0:T(1,128)}, u32[]{:S(2)}) copy-start(f32[1,128]{1,0:T(1,128)} %get-tuple-element.94) | copy-start | bytes 1540
  324.3 6.4 %copy-start.40 = (f32[1,128]{1,0:T(1,128)S(1)}, f32[1,128]{1,0:T(1,128)}, u32[]{:S(2)}) copy-start(f32[1,128]{1,0:T(1,128)} %get-tuple-element.95) | copy-start | bytes 1540
  324.3 6.4 %copy-start.39 = (f32[1,128]{1,0:T(1,128)S(1)}, f32[1,128]{1,0:T(1,128)}, u32[]{:S(2)}) copy-start(f32[1,128]{1,0:T(1,128)} %get-tuple-element.96) | copy-start | bytes 1540
  499.4 4.7 copy-start.7
  501.8 3.2 copy-start.8
  501.8 3.9 copy-start.9
  501.8 9.5 %copy-start.21 = (f32[512]{0:T(512)S(1)}, f32[512]{0:T(512)}, u32[]{:S(2)}) copy-start(f32[512]{0:T(512)} %copy-done.20) | copy-start | bytes 6148
  501.8 10.2 %copy-start.19 = (f32[512]{0:T(512)S(1)}, f32[512]{0:T(512)}, u32[]{:S(2)}) copy-start(f32[512]{0:T(512)} %copy-done.18) | copy-start | bytes 6148
Sparse Core Ops, SparseCore 0:
  179.5 47.8 reduce-scatter.1
  229.7 35.7 all-gather.4
